TPU v7x, 32 devices: a whole 2x2x4 slice. The times are simulated.
32 devices in a mesh: ctx: 8 (over z, x), fsdp: 4 (over y, core).
Axes of the slice: x: 2, y: 2, z: 4, core: 2. Of those that a mesh axis runs over, the one named last changes fastest.
Arguments:
- layer_input: bfloat16 [4, 8192, 512], P('fsdp', 'ctx'), may hold values from -6 to 6
- doc_lengths: int32 [4, 8], P('fsdp'), may hold values from 1 to 7168, as said below
- ln1_gain: bfloat16 [512], P('fsdp'), may hold values from 0.099609375 to 1.8984375
- ln1_bias: bfloat16 [512], P('fsdp'), may hold values from -1.75 to 1.75
- qkv_weight: bfloat16 [512, 1536], P('fsdp'), may hold values from -0.375 to 0.375
- query_bias: bfloat16 [512], P('fsdp'), may hold values from -3 to 3
- value_bias: bfloat16 [512], P('fsdp'), may hold values from -3 to 3
- out_weight: bfloat16 [512, 512], P('fsdp'), may hold values from -1 to 1
- out_bias: bfloat16 [512], P('fsdp'), may hold values from -1.75 to 1.75
- ln2_gain: bfloat16 [512], P('fsdp'), may hold values from 0.099609375 to 1.8984375
- ln2_bias: bfloat16 [512], P('fsdp'), may hold values from -1.75 to 1.75
- up_weight: bfloat16 [512, 2048], P('fsdp'), may hold values from -0.25 to 0.25
- up_bias: bfloat16 [2048], P('fsdp'), may hold values from -1.75 to 1.75
- down_weight: bfloat16 [2048, 512], P('fsdp'), may hold values from -0.1875 to 0.1875
- down_bias: bfloat16 [512], P('fsdp'), may hold values from -1.75 to 1.75
- cotangent: bfloat16 [4, 8192, 512], P('fsdp', 'ctx'), may hold values from -8 to 8
Outputs:
- output: bfloat16 [4, 8192, 512], P('fsdp', 'ctx')
- input_grad: float32 [4, 8192, 512], P('fsdp', 'ctx')
- ln1_gain_grad: float32 [512], P('fsdp')
- ln1_bias_grad: float32 [512], P('fsdp')
- qkv_weight_grad: float32 [512, 1536], P('fsdp')
- query_bias_grad: float32 [512], P('fsdp')
- value_bias_grad: float32 [512], P('fsdp')
- out_weight_grad: float32 [512, 512], P('fsdp')
- out_bias_grad: float32 [512], P('fsdp')
- ln2_gain_grad: float32 [512], P('fsdp')
- ln2_bias_grad: float32 [512], P('fsdp')
- up_weight_grad: float32 [512, 2048], P('fsdp')
- up_bias_grad: float32 [2048], P('fsdp')
- down_weight_grad: float32 [2048, 512], P('fsdp')
- down_bias_grad: float32 [512], P('fsdp')
Inputs may be any that keep to these rules, and one draw needn't show every extreme that they name: `doc_lengths`: each row gives the lengths of a stream's 8 documents in order; they sum to 8192; exactly one document has 7168 tokens, neither first nor last, so that it begins among the first 1024 tokens and ends among the last 1024; the others together hold 1024 tokens.
All inputs are finite; a program needn't handle non-finite values.
Results may differ from a plain program's by a relative error of at most 0.011.
The roundings to bfloat16 on the way count: a program that leaves them out, or rounds other values in their place, can miss the bound.
Values may be sent and summed in bfloat16 or wider, within the bound.
No kernel may reach another device: no remote copies, remote signals or barrier semaphores. Data moves between devices by JAX's collectives and lax.ppermute only.
A program may use at most 192 MiB of HBM per device.

v0:
```python
from functools import partial
import math

import jax
import jax.numpy as jnp
from jax import lax
from jax.sharding import PartitionSpec as P

ATTENTION_HEADS = 8
BLOCK = 16
LEVELS = 10
NEAR = 4


norm_epsilon = 1e-05
masked_score = -1e30
inverse_root_two = 1.0 / math.sqrt(2.0)
inverse_root_two_pi = 1.0 / math.sqrt(2.0 * math.pi)


def shifted(block, axis, distance):
    devices = range(lax.axis_size(axis))
    route = [(i - distance, i) for i in devices if i - distance in devices]
    return lax.ppermute(block, axis, route)


def gelu_slope(values):
    return (
        0.5 * (1.0 + jax.scipy.special.erf(values * inverse_root_two))
        + values * jnp.exp(-0.5 * values * values) * inverse_root_two_pi
    )


def norm_forward(values, norm_gain, norm_bias):
    row_mean = jnp.mean(values, axis=-1, keepdims=True)
    centred = values - row_mean
    variance = jnp.mean(centred * centred, axis=-1, keepdims=True)
    inverse = lax.rsqrt(variance + norm_epsilon)
    scaled = centred * inverse
    return (scaled * norm_gain + norm_bias, scaled, inverse)


def norm_backward(grad_out, scaled, inverse, norm_gain):
    grad_scaled = grad_out * norm_gain
    first_mean = jnp.mean(grad_scaled, axis=-1, keepdims=True)
    second_mean = jnp.mean(grad_scaled * scaled, axis=-1, keepdims=True)
    grad_in = inverse * (grad_scaled - first_mean - scaled * second_mean)
    return (grad_in, jnp.sum(grad_out * scaled, axis=0), jnp.sum(grad_out, axis=0))


def doc_index(positions, starts):
    return jnp.sum((starts[None, :] <= positions[:, None]).astype(jnp.int32), axis=1) - 1


def allowed(query_pos, key_first, key_level, key_span, starts, total):
    block_span = BLOCK * key_span[None, :]
    parent_span = jnp.maximum(block_span // 2, 1)
    query_col = query_pos[:, None]
    first_row = key_first[None, :]
    block_gap = jnp.abs(first_row // block_span - query_col // block_span)
    parent_gap = jnp.abs(first_row // parent_span - query_col // parent_span)
    level_ok = jnp.where(
        key_level[None, :] == 0, block_gap <= 1, (block_gap == 1) & (parent_gap > 1)
    )
    inside = (key_first >= 0) & (key_first < total)
    first_doc = doc_index(key_first, starts)
    last_doc = doc_index(key_first + key_span - 1, starts)
    key_doc = jnp.where(inside & (first_doc == last_doc), first_doc, -2)
    query_doc = doc_index(query_pos, starts)
    return level_ok & (key_doc[None, :] == query_doc[:, None])


def pair_mean(rows):
    paired = rows.reshape(rows.shape[0] // 2, 2, rows.shape[1])
    return 0.5 * (paired[:, 0] + paired[:, 1])


def spread_back(grad_rows):
    return jnp.repeat(0.5 * grad_rows, 2, axis=0)


def contract_rows(left, right):
    return lax.dot_general(
        left, right, (((0,), (0,)), ((), ())), preferred_element_type=jnp.float32
    )


def times_transpose(left, right):
    return lax.dot_general(
        left, right, (((1,), (1,)), ((), ())), preferred_element_type=jnp.float32
    )


def head_groups(matrix):
    group_count = ATTENTION_HEADS // 2
    return matrix.reshape(matrix.shape[0], group_count, matrix.shape[1] // group_count).transpose(
        1, 0, 2
    )


def ungroup(stacked):
    return stacked.transpose(1, 0, 2).reshape(stacked.shape[1], stacked.shape[0] * stacked.shape[2])


def group_scores(query_group, key_group, mask, level_weight):
    head_dim = query_group.shape[1] // 2
    attention_scores = jnp.einsum(
        "cse,jse->scj",
        query_group.reshape(query_group.shape[0], 2, head_dim),
        key_group.reshape(key_group.shape[0], 2, head_dim),
        preferred_element_type=jnp.float32,
    ) * (1.0 / math.sqrt(head_dim))
    attention_scores = attention_scores + level_weight[None, None, :]
    return jnp.where(mask[None], attention_scores, masked_score)


def group_forward(operands, mask, level_weight):
    query_group, key_group, value_group = operands
    head_dim = query_group.shape[1] // 2
    attention_scores = group_scores(query_group, key_group, mask, level_weight)
    row_top = jnp.max(attention_scores, axis=-1, keepdims=True)
    exponent = jnp.exp(attention_scores - row_top)
    totals = jnp.sum(exponent, axis=-1, keepdims=True)
    attention_probabilities = exponent / totals
    attended_output = jnp.einsum(
        "fao,ofx->afx",
        attention_probabilities.astype(jnp.bfloat16),
        value_group.reshape(value_group.shape[0], 2, head_dim),
        preferred_element_type=jnp.float32,
    )
    return (
        attended_output.reshape(query_group.shape[0], 2 * head_dim),
        (row_top + jnp.log(totals))[..., 0],
    )


def group_backward(operands, mask, level_weight):
    query_group, key_group, value_group, grad_group, log_total = operands
    head_dim = query_group.shape[1] // 2
    query_triple = query_group.reshape(query_group.shape[0], 2, head_dim)
    key_triple = key_group.reshape(key_group.shape[0], 2, head_dim)
    value_triple = value_group.reshape(value_group.shape[0], 2, head_dim)
    triple_gradient = grad_group.reshape(grad_group.shape[0], 2, head_dim)
    attention_scores = group_scores(query_group, key_group, mask, level_weight)
    attention_probabilities = jnp.exp(attention_scores - log_total[..., None])
    grad_probs = jnp.einsum(
        "cse,jse->scj", triple_gradient, value_triple, preferred_element_type=jnp.float32
    )
    delta_sum = jnp.sum(attention_probabilities * grad_probs, axis=-1, keepdims=True)
    score_gradient = (attention_probabilities * (grad_probs - delta_sum)).astype(jnp.bfloat16)
    score_scale = 1.0 / math.sqrt(head_dim)
    grad_query = (
        jnp.einsum("fao,ofx->afx", score_gradient, key_triple, preferred_element_type=jnp.float32)
        * score_scale
    )
    grad_key = (
        jnp.einsum("lsk,sli->kli", score_gradient, query_triple, preferred_element_type=jnp.float32)
        * score_scale
    )
    grad_value = jnp.einsum(
        "lsk,sli->kli",
        attention_probabilities.astype(jnp.bfloat16),
        triple_gradient,
        preferred_element_type=jnp.float32,
    )
    return (
        grad_query.reshape(query_group.shape[0], 2 * head_dim),
        grad_key.reshape(key_group.shape[0], 2 * head_dim),
        grad_value.reshape(key_group.shape[0], 2 * head_dim),
    )


def shards(
    layer_input,
    doc_lengths,
    ln1_gain,
    ln1_bias,
    qkv_weight,
    query_bias,
    value_bias,
    out_weight,
    out_bias,
    ln2_gain,
    ln2_bias,
    up_weight,
    up_bias,
    down_weight,
    down_bias,
    cotangent,
):
    gathered = (
        lax.all_gather(ln1_gain, "fsdp", axis=0, tiled=True),
        lax.all_gather(ln1_bias, "fsdp", axis=0, tiled=True),
        lax.all_gather(qkv_weight, "fsdp", axis=0, tiled=True),
        lax.all_gather(query_bias, "fsdp", axis=0, tiled=True),
        lax.all_gather(value_bias, "fsdp", axis=0, tiled=True),
        lax.all_gather(out_weight, "fsdp", axis=0, tiled=True),
        lax.all_gather(out_bias, "fsdp", axis=0, tiled=True),
        lax.all_gather(ln2_gain, "fsdp", axis=0, tiled=True),
        lax.all_gather(ln2_bias, "fsdp", axis=0, tiled=True),
        lax.all_gather(up_weight, "fsdp", axis=0, tiled=True),
        lax.all_gather(up_bias, "fsdp", axis=0, tiled=True),
        lax.all_gather(down_weight, "fsdp", axis=0, tiled=True),
        lax.all_gather(down_bias, "fsdp", axis=0, tiled=True),
    )
    gain_first = gathered[0].astype(jnp.float32)
    shift_first = gathered[1].astype(jnp.float32)
    qkv_full = gathered[2]
    bias_row = jnp.concatenate([gathered[3], jnp.zeros_like(gathered[3]), gathered[4]]).astype(
        jnp.float32
    )
    out_full = gathered[5]
    out_shift = gathered[6].astype(jnp.float32)
    gain_second = gathered[7].astype(jnp.float32)
    shift_second = gathered[8].astype(jnp.float32)
    up_full = gathered[9]
    up_shift = gathered[10].astype(jnp.float32)
    down_full = gathered[11]
    down_shift = gathered[12].astype(jnp.float32)
    rows_dev = layer_input.shape[1]
    model_width = layer_input.shape[2]
    total = rows_dev * lax.axis_size("ctx")
    offset = lax.axis_index("ctx") * rows_dev
    positions = offset + jnp.arange(rows_dev, dtype=jnp.int32)
    starts = jnp.cumsum(doc_lengths[0]) - doc_lengths[0]
    rows = layer_input[0].astype(jnp.float32)
    normed, scaled_first, inverse_first = norm_forward(rows, gain_first, shift_first)
    normed_first = normed.astype(jnp.bfloat16)
    qkv = (jnp.dot(normed_first, qkv_full, preferred_element_type=jnp.float32) + bias_row).astype(
        jnp.bfloat16
    )
    queries = qkv[:, :model_width]
    level_rows = [qkv[:, model_width:]]
    for level_num in range(1, NEAR + 1):
        level_rows.append(pair_mean(level_rows[-1].astype(jnp.float32)).astype(jnp.bfloat16))
    tail_send = jnp.concatenate(
        [level_rows[level_num][-BLOCK:] for level_num in range(NEAR)], axis=0
    )
    head_send = jnp.concatenate(
        [level_rows[level_num][:BLOCK] for level_num in range(NEAR)], axis=0
    )
    from_left = shifted(tail_send, "ctx", 1)
    from_right = shifted(head_send, "ctx", -1)
    far_base = lax.all_gather(level_rows[NEAR], "ctx", axis=0, tiled=True)
    far_rows = [far_base]
    for level_num in range(NEAR + 1, LEVELS):
        far_rows.append(pair_mean(far_rows[-1].astype(jnp.float32)).astype(jnp.bfloat16))
    key_parts, first_parts, level_parts, span_parts = ([], [], [], [])
    for level_num in range(NEAR):
        level_span = 2**level_num
        local_count = rows_dev // level_span
        key_parts += [
            from_left[level_num * BLOCK : (level_num + 1) * BLOCK],
            level_rows[level_num],
            from_right[level_num * BLOCK : (level_num + 1) * BLOCK],
        ]
        first_parts += [
            offset - BLOCK * level_span + jnp.arange(BLOCK, dtype=jnp.int32) * level_span,
            offset + jnp.arange(local_count, dtype=jnp.int32) * level_span,
            offset + rows_dev + jnp.arange(BLOCK, dtype=jnp.int32) * level_span,
        ]
        level_parts.append(jnp.full((2 * BLOCK + local_count,), level_num, jnp.int32))
        span_parts.append(jnp.full((2 * BLOCK + local_count,), level_span, jnp.int32))
    window_starts, window_sizes = ([], [])
    for level_num in range(NEAR, LEVELS):
        level_span = 2**level_num
        level_count = total // level_span
        window_size = min(level_count, rows_dev // level_span + 4 * BLOCK)
        window_start = (offset // (BLOCK * level_span) - 1) * BLOCK
        window_start = jnp.clip(window_start, 0, level_count - window_size)
        window_starts.append(window_start)
        window_sizes.append(window_size)
        key_parts.append(
            lax.dynamic_slice_in_dim(far_rows[level_num - NEAR], window_start, window_size, 0)
        )
        first_parts.append((window_start + jnp.arange(window_size, dtype=jnp.int32)) * level_span)
        level_parts.append(jnp.full((window_size,), level_num, jnp.int32))
        span_parts.append(jnp.full((window_size,), level_span, jnp.int32))
    key_row_block = jnp.concatenate(key_parts, axis=0)
    key_first = jnp.concatenate(first_parts)
    key_level = jnp.concatenate(level_parts)
    key_span = jnp.concatenate(span_parts)
    mask = allowed(positions, key_first, key_level, key_span, starts, total)
    level_weight = key_level.astype(jnp.float32) * math.log(2.0)
    query_groups = head_groups(queries)
    key_groups = head_groups(key_row_block[:, :model_width])
    value_groups = head_groups(key_row_block[:, model_width:])
    attended_groups, log_totals = lax.map(
        partial(group_forward, mask=mask, level_weight=level_weight),
        (query_groups, key_groups, value_groups),
    )
    attended_output = ungroup(attended_groups).astype(jnp.bfloat16)
    middle = (
        rows + jnp.dot(attended_output, out_full, preferred_element_type=jnp.float32) + out_shift
    )
    normed, scaled_second, inverse_second = norm_forward(middle, gain_second, shift_second)
    normed_second = normed.astype(jnp.bfloat16)
    pre = jnp.dot(normed_second, up_full, preferred_element_type=jnp.float32) + up_shift
    hidden = jax.nn.gelu(pre, approximate=False).astype(jnp.bfloat16)
    output = (
        middle + jnp.dot(hidden, down_full, preferred_element_type=jnp.float32) + down_shift
    ).astype(jnp.bfloat16)
    grad_low = cotangent[0]
    grad_out = grad_low.astype(jnp.float32)
    down_weight_grad = contract_rows(hidden, grad_low)
    down_bias_grad = jnp.sum(grad_out, axis=0)
    grad_hidden = times_transpose(grad_low, down_full)
    grad_pre = (grad_hidden * gelu_slope(pre)).astype(jnp.bfloat16)
    up_weight_grad = contract_rows(normed_second, grad_pre)
    up_bias_grad = jnp.sum(grad_pre.astype(jnp.float32), axis=0)
    grad_norm_in, gain_second_grad, shift_second_grad = norm_backward(
        times_transpose(grad_pre, up_full), scaled_second, inverse_second, gain_second
    )
    grad_middle = grad_out + grad_norm_in
    grad_proj = grad_middle.astype(jnp.bfloat16)
    out_weight_grad = contract_rows(attended_output, grad_proj)
    out_bias_grad = jnp.sum(grad_proj.astype(jnp.float32), axis=0)
    grad_attended = times_transpose(grad_proj, out_full).astype(jnp.bfloat16)
    grad_query_groups, grad_key_groups, grad_value_groups = lax.map(
        partial(group_backward, mask=mask, level_weight=level_weight),
        (query_groups, key_groups, value_groups, head_groups(grad_attended), log_totals),
    )
    grad_query = ungroup(grad_query_groups)
    grad_entries = jnp.concatenate([ungroup(grad_key_groups), ungroup(grad_value_groups)], axis=1)
    cursor = 0
    tail_grads, local_grads, head_grads, far_grads = ([], [], [], [])
    for level_num in range(NEAR):
        local_count = rows_dev // 2**level_num
        tail_grads.append(grad_entries[cursor : cursor + BLOCK])
        cursor += BLOCK
        local_grads.append(grad_entries[cursor : cursor + local_count])
        cursor += local_count
        head_grads.append(grad_entries[cursor : cursor + BLOCK])
        cursor += BLOCK
    for level_num in range(NEAR, LEVELS):
        level_count = total // 2**level_num
        window_size = window_sizes[level_num - NEAR]
        window_grad = grad_entries[cursor : cursor + window_size]
        cursor += window_size
        placed = jnp.zeros((level_count, 2 * model_width), jnp.float32)
        far_grads.append(
            lax.dynamic_update_slice_in_dim(placed, window_grad, window_starts[level_num - NEAR], 0)
        )
    carry_grad = far_grads[-1]
    for level_num in range(LEVELS - 2, NEAR - 1, -1):
        carry_grad = far_grads[level_num - NEAR] + spread_back(carry_grad)
    base_grad = lax.psum_scatter(carry_grad, "ctx", scatter_dimension=0, tiled=True)
    returned_tail = shifted(jnp.concatenate(tail_grads, axis=0), "ctx", -1)
    returned_head = shifted(jnp.concatenate(head_grads, axis=0), "ctx", 1)
    carry_grad = base_grad
    for level_num in range(NEAR - 1, -1, -1):
        local_count = rows_dev // 2**level_num
        zero_rows = jnp.zeros((local_count - BLOCK, 2 * model_width), jnp.float32)
        head_part = jnp.concatenate(
            [returned_head[level_num * BLOCK : (level_num + 1) * BLOCK], zero_rows], axis=0
        )
        tail_part = jnp.concatenate(
            [zero_rows, returned_tail[level_num * BLOCK : (level_num + 1) * BLOCK]], axis=0
        )
        carry_grad = local_grads[level_num] + spread_back(carry_grad) + head_part + tail_part
    grad_qkv = jnp.concatenate([grad_query, carry_grad], axis=1).astype(jnp.bfloat16)
    qkv_weight_grad = contract_rows(normed_first, grad_qkv)
    grad_qkv_wide = grad_qkv.astype(jnp.float32)
    query_bias_grad = jnp.sum(grad_qkv_wide[:, :model_width], axis=0)
    value_bias_grad = jnp.sum(grad_qkv_wide[:, 2 * model_width :], axis=0)
    grad_norm_first, gain_first_grad, shift_first_grad = norm_backward(
        times_transpose(grad_qkv, qkv_full), scaled_first, inverse_first, gain_first
    )
    input_grad = grad_middle + grad_norm_first
    grads = (
        gain_first_grad,
        shift_first_grad,
        qkv_weight_grad,
        query_bias_grad,
        value_bias_grad,
        out_weight_grad,
        out_bias_grad,
        gain_second_grad,
        shift_second_grad,
        up_weight_grad,
        up_bias_grad,
        down_weight_grad,
        down_bias_grad,
    )
    owned = (
        lax.psum_scatter(grads[0], "fsdp", scatter_dimension=0, tiled=True),
        lax.psum_scatter(grads[1], "fsdp", scatter_dimension=0, tiled=True),
        lax.psum_scatter(grads[2], "fsdp", scatter_dimension=0, tiled=True),
        lax.psum_scatter(grads[3], "fsdp", scatter_dimension=0, tiled=True),
        lax.psum_scatter(grads[4], "fsdp", scatter_dimension=0, tiled=True),
        lax.psum_scatter(grads[5], "fsdp", scatter_dimension=0, tiled=True),
        lax.psum_scatter(grads[6], "fsdp", scatter_dimension=0, tiled=True),
        lax.psum_scatter(grads[7], "fsdp", scatter_dimension=0, tiled=True),
        lax.psum_scatter(grads[8], "fsdp", scatter_dimension=0, tiled=True),
        lax.psum_scatter(grads[9], "fsdp", scatter_dimension=0, tiled=True),
        lax.psum_scatter(grads[10], "fsdp", scatter_dimension=0, tiled=True),
        lax.psum_scatter(grads[11], "fsdp", scatter_dimension=0, tiled=True),
        lax.psum_scatter(grads[12], "fsdp", scatter_dimension=0, tiled=True),
    )
    summed = lax.psum(
        (
            owned[0],
            owned[1],
            owned[2],
            owned[3],
            owned[4],
            owned[5],
            owned[6],
            owned[7],
            owned[8],
            owned[9],
            owned[10],
            owned[11],
            owned[12],
        ),
        "ctx",
    )
    return (
        output[None],
        input_grad[None],
        summed[0],
        summed[1],
        summed[2],
        summed[3],
        summed[4],
        summed[5],
        summed[6],
        summed[7],
        summed[8],
        summed[9],
        summed[10],
        summed[11],
        summed[12],
    )


def solution(mesh):
    placed = (
        P("fsdp", "ctx", None),
        P("fsdp", None),
        P("fsdp"),
        P("fsdp"),
        P("fsdp", None),
        P("fsdp"),
        P("fsdp"),
        P("fsdp", None),
        P("fsdp"),
        P("fsdp"),
        P("fsdp"),
        P("fsdp", None),
        P("fsdp"),
        P("fsdp", None),
        P("fsdp"),
        P("fsdp", "ctx", None),
    )
    return jax.shard_map(
        shards,
        mesh=mesh,
        in_specs=placed,
        out_specs=(
            P("fsdp", "ctx", None),
            P("fsdp", "ctx", None),
            P("fsdp"),
            P("fsdp"),
            P("fsdp", None),
            P("fsdp"),
            P("fsdp"),
            P("fsdp", None),
            P("fsdp"),
            P("fsdp"),
            P("fsdp"),
            P("fsdp", None),
            P("fsdp"),
            P("fsdp", None),
            P("fsdp"),
        ),
        check_vma=False,
    )
```

profile of v0, /device:TPU:0, one launch (start us, length us, event | category | flops | bytes accessed | tf_op | source)
XLA Modules:
  0.0 1184.9 jit_solution(4701927021815699515)
XLA Ops:
  53.7 16.0 %reshape.1187 = f32[256,2,1024]{2,1,0:T(2,128)S(1)} reshape(bf16[512,1,1024]{2,0,1:T(8,128)(2,1)S(1)} %fusion.62) | data formatting | bytes 3145728 | tf_op jit(solution)/shard_map/convert_element_type | solution.py:235
  77.7 206.4 %fusion.16 = pred[1024,2464]{0,1:T(8,128)(4,1)} fusion(s32[2464]{0:T(1024)S(1)} %copy-done.21, s32[2464]{0:T(1024)S(1)} %copy-done.22, s32[1024]{0:T(1024)S(1)} %bitcast.277, s32[1024]{0:T(1024)S(1)} %broadcast_add_fusion, s32[2464]{0:T(1024)S(1)} %get-tuple-element.302, s32[2464]{0:T(1024)S(1)} %get-tuple-element.303, s32[2464]{0:T(1024)S(1)} %get-tuple-element.301, ...), kind=kLoop, calls=%fused_computation.77 | loop fusion | flops 58032128 | bytes 2584096 | tf_op jit(solution)/shard_map/and | solution.py:70
  362.1 115.5 %while.26 = (s32[]{:T(128)}, bf16[4,1024,128]{1,2,0:T(8,128)(2,1)}, f32[4,2,1024]{2,1,0:T(2,128)}, bf16[4,2464,128]{1,2,0:T(8,128)(2,1)}, pred[1024,2464]{0,1:T(...) while((s32[]{:T(128)}, bf16[4,1024,128]{1,2,0:T(8,128)(2,1)}, ...), condition=%wide.region_9.12_spmd, body=%wide.region_6.11_spmd.sunk | while | flops 1367537664 | bytes 73577456 | solution.py:288
  480.6 24.5 %fusion.19 = (bf16[1024,2048]{1,0:T(8,128)(2,1)}, f32[1024,2048]{1,0:T(8,128)}) fusion(f32[2048]{0:T(1024)S(1)} %bitcast.278, bf16[512,2048]{1,0:T(8,128)(2,1)} %all-gather.17.cloned.1.call-done, f32[1024,512]{0,1:T(8,128)S(1)} %get-tuple-element.305, f32[512]{0:T(512)S(1)} %bitcast.284, f32[512]{0:T(512)S(1)} %bitcast.269, f32[1024]{0:T(1024)S(1)} %add_rsqrt_fusion, ...), kind=kOutput, calls=%fused_computation.80 | convolution fusion | flops 2288517120 | bytes 16797696 | tf_op jit(solution)/shard_map/dot_general | solution.py:298
  528.9 242.7 %while.27 = (s32[]{:T(128)}, bf16[4,1024,128]{1,2,0:T(8,128)(2,1)}, f32[4,2464,128]{1,2,0:T(8,128)}, f32[4,2464,128]{1,2,0:T(8,128)}, bf16[4,2464,128]{1,2,0:T(8...) while((s32[]{:T(128)}, bf16[4,1024,128]{1,2,0:T(8,128)(2,1)}, ...), condition=%wide.region_16.19_spmd, body=%wide.region_14.18_spmd.sunk | while | flops 3280652288 | bytes 168929056 | solution.py:319
  541.2 17.2 %multiply_reduce_fusion.7 = (f32[2,1024]{1,0:T(2,128)S(1)}, f32[2,1024,2464]{1,2,0:T(8,128)}) fusion(f32[2,1024,2464]{1,2,0:T(8,128)} %fusion.214, f32[2,1024]{1,0:T(2,128)S(1)} %dynamic-slice_bitcast_fusion.2, f32[2464]{0:T(1024)S(1)} %get-tuple-element.508, bf16[1024,2,64]{0,2,1:T(8,128)(2,1)S(1)} %bitcast.257, ...), kind=kOutput, calls=%fused_computation.14.clone.1 | convolution fusion | flops 676198400 | bytes 43812480 | tf_op jit(solution)/shard_map/while/body/eval_jaxpr/cse,jse->scj/dot_general | solution.py:107
  558.5 14.0 %multiply_convert_fusion.2 = bf16[2,1024,2464]{1,2,0:T(8,128)(2,1)S(1)} fusion(f32[2,1024,2464]{1,2,0:T(8,128)} %get-tuple-element.442, f32[2,1024,2464]{1,2,0:T(8,128)} %fusion.214, f32[2,1024]{1,0:T(2,128)S(1)} %get-tuple-element.443), kind=kLoop, calls=%fused_computation.13.clone.1 | loop fusion | flops 15138816 | bytes 50470912 | tf_op jit(solution)/shard_map/while/body/eval_jaxpr/convert_element_type | solution.py:150
  572.4 9.8 fusion.215
  601.9 17.2 %multiply_reduce_fusion.7 = (f32[2,1024]{1,0:T(2,128)S(1)}, f32[2,1024,2464]{1,2,0:T(8,128)}) fusion(f32[2,1024,2464]{1,2,0:T(8,128)} %fusion.214, f32[2,1024]{1,0:T(2,128)S(1)} %dynamic-slice_bitcast_fusion.2, f32[2464]{0:T(1024)S(1)} %get-tuple-element.508, bf16[1024,2,64]{0,2,1:T(8,128)(2,1)S(1)} %bitcast.257, ...), kind=kOutput, calls=%fused_computation.14.clone.1 | convolution fusion | flops 676198400 | bytes 43812480 | tf_op jit(solution)/shard_map/while/body/eval_jaxpr/cse,jse->scj/dot_general | solution.py:107
  619.1 14.0 %multiply_convert_fusion.2 = bf16[2,1024,2464]{1,2,0:T(8,128)(2,1)S(1)} fusion(f32[2,1024,2464]{1,2,0:T(8,128)} %get-tuple-element.442, f32[2,1024,2464]{1,2,0:T(8,128)} %fusion.214, f32[2,1024]{1,0:T(2,128)S(1)} %get-tuple-element.443), kind=kLoop, calls=%fused_computation.13.clone.1 | loop fusion | flops 15138816 | bytes 50470912 | tf_op jit(solution)/shard_map/while/body/eval_jaxpr/convert_element_type | solution.py:150
  633.1 9.8 fusion.215
  662.5 17.2 %multiply_reduce_fusion.7 = (f32[2,1024]{1,0:T(2,128)S(1)}, f32[2,1024,2464]{1,2,0:T(8,128)}) fusion(f32[2,1024,2464]{1,2,0:T(8,128)} %fusion.214, f32[2,1024]{1,0:T(2,128)S(1)} %dynamic-slice_bitcast_fusion.2, f32[2464]{0:T(1024)S(1)} %get-tuple-element.508, bf16[1024,2,64]{0,2,1:T(8,128)(2,1)S(1)} %bitcast.257, ...), kind=kOutput, calls=%fused_computation.14.clone.1 | convolution fusion | flops 676198400 | bytes 43812480 | tf_op jit(solution)/shard_map/while/body/eval_jaxpr/cse,jse->scj/dot_general | solution.py:107
  679.8 14.0 %multiply_convert_fusion.2 = bf16[2,1024,2464]{1,2,0:T(8,128)(2,1)S(1)} fusion(f32[2,1024,2464]{1,2,0:T(8,128)} %get-tuple-element.442, f32[2,1024,2464]{1,2,0:T(8,128)} %fusion.214, f32[2,1024]{1,0:T(2,128)S(1)} %get-tuple-element.443), kind=kLoop, calls=%fused_computation.13.clone.1 | loop fusion | flops 15138816 | bytes 50470912 | tf_op jit(solution)/shard_map/while/body/eval_jaxpr/convert_element_type | solution.py:150
  693.7 9.8 fusion.215
  723.3 17.2 %multiply_reduce_fusion.7 = (f32[2,1024]{1,0:T(2,128)S(1)}, f32[2,1024,2464]{1,2,0:T(8,128)}) fusion(f32[2,1024,2464]{1,2,0:T(8,128)} %fusion.214, f32[2,1024]{1,0:T(2,128)S(1)} %dynamic-slice_bitcast_fusion.2, f32[2464]{0:T(1024)S(1)} %get-tuple-element.508, bf16[1024,2,64]{0,2,1:T(8,128)(2,1)S(1)} %bitcast.257, ...), kind=kOutput, calls=%fused_computation.14.clone.1 | convolution fusion | flops 676198400 | bytes 43812480 | tf_op jit(solution)/shard_map/while/body/eval_jaxpr/cse,jse->scj/dot_general | solution.py:107
  740.5 14.0 %multiply_convert_fusion.2 = bf16[2,1024,2464]{1,2,0:T(8,128)(2,1)S(1)} fusion(f32[2,1024,2464]{1,2,0:T(8,128)} %get-tuple-element.442, f32[2,1024,2464]{1,2,0:T(8,128)} %fusion.214, f32[2,1024]{1,0:T(2,128)S(1)} %get-tuple-element.443), kind=kLoop, calls=%fused_computation.13.clone.1 | loop fusion | flops 15138816 | bytes 50470912 | tf_op jit(solution)/shard_map/while/body/eval_jaxpr/convert_element_type | solution.py:150
  754.5 9.8 fusion.215
  838.6 34.7 %reduce-scatter.6.cloned.1.call-done = f32[64,1024]{1,0:T(8,128)} async-done(((f32[512,1024]{1,0:T(8,128)}), f32[64,1024]{1,0:T(8,128)}) %reduce-scatter.6.cloned.1.call-update) | async-done | bytes 262160 | tf_op jit(solution)/shard_map/reduce_scatter | solution.py:347
  908.2 38.6 %reduce-scatter.14.cloned.1.call-done = f32[512,512]{1,0:T(8,128)} async-done(((f32[2048,512]{1,0:T(8,128)}), f32[512,512]{1,0:T(8,128)}) %reduce-scatter.14.cloned.1.call-update) | async-done | bytes 1048592 | tf_op jit(solution)/shard_map/reduce_scatter | solution.py:397
  946.9 47.0 %reduce-scatter.12.cloned.1.call-done = f32[128,2048]{1,0:T(8,128)} async-done(((f32[512,2048]{1,0:T(8,128)}), f32[128,2048]{1,0:T(8,128)}) %reduce-scatter.12.cloned.1.call-update) | async-done | bytes 1048592 | tf_op jit(solution)/shard_map/reduce_scatter | solution.py:395
  993.9 40.7 %reduce-scatter.8.cloned.1.call-done = f32[128,1536]{1,0:T(8,128)} async-done(((f32[512,1536]{1,0:T(8,128)}), f32[128,1536]{1,0:T(8,128)}) %reduce-scatter.8.cloned.1.call-update) | async-done | bytes 786448 | tf_op jit(solution)/shard_map/reduce_scatter | solution.py:388
  1071.4 11.2 all-reduce.19
  1083.3 22.1 %all-reduce.17 = (f32[128]{0:T(128)}, f32[128]{0:T(128)}, f32[128]{0:T(128)}, f32[128]{0:T(128)}, f32[128]{0:T(128)}, /*index=5*/f32[128]{0:T(128)}, f32[128]{0:T(128)}, f32[512]{0:T(512)}, f32[128]{0:T(128)}) all-reduce(f32[128]{0:T(128)S(1)} %dynamic-slice.7, f32[128]{0:T(128)S(1)} %dynamic-slice.9, ...), channel_id=1, replica_groups=mesh['ctx'=8,'fsdp'=4] {'ctx'}, use_global_device_ids=true, to_apply=%region_22.25 | all-reduce | flops 1536 | bytes 12288 | tf_op jit(solution)/shard_map/psum | solution.py:400
  1105.3 64.2 %all-reduce.22.cloned.1.call-done = (f32[128,1536]{1,0:T(8,128)}, f32[128,512]{1,0:T(8,128)}, f32[128,2048]{1,0:T(8,128)}, f32[512,512]{1,0:T(8,128)}) async-done(((f32[128,1536]{1,0:T(8,128)}, f32[128,512]{1,0:T(8,128)}, f32[128,2048]{1,0:T(8,128)}, f32[512,512]{1,0:T(8,128)}), (f32[128,1536]{1,0:T(8,128)}, f32[128,512]{1,0:T(8,128)}, f32[128,2048]{1,0:T(8,128)}, ...) | async-done | bytes 3145744 | tf_op jit(solution)/shard_map/psum | solution.py:400
  (398 shorter events, 497.8 us)
Async XLA Ops:
  7.2 24.8 %all-gather.15.cloned.1.call-start = ((), (), s32[]{:S(2)}) async-start(), calls=%async_computation.5 | async-start | bytes 1966080 | tf_op jit(solution)/shard_map/all_gather | solution.py:194
  7.9 328.9 %all-gather.21.cloned.1.call-start = ((), (), s32[]{:S(2)}) async-start(), calls=%async_computation.13 | async-start | bytes 1179648 | tf_op jit(solution)/shard_map/all_gather | solution.py:244
  72.5 216.0 %copy-start.16 = (bf16[128,512]{1,0:T(8,128)(2,1)S(1)}, bf16[128,512]{1,0:T(8,128)(2,1)}, u32[]{:S(2)}) copy-start(bf16[128,512]{1,0:T(8,128)(2,1)} %param.31) | copy-start | bytes 393220
  73.4 222.9 %copy-start.45 = (bf16[128]{0:T(256)(128)(2,1)S(1)}, bf16[128]{0:T(256)(128)(2,1)}, u32[]{:S(2)}) copy-start(bf16[128]{0:T(256)(128)(2,1)} %param.32) | copy-start | bytes 772
  73.4 228.5 %copy-start.46 = (bf16[128]{0:T(256)(128)(2,1)S(1)}, bf16[128]{0:T(256)(128)(2,1)}, u32[]{:S(2)}) copy-start(bf16[128]{0:T(256)(128)(2,1)} %param.33) | copy-start | bytes 772
  73.4 234.1 %copy-start.47 = (bf16[128]{0:T(256)(128)(2,1)S(1)}, bf16[128]{0:T(256)(128)(2,1)}, u32[]{:S(2)}) copy-start(bf16[128]{0:T(256)(128)(2,1)} %param.34) | copy-start | bytes 772
  73.4 239.7 %copy-start.44 = (bf16[512]{0:T(512)(128)(2,1)S(1)}, bf16[512]{0:T(512)(128)(2,1)}, u32[]{:S(2)}) copy-start(bf16[512]{0:T(512)(128)(2,1)} %param.36) | copy-start | bytes 3076
  75.1 246.0 %slice-start = ((bf16[1024,1536]{1,0:T(8,128)(2,1)}), bf16[1024,512]{1,0:T(8,128)(2,1)S(1)}, s32[]{:S(2)}) async-start(bf16[1024,1536]{1,0:T(8,128)(2,1)} %copy-done.6), calls=%async_computation.15 | async-start | bytes 2097152 | tf_op jit(solution)/shard_map/slice | solution.py:232
  75.1 405.4 %all-gather.17.cloned.1.call-start = ((), (), s32[]{:S(2)}) async-start(), calls=%async_computation.6 | async-start | bytes 2621440 | tf_op jit(solution)/shard_map/all_gather | solution.py:201
  75.9 429.2 %all-gather.19.cloned.1.call-start = ((), (), s32[]{:S(2)}) async-start(), calls=%async_computation.7 | async-start | bytes 2621440 | tf_op jit(solution)/shard_map/all_gather | solution.py:203
  76.5 796.8 %reduce-scatter.6.cloned.1.call-start = ((), (), s32[]{:S(2)}) async-start(), calls=%async_computation.8 | async-start | bytes 2359296 | tf_op jit(solution)/shard_map/reduce_scatter | solution.py:347
  284.9 38.8 %collective-permute-start = (bf16[64,1024]{1,0:T(8,128)(2,1)S(1)}, bf16[64,1024]{1,0:T(8,128)(2,1)S(1)}, u32[]{:S(2)}, u32[]{:S(2)}) collective-permute-start(bf16[64,1024]{1,0:T(8,128)(2,1)S(1)} %pad_maximum_fusion.4), channel_id=1, source_target_pairs={{0,4},{4,8},{8,12},{12,16},{16,20},{20,24},{24,28},{1,5},{5,9},{9,... | collective-permute-start | bytes 393224 | tf_op jit(solution)/shard_map/ppermute | solution.py:24
  322.4 7.6 collective-permute-start.1
  362.1 115.5 %copy-start.43 = (f32[4,1,128]{2,1,0:T(1,128)S(1)}, f32[4,1,128]{2,1,0:T(1,128)}, u32[]{:S(2)}) copy-start(f32[4,1,128]{2,1,0:T(1,128)} %convert_element_type.280) | copy-start | bytes 6148
  480.1 43.8 %copy-start.4 = (f32[1024,512]{0,1:T(8,128)}, f32[1024,512]{0,1:T(8,128)S(1)}, u32[]{:S(2)}) copy-start(f32[1024,512]{0,1:T(8,128)S(1)} %get-tuple-element.305) | copy-start | bytes 6291460
  801.9 106.4 %reduce-scatter.10.cloned.1.call-start = ((), (), s32[]{:S(2)}) async-start(), calls=%async_computation.10 | async-start | bytes 1310720 | tf_op jit(solution)/shard_map/reduce_scatter | solution.py:391
  803.7 143.2 %reduce-scatter.14.cloned.1.call-start = ((), (), s32[]{:S(2)}) async-start(), calls=%async_computation.12 | async-start | bytes 5242880 | tf_op jit(solution)/shard_map/reduce_scatter | solution.py:397
  810.7 183.2 %reduce-scatter.12.cloned.1.call-start = ((), (), s32[]{:S(2)}) async-start(), calls=%async_computation.11 | async-start | bytes 5242880 | tf_op jit(solution)/shard_map/reduce_scatter | solution.py:395
  818.1 216.5 %reduce-scatter.8.cloned.1.call-start = ((), (), s32[]{:S(2)}) async-start(), calls=%async_computation.9 | async-start | bytes 3932160 | tf_op jit(solution)/shard_map/reduce_scatter | solution.py:388
  819.1 16.9 %collective-permute-start.2 = (f32[64,1024]{1,0:T(8,128)S(1)}, f32[64,1024]{1,0:T(8,128)}, u32[]{:S(2)}, u32[]{:S(2)}) collective-permute-start(f32[64,1024]{1,0:T(8,128)S(1)} %pad_maximum_fusion.3), channel_id=1, source_target_pairs={{0,4},{4,8},{8,12},{12,16},{16,20},{20,24},{24,28},{1,5},{5,9},{9,... | collective-permute-start | bytes 786440 | tf_op jit(solution)/shard_map/ppermute | solution.py:24
  824.1 12.9 %collective-permute-start.3 = (f32[64,1024]{1,0:T(8,128)}, f32[64,1024]{1,0:T(8,128)}, u32[]{:S(2)}, u32[]{:S(2)}) collective-permute-start(f32[64,1024]{1,0:T(8,128)} %get-tuple-element.255), channel_id=1, source_target_pairs={{4,0},{8,4},{12,8},{16,12},{20,16},{24,20},{28,24},{5,1},{9,5},{13... | collective-permute-start | bytes 786440 | tf_op jit(solution)/shard_map/ppermute | solution.py:24
  908.1 126.5 %copy-start.51 = (u32[32]{0:T(128)S(1)}, u32[32]{0:T(128)}, u32[]{:S(2)}) copy-start(u32[32]{0:T(128)} %constant.453) | copy-start | bytes 388
  908.1 128.4 %copy-start.48 = (bf16[128]{0:T(256)(128)(2,1)S(1)}, bf16[128]{0:T(256)(128)(2,1)}, u32[]{:S(2)}) copy-start(bf16[128]{0:T(256)(128)(2,1)} %param.38) | copy-start | bytes 772
  908.2 261.4 %all-reduce.22.cloned.1.call-start = ((), (), s32[]{:S(2)}) async-start(), calls=%async_computation.14 | async-start | bytes 6291456 | tf_op jit(solution)/shard_map/psum | solution.py:400
  (44 other events, 332.9 us)
Sparse Core Ops, SparseCore 0:
  9.6 22.3 all-gather.14
  75.3 41.7 all-gather.20
  118.6 21.3 all-gather.16
  141.5 22.5 all-gather.18
  802.0 71.2 reduce-scatter.5
  875.7 23.9 reduce-scatter.9
  902.3 44.5 reduce-scatter.13
  949.4 44.4 reduce-scatter.11
  996.6 37.9 reduce-scatter.7
  1038.3 131.1 all-reduce.21
where the time goes:
time: 1200 us; the launch traced here: 1180 us
  other arithmetic  341 us (28%)
  matrix products  304 us (25%)
  waiting for transfers between devices  239 us (20%)
  local copies, waits for them, and re-layouts  184 us (15%)
  blocking collectives  88.1 us (7%)
  between operations  17 us (1%)
    and x1, other arithmetic, allowed(): return level_ok & (key_doc[None, :] == query_doc[:, None])  206 us
    dot_general x8, matrix products, group_scores(): jnp.einsum('cse,jse->scj', query_group.reshape(query_group.shape[0], 2, h...  96.7 us
    psum x1, waiting for transfers between devices, shards(): lax.psum((owned[0], owned[1], owned[2], owned[3], owned[4], owned[5], own...  64.2 us
    convert_element_type x4, other arithmetic, group_backward(): (attention_probabilities * (grad_probs - delta_sum)).astype(jnp.bfloat16)  55.8 us
    reduce_scatter x1, waiting for transfers between devices, shards(): lax.psum_scatter(grads[9], 'fsdp', scatter_dimension=0, tiled=True)  47 us
    reduce_scatter x1, waiting for transfers between devices, shards(): lax.psum_scatter(grads[2], 'fsdp', scatter_dimension=0, tiled=True)  40.7 us
    dot_general x4, matrix products, group_backward(): jnp.einsum('lsk,sli->kli', attention_probabilities.astype(jnp.bfloat16),...  39.3 us
    reduce_scatter x1, waiting for transfers between devices, shards(): lax.psum_scatter(grads[11], 'fsdp', scatter_dimension=0, tiled=True)  38.6 us
  transfers between devices with their start and end apart: 14, of which 7 were waited for; matrix products, arithmetic and copies ran while one was open for 40% of the time, Pallas kernels for 0%

commit v1 on v0

v1 whole, which is shorter than its diff:
```python
from functools import partial
import math

import jax
import jax.numpy as jnp
from jax import lax
from jax.experimental import pallas as pl
from jax.experimental.pallas import tpu as pltpu
from jax.sharding import PartitionSpec as P

HEADS = 8
BLOCK = 16
LEVELS = 10
NEAR = 4
LOCAL = 7
CHUNK = 128
WIDTH = 512
PAIRS = HEADS // 2
MASKED = -1e30
EPSILON = 1e-05
VMEM_LIMIT = 56 * 1024 * 1024

f32 = jnp.float32
bf16 = jnp.bfloat16


def level_rows(rows, level):
    return rows // 2**level


def far_levels(total):
    return [l for l in range(LOCAL, LEVELS) if total // (BLOCK * 2**l) >= 2]


def extended_offsets(rows, far):
    offsets, cursor = [], 0
    for level in range(LOCAL):
        offsets.append(cursor)
        cursor += level_rows(rows, level) + 2 * BLOCK
    for _ in far:
        offsets.append(cursor)
        cursor += 2 * BLOCK
    return offsets, cursor


def slot_layout(far):
    parts = [(level, CHUNK // 2**level + 2 * BLOCK) for level in range(NEAR)]
    parts += [(level, BLOCK) for level in list(range(NEAR, LOCAL)) + far for _ in range(2)]
    return parts, sum(count for _, count in parts)


def slot_sources(rows, far, chunk):
    offsets, _ = extended_offsets(rows, far)
    sources = []
    for level in range(NEAR):
        sources.append((offsets[level] + chunk * (CHUNK // 2**level), CHUNK // 2**level + 2 * BLOCK))
    for level in range(NEAR, LOCAL):
        block = chunk // (BLOCK * 2**level // CHUNK)
        sources.append((offsets[level] + block * BLOCK, BLOCK))
        sources.append((offsets[level] + block * BLOCK + 2 * BLOCK, BLOCK))
    for at in range(len(far)):
        sources.append((offsets[LOCAL + at], BLOCK))
        sources.append((offsets[LOCAL + at] + BLOCK, BLOCK))
    return sources


def count_starts(positions, starts):
    total = jnp.zeros(positions.shape, jnp.int32)
    for at in range(starts.shape[0]):
        total = total + (starts[at] <= positions).astype(jnp.int32)
    return total - 1


def score_bias(rows, total, offset, starts, far):
    chunks = rows // CHUNK
    bases = offset + CHUNK * jnp.arange(chunks, dtype=jnp.int32)
    firsts, spans, levels = [], [], []
    for level in range(NEAR):
        span = 2**level
        count = CHUNK // span + 2 * BLOCK
        firsts.append(bases[:, None] + (jnp.arange(count, dtype=jnp.int32)[None, :] - BLOCK) * span)
        spans += [span] * count
        levels += [level] * count
    for level in list(range(NEAR, LOCAL)) + far:
        span = 2**level
        block = bases // (BLOCK * span)
        for side in (-1, 1):
            firsts.append(
                (block[:, None] + side) * (BLOCK * span)
                + jnp.arange(BLOCK, dtype=jnp.int32)[None, :] * span
            )
            spans += [span] * BLOCK
            levels += [level] * BLOCK
    first = jnp.concatenate(firsts, axis=1)
    span = jnp.array(spans, jnp.int32)[None, :]
    level = jnp.array(levels, jnp.int32)[None, :]
    inside = (first >= 0) & (first < total)
    first_doc = count_starts(first, starts)
    last_doc = count_starts(first + span - 1, starts)
    key_doc = jnp.where(inside & (first_doc == last_doc), first_doc, -2)
    query = bases[:, None] + jnp.arange(CHUNK, dtype=jnp.int32)[None, :]
    query_doc = count_starts(query, starts)
    shift = level + 4
    parent = jnp.maximum(shift - 1, 0)
    first3, shift3, parent3, query3 = (
        first[:, :, None],
        shift[:, :, None],
        parent[:, :, None],
        query[:, None, :],
    )
    gap = jnp.abs((first3 >> shift3) - (query3 >> shift3))
    parent_gap = jnp.abs((first3 >> parent3) - (query3 >> parent3))
    seen = jnp.where(level[:, :, None] == 0, gap <= 1, (gap == 1) & (parent_gap > 1))
    seen = seen & (key_doc[:, :, None] == query_doc[:, None, :])
    return jnp.where(seen, level[:, :, None].astype(f32) * math.log(2.0), MASKED)


def dot_nt(left, right):
    return lax.dot_general(left, right, (((1,), (1,)), ((), ())), preferred_element_type=f32)


def dot_tn(left, right):
    return lax.dot_general(left, right, (((0,), (0,)), ((), ())), preferred_element_type=f32)


def dot_nn(left, right):
    return jnp.dot(left, right, preferred_element_type=f32)


def pool_matrix(count):
    row = lax.broadcasted_iota(jnp.int32, (count // 2, count), 0)
    column = lax.broadcasted_iota(jnp.int32, (count // 2, count), 1)
    return jnp.where((column >> 1) == row, 0.5, 0.0).astype(bf16)


def spread_matrix(count):
    row = lax.broadcasted_iota(jnp.int32, (2 * count, count), 0)
    column = lax.broadcasted_iota(jnp.int32, (2 * count, count), 1)
    return jnp.where((row >> 1) == column, 0.5, 0.0).astype(bf16)


def spread(values):
    count = values.shape[0]
    tile = min(count, 128)
    matrix = spread_matrix(tile)
    high = values.astype(bf16)
    low = (values - high.astype(f32)).astype(bf16)
    parts = [
        dot_nn(matrix, high[at : at + tile]) + dot_nn(matrix, low[at : at + tile])
        for at in range(0, count, tile)
    ]
    return parts[0] if len(parts) == 1 else jnp.concatenate(parts, axis=0)


def norm_rows(values):
    mean = jnp.mean(values, axis=-1, keepdims=True)
    centred = values - mean
    variance = jnp.mean(centred * centred, axis=-1, keepdims=True)
    inverse = lax.rsqrt(variance + EPSILON)
    return centred * inverse, inverse


def norm_back(grad_out, scaled, inverse, gain):
    grad_scaled = grad_out * gain
    first = jnp.mean(grad_scaled, axis=-1, keepdims=True)
    second = jnp.mean(grad_scaled * scaled, axis=-1, keepdims=True)
    return inverse * (grad_scaled - first - scaled * second)


def split_heads(pair):
    lane = lax.broadcasted_iota(jnp.int32, pair.shape, 1)
    zero = jnp.zeros_like(pair)
    return jnp.concatenate([jnp.where(lane < 64, pair, zero), jnp.where(lane < 64, zero, pair)], axis=0)


def join_heads(stacked):
    rows = stacked.shape[0] // 2
    lane = lax.broadcasted_iota(jnp.int32, (rows, stacked.shape[1]), 1)
    return jnp.where(lane < 64, stacked[:rows], stacked[rows:])


def qkv_kernel(rows, x_ref, w_ref, bias_ref, gain_ref, shift_ref, normed_ref, q_ref, *level_refs):
    tail_ref, head_ref = level_refs[LOCAL], level_refs[LOCAL + 1]
    level_refs = level_refs[:LOCAL]
    tile = 256

    def body(at, _):
        start = pl.multiple_of(at * tile, tile)
        scaled, _ = norm_rows(x_ref[pl.ds(start, tile), :].astype(f32))
        normed = (scaled * gain_ref[...] + shift_ref[...]).astype(bf16)
        normed_ref[pl.ds(start, tile), :] = normed
        qkv = (dot_nn(normed, w_ref[...]) + bias_ref[...]).astype(bf16)
        q_ref[pl.ds(start, tile), :] = qkv[:, :WIDTH] * jnp.asarray(0.125, bf16)
        current = qkv[:, WIDTH:]
        level_refs[0][pl.ds(start, tile), :] = current
        for level in range(1, 5):
            count = tile // 2**level
            current = dot_nn(pool_matrix(2 * count), current).astype(bf16)
            level_refs[level][pl.ds(pl.multiple_of(at * count, count), count), :] = current
        return 0

    lax.fori_loop(0, rows // tile, body, 0)
    for level in range(5, LOCAL):
        below = level_refs[level - 1][...]
        level_refs[level][...] = dot_nn(pool_matrix(below.shape[0]), below).astype(bf16)
    for level in range(LOCAL):
        count = level_rows(rows, level)
        tail_ref[BLOCK * level : BLOCK * (level + 1), :] = level_refs[level][count - BLOCK :, :]
        head_ref[BLOCK * level : BLOCK * (level + 1), :] = level_refs[level][:BLOCK, :]


def vmem_specs(count):
    return [pl.BlockSpec(memory_space=pltpu.VMEM)] * count


def qkv_call(rows, x, weight, bias, gain, shift):
    shapes = [(rows, WIDTH), (rows, WIDTH)]
    shapes += [(level_rows(rows, level), 2 * WIDTH) for level in range(LOCAL)]
    shapes += [(BLOCK * LOCAL, 2 * WIDTH)] * 2
    return pl.pallas_call(
        partial(qkv_kernel, rows),
        out_shape=[jax.ShapeDtypeStruct(s, bf16) for s in shapes],
        in_specs=vmem_specs(5),
        out_specs=vmem_specs(len(shapes)),
        compiler_params=pltpu.CompilerParams(vmem_limit_bytes=VMEM_LIMIT),
        cost_estimate=pl.CostEstimate(flops=2 * rows * WIDTH * 3 * WIDTH, bytes_accessed=10 << 20, transcendentals=0),
        name="qkv_levels",
    )(x, weight, bias, gain, shift)


def assemble(rows, devices, far, here, level_refs, left_ref, right_ref, base_ref, ext_ref, far_ref):
    offsets, _ = extended_offsets(rows, far)
    for level in range(LOCAL):
        at, count = offsets[level], level_rows(rows, level)
        ext_ref[at : at + BLOCK, :] = left_ref[BLOCK * level : BLOCK * (level + 1), :]
        ext_ref[at + BLOCK : at + BLOCK + count, :] = level_refs[level][...]
        ext_ref[at + BLOCK + count : at + 2 * BLOCK + count, :] = right_ref[
            BLOCK * level : BLOCK * (level + 1), :
        ]
    current = base_ref[...]
    for index, level in enumerate(far):
        current = dot_nn(pool_matrix(current.shape[0]), current).astype(bf16)
        count = current.shape[0]
        far_ref[0:count, :] = current
        block = here >> (level - 6)
        last = count // BLOCK - 1
        for side, neighbour in enumerate((block - 1, block + 1)):
            start = pl.multiple_of(jnp.clip(neighbour, 0, last) * BLOCK, BLOCK)
            at = offsets[LOCAL + index] + side * BLOCK
            ext_ref[at : at + BLOCK, :] = far_ref[pl.ds(start, BLOCK), :]


def load_slots(rows, far, chunk, ext_ref, slots_ref):
    at = 0
    for start, count in slot_sources(rows, far, chunk):
        if not isinstance(start, int):
            start = pl.multiple_of(start, BLOCK)
        slots_ref[at : at + count, :] = ext_ref[pl.ds(start, count), :]
        at += count


def attend_kernel(rows, devices, far, here_ref, q_ref, bias_ref, *refs):
    level_refs, refs = refs[:LOCAL], refs[LOCAL:]
    left_ref, right_ref, base_ref, out_ref, log_ref, ext_ref, far_ref, slots_ref = refs
    chunk = pl.program_id(0)

    @pl.when(chunk == 0)
    def _():
        assemble(rows, devices, far, here_ref[0], level_refs, left_ref, right_ref, base_ref, ext_ref, far_ref)

    load_slots(rows, far, chunk, ext_ref, slots_ref)
    bias = bias_ref[0]
    bias = jnp.concatenate([bias, bias], axis=1)
    for pair in range(PAIRS):
        lanes = slice(128 * pair, 128 * (pair + 1))
        values = slots_ref[:, WIDTH + 128 * pair : WIDTH + 128 * (pair + 1)]
        scores = dot_nt(slots_ref[:, lanes], split_heads(q_ref[:, lanes])) + bias
        top = jnp.max(scores, axis=0, keepdims=True)
        exponent = jnp.exp(scores - top)
        total = jnp.sum(exponent, axis=0, keepdims=True)
        probs = (exponent * (1.0 / total)).astype(bf16)
        out_ref[:, lanes] = join_heads(dot_tn(probs, values)).astype(bf16)
        log_ref[0, pair : pair + 1, :] = top + jnp.log(total)


def attend_call(rows, devices, far, here, q, bias, levels, left, right, base):
    chunks = rows // CHUNK
    _, entries = extended_offsets(rows, far)
    _, slots = slot_layout(far)
    return pl.pallas_call(
        partial(attend_kernel, rows, devices, far),
        grid=(chunks,),
        out_shape=[
            jax.ShapeDtypeStruct((rows, WIDTH), bf16),
            jax.ShapeDtypeStruct((chunks, 8, 2 * CHUNK), f32),
        ],
        in_specs=[
            pl.BlockSpec(memory_space=pltpu.SMEM),
            pl.BlockSpec((CHUNK, WIDTH), lambda i: (i, 0)),
            pl.BlockSpec((1, slots, CHUNK), lambda i: (i, 0, 0)),
        ]
        + vmem_specs(LOCAL + 3),
        out_specs=[
            pl.BlockSpec((CHUNK, WIDTH), lambda i: (i, 0)),
            pl.BlockSpec((1, 8, 2 * CHUNK), lambda i: (i, 0, 0)),
        ],
        scratch_shapes=[
            pltpu.VMEM((entries, 2 * WIDTH), bf16),
            pltpu.VMEM((8 * devices, 2 * WIDTH), bf16),
            pltpu.VMEM((slots, 2 * WIDTH), bf16),
        ],
        compiler_params=pltpu.CompilerParams(vmem_limit_bytes=VMEM_LIMIT),
        cost_estimate=pl.CostEstimate(flops=16 << 30, bytes_accessed=12 << 20, transcendentals=4 << 20),
        name="attend",
    )(here, q, bias, *levels, left, right, base)


def attend_back_kernel(rows, devices, far, here_ref, q_ref, grad_ref, bias_ref, log_ref, *refs):
    level_refs, refs = refs[:LOCAL], refs[LOCAL:]
    left_ref, right_ref, base_ref, refs = refs[0], refs[1], refs[2], refs[3:]
    dq_ref, local_ref, to_left_ref, to_right_ref, to_far_ref = refs[:5]
    ext_ref, far_ref, slots_ref, acc_ref, tree_ref = refs[5:]
    chunk = pl.program_id(0)
    offsets, _ = extended_offsets(rows, far)

    @pl.when(chunk == 0)
    def _():
        assemble(rows, devices, far, here_ref[0], level_refs, left_ref, right_ref, base_ref, ext_ref, far_ref)
        acc_ref[...] = jnp.zeros_like(acc_ref)

    load_slots(rows, far, chunk, ext_ref, slots_ref)
    bias = bias_ref[0]
    bias = jnp.concatenate([bias, bias], axis=1)
    sources = slot_sources(rows, far, chunk)
    for pair in range(PAIRS):
        lanes = slice(128 * pair, 128 * (pair + 1))
        value_lanes = slice(WIDTH + 128 * pair, WIDTH + 128 * (pair + 1))
        keys, values = slots_ref[:, lanes], slots_ref[:, value_lanes]
        queries, grads = split_heads(q_ref[:, lanes]), split_heads(grad_ref[:, lanes])
        probs = jnp.exp(dot_nt(keys, queries) + bias - log_ref[0, pair : pair + 1, :])
        grad_probs = dot_nt(values, grads)
        delta = jnp.sum(probs * grad_probs, axis=0, keepdims=True)
        grad_scores = (probs * (grad_probs - delta)).astype(bf16)
        dq_ref[:, lanes] = (join_heads(dot_tn(grad_scores, keys)) * 0.125).astype(bf16)
        grad_keys = dot_nn(grad_scores, queries)
        grad_values = dot_nn(probs.astype(bf16), grads)
        at = 0
        for start, count in sources:
            if not isinstance(start, int):
                start = pl.multiple_of(start, BLOCK)
            acc_ref[pl.ds(start, count), lanes] += grad_keys[at : at + count]
            acc_ref[pl.ds(start, count), value_lanes] += grad_values[at : at + count]
            at += count

    @pl.when(chunk == pl.num_programs(0) - 1)
    def _():
        for level in range(LOCAL):
            at, count = offsets[level], level_rows(rows, level)
            to_left_ref[BLOCK * level : BLOCK * (level + 1), :] = acc_ref[at : at + BLOCK, :].astype(bf16)
            to_right_ref[BLOCK * level : BLOCK * (level + 1), :] = acc_ref[
                at + BLOCK + count : at + 2 * BLOCK + count, :
            ].astype(bf16)
        for level in range(LOCAL - 1, 0, -1):
            at, count = offsets[level] + BLOCK, level_rows(rows, level)
            below = offsets[level - 1] + BLOCK
            tile = min(count, 128)
            for row in range(0, count, tile):
                carry = spread(acc_ref[at + row : at + row + tile, :])
                target = slice(below + 2 * row, below + 2 * (row + tile))
                total = acc_ref[target, :] + carry
                if level == 1:
                    local_ref[2 * row : 2 * (row + tile), :] = total
                else:
                    acc_ref[target, :] = total
        carry = None
        for index in range(len(far) - 1, -1, -1):
            level = far[index]
            count = 8 * devices // 2 ** (level - LOCAL)
            tree_ref[0:count, :] = jnp.zeros((count, 2 * WIDTH), f32) if carry is None else spread(carry)
            block = here_ref[0] >> (level - 6)
            last = count // BLOCK - 1
            for side, neighbour in enumerate((block - 1, block + 1)):
                start = pl.multiple_of(jnp.clip(neighbour, 0, last) * BLOCK, BLOCK)
                at = offsets[LOCAL + index] + side * BLOCK
                tree_ref[pl.ds(start, BLOCK), :] += acc_ref[at : at + BLOCK, :]
            carry = tree_ref[0:count, :]
        to_far_ref[...] = carry


def attend_back_call(rows, devices, far, here, q, grads, bias, logs, levels, left, right, base):
    chunks = rows // CHUNK
    _, entries = extended_offsets(rows, far)
    _, slots = slot_layout(far)
    edge = (BLOCK * LOCAL, 2 * WIDTH)
    return pl.pallas_call(
        partial(attend_back_kernel, rows, devices, far),
        grid=(chunks,),
        out_shape=[
            jax.ShapeDtypeStruct((rows, WIDTH), bf16),
            jax.ShapeDtypeStruct((rows, 2 * WIDTH), f32),
            jax.ShapeDtypeStruct(edge, bf16),
            jax.ShapeDtypeStruct(edge, bf16),
            jax.ShapeDtypeStruct((8 * devices, 2 * WIDTH), f32),
        ],
        in_specs=[
            pl.BlockSpec(memory_space=pltpu.SMEM),
            pl.BlockSpec((CHUNK, WIDTH), lambda i: (i, 0)),
            pl.BlockSpec((CHUNK, WIDTH), lambda i: (i, 0)),
            pl.BlockSpec((1, slots, CHUNK), lambda i: (i, 0, 0)),
            pl.BlockSpec((1, 8, 2 * CHUNK), lambda i: (i, 0, 0)),
        ]
        + vmem_specs(LOCAL + 3),
        out_specs=[pl.BlockSpec((CHUNK, WIDTH), lambda i: (i, 0))] + vmem_specs(4),
        scratch_shapes=[
            pltpu.VMEM((entries, 2 * WIDTH), bf16),
            pltpu.VMEM((8 * devices, 2 * WIDTH), bf16),
            pltpu.VMEM((slots, 2 * WIDTH), bf16),
            pltpu.VMEM((entries, 2 * WIDTH), f32),
            pltpu.VMEM((8 * devices, 2 * WIDTH), f32),
        ],
        compiler_params=pltpu.CompilerParams(vmem_limit_bytes=VMEM_LIMIT),
        cost_estimate=pl.CostEstimate(flops=40 << 30, bytes_accessed=24 << 20, transcendentals=4 << 20),
        name="attend_back",
    )(here, q, grads, bias, logs, *levels, left, right, base)


def normal_parts(values):
    size = jnp.abs(values)
    bell = jnp.exp(-0.5 * values * values)
    t = 1.0 / (1.0 + (0.3275911 / math.sqrt(2.0)) * size)
    poly = t * (
        0.5 * 0.254829592
        + t * (0.5 * -0.284496736 + t * (0.5 * 1.421413741 + t * (0.5 * -1.453152027 + t * (0.5 * 1.061405429))))
    )
    tail = poly * bell
    return jnp.where(values < 0, tail, 1.0 - tail), bell * (1.0 / math.sqrt(2.0 * math.pi))


def feed_kernel(
    hidden_width,
    x_ref,
    attended_ref,
    cot_ref,
    out_w_ref,
    up_w_ref,
    down_w_ref,
    vec_ref,
    up_bias_ref,
    y_ref,
    grad_middle_ref,
    grad_attended_ref,
    weights_ref,
    vec_grad_ref,
    up_bias_grad_ref,
    down_acc,
    up_acc,
    out_acc,
):
    step = pl.program_id(0)

    @pl.when(step == 0)
    def _():
        down_acc[...] = jnp.zeros_like(down_acc)
        up_acc[...] = jnp.zeros_like(up_acc)
        out_acc[...] = jnp.zeros_like(out_acc)
        vec_grad_ref[...] = jnp.zeros_like(vec_grad_ref)
        up_bias_grad_ref[...] = jnp.zeros_like(up_bias_grad_ref)

    out_bias, gain, shift, down_bias = (vec_ref[at : at + 1, :] for at in range(4))
    attended = attended_ref[...]
    middle = x_ref[...].astype(f32) + dot_nn(attended, out_w_ref[...]) + out_bias
    scaled, inverse = norm_rows(middle)
    normed = (scaled * gain + shift).astype(bf16)
    cot = cot_ref[...]
    wide = cot.astype(f32)
    lowered = jnp.zeros_like(middle)
    grad_normed = jnp.zeros_like(middle)
    part = 512
    for at in range(0, hidden_width, part):
        columns = slice(at, at + part)
        pre = dot_nn(normed, up_w_ref[:, columns]) + up_bias_ref[:, columns]
        phi, bell = normal_parts(pre)
        hidden = (pre * phi).astype(bf16)
        lowered += dot_nn(hidden, down_w_ref[columns, :])
        grad_hidden = dot_nt(cot, down_w_ref[columns, :])
        grad_pre_wide = grad_hidden * (phi + pre * bell)
        grad_pre = grad_pre_wide.astype(bf16)
        up_bias_grad_ref[:, columns] += jnp.sum(grad_pre.astype(f32), axis=0, keepdims=True)
        grad_normed += dot_nt(grad_pre, up_w_ref[:, columns])
        down_acc[columns, :] += dot_tn(hidden, cot)
        up_acc[:, columns] += dot_tn(normed, grad_pre)
    y_ref[...] = (middle + lowered + down_bias).astype(bf16)
    grad_middle = wide + norm_back(grad_normed, scaled, inverse, gain)
    grad_middle_ref[...] = grad_middle
    grad_proj = grad_middle.astype(bf16)
    grad_attended_ref[...] = dot_nt(grad_proj, out_w_ref[...]).astype(bf16)
    out_acc[...] += dot_tn(attended, grad_proj)
    vec_grad_ref[0:1, :] += jnp.sum(grad_proj.astype(f32), axis=0, keepdims=True)
    vec_grad_ref[1:2, :] += jnp.sum(grad_normed * scaled, axis=0, keepdims=True)
    vec_grad_ref[2:3, :] += jnp.sum(grad_normed, axis=0, keepdims=True)
    vec_grad_ref[3:4, :] += jnp.sum(wide, axis=0, keepdims=True)

    @pl.when(step == pl.num_programs(0) - 1)
    def _():
        owners = weights_ref.shape[0]
        wide_rows, rows = hidden_width // owners, WIDTH // owners
        for owner in range(owners):
            weights_ref[owner, 0:wide_rows, :] = down_acc[owner * wide_rows : (owner + 1) * wide_rows, :].astype(bf16)
            for block in range(hidden_width // WIDTH):
                at = wide_rows + block * rows
                weights_ref[owner, at : at + rows, :] = up_acc[
                    owner * rows : (owner + 1) * rows, block * WIDTH : (block + 1) * WIDTH
                ].astype(bf16)
            at = 2 * wide_rows
            weights_ref[owner, at : at + rows, :] = out_acc[owner * rows : (owner + 1) * rows, :].astype(bf16)


def feed_call(owners, x, attended, cot, out_w, up_w, down_w, vectors, up_bias):
    rows, hidden_width = x.shape[0], up_w.shape[1]
    tile = 256
    row_spec = pl.BlockSpec((tile, WIDTH), lambda i: (i, 0))
    packed = 2 * (hidden_width // owners) + WIDTH // owners
    return pl.pallas_call(
        partial(feed_kernel, hidden_width),
        grid=(rows // tile,),
        out_shape=[
            jax.ShapeDtypeStruct((rows, WIDTH), bf16),
            jax.ShapeDtypeStruct((rows, WIDTH), f32),
            jax.ShapeDtypeStruct((rows, WIDTH), bf16),
            jax.ShapeDtypeStruct((owners, packed, WIDTH), bf16),
            jax.ShapeDtypeStruct((8, WIDTH), f32),
            jax.ShapeDtypeStruct((1, hidden_width), f32),
        ],
        in_specs=[row_spec, row_spec, row_spec] + vmem_specs(5),
        out_specs=[row_spec, row_spec, row_spec] + vmem_specs(3),
        scratch_shapes=[
            pltpu.VMEM((hidden_width, WIDTH), f32),
            pltpu.VMEM((WIDTH, hidden_width), f32),
            pltpu.VMEM((WIDTH, WIDTH), f32),
        ],
        compiler_params=pltpu.CompilerParams(vmem_limit_bytes=VMEM_LIMIT),
        cost_estimate=pl.CostEstimate(flops=15 << 30, bytes_accessed=20 << 20, transcendentals=4 << 20),
        name="feed_forward",
    )(x, attended, cot, out_w, up_w, down_w, vectors, up_bias)


def project_back_kernel(
    rows,
    x_ref,
    normed_ref,
    dq_ref,
    local_ref,
    grad_middle_ref,
    from_right_ref,
    from_left_ref,
    base_ref,
    w_ref,
    gain_ref,
    input_grad_ref,
    weights_ref,
    vec_grad_ref,
    tree_ref,
    acc_ref,
):
    carry = spread(base_ref[...])
    for level in range(LOCAL - 1, -1, -1):
        count = level_rows(rows, level)
        edge = slice(BLOCK * level, BLOCK * (level + 1))
        if level == LOCAL - 1:
            tree_ref[0:count, :] = carry
        tree_ref[0:BLOCK, :] += from_left_ref[edge, :].astype(f32)
        tree_ref[count - BLOCK : count, :] += from_right_ref[edge, :].astype(f32)
        if level:
            tile = min(count, 128)
            for row in range(count - tile, -1, -tile):
                tree_ref[2 * row : 2 * (row + tile), :] = spread(tree_ref[row : row + tile, :])
    acc_ref[...] = jnp.zeros_like(acc_ref)
    vec_grad_ref[...] = jnp.zeros_like(vec_grad_ref)
    tile = 256

    def body(at, _):
        span = pl.ds(pl.multiple_of(at * tile, tile), tile)
        scaled, inverse = norm_rows(x_ref[span, :].astype(f32))
        normed = normed_ref[span, :]
        dkv = (local_ref[span, :] + tree_ref[span, :]).astype(bf16)
        dq = dq_ref[span, :]
        acc_ref[:, :WIDTH] += dot_tn(normed, dq)
        acc_ref[:, WIDTH:] += dot_tn(normed, dkv)
        grad = dot_nt(dq, w_ref[:, :WIDTH]) + dot_nt(dkv, w_ref[:, WIDTH:])
        input_grad_ref[span, :] = grad_middle_ref[span, :] + norm_back(grad, scaled, inverse, gain_ref[...])
        vec_grad_ref[0:1, :] += jnp.sum(grad * scaled, axis=0, keepdims=True)
        vec_grad_ref[1:2, :] += jnp.sum(grad, axis=0, keepdims=True)
        vec_grad_ref[2:3, :] += jnp.sum(dq.astype(f32), axis=0, keepdims=True)
        vec_grad_ref[3:4, :] += jnp.sum(dkv[:, WIDTH:].astype(f32), axis=0, keepdims=True)
        return 0

    lax.fori_loop(0, rows // tile, body, 0)
    owners = weights_ref.shape[0]
    part = WIDTH // owners
    for owner in range(owners):
        for block in range(3):
            weights_ref[owner, block * part : (block + 1) * part, :] = acc_ref[
                owner * part : (owner + 1) * part, block * WIDTH : (block + 1) * WIDTH
            ].astype(bf16)


def project_back_call(owners, x, normed, dq, local, grad_middle, from_right, from_left, base, weight, gain):
    rows = x.shape[0]
    return pl.pallas_call(
        partial(project_back_kernel, rows),
        out_shape=[
            jax.ShapeDtypeStruct((rows, WIDTH), f32),
            jax.ShapeDtypeStruct((owners, 3 * WIDTH // owners, WIDTH), bf16),
            jax.ShapeDtypeStruct((8, WIDTH), f32),
        ],
        in_specs=vmem_specs(10),
        out_specs=vmem_specs(3),
        scratch_shapes=[pltpu.VMEM((rows, 2 * WIDTH), f32), pltpu.VMEM((WIDTH, 3 * WIDTH), f32)],
        compiler_params=pltpu.CompilerParams(vmem_limit_bytes=VMEM_LIMIT),
        cost_estimate=pl.CostEstimate(flops=4 << 30, bytes_accessed=20 << 20, transcendentals=0),
        name="project_back",
    )(x, normed, dq, local, grad_middle, from_right, from_left, base, weight, gain)


def shifted(block, axis, distance):
    devices = range(lax.axis_size(axis))
    route = [(i - distance, i) for i in devices if i - distance in devices]
    return lax.ppermute(block, axis, route)


def swap(block, axis, bit):
    return lax.ppermute(block, axis, [(i, i ^ bit) for i in range(lax.axis_size(axis))])


def add_low(left, right):
    return (left.astype(f32) + right.astype(f32)).astype(bf16)


def scatter_step(parts, axis, bit):
    mine = (lax.axis_index(axis) // bit) % 2
    keep = lax.dynamic_index_in_dim(parts, mine, 0, keepdims=False)
    send = lax.dynamic_index_in_dim(parts, 1 - mine, 0, keepdims=False)
    return add_low(keep, swap(send, axis, bit))


def gather_step(part, axis, bit):
    mine = (lax.axis_index(axis) // bit) % 2
    other = swap(part, axis, bit)
    first = jnp.where(mine == 0, part, other)
    second = jnp.where(mine == 0, other, part)
    return jnp.concatenate([first, second], axis=0)


def gather_ctx(block, axis):
    bit = 1
    while bit < lax.axis_size(axis):
        block = gather_step(block, axis, bit)
        bit *= 2
    return block


def scatter_ctx(block, axis):
    bit = lax.axis_size(axis) // 2
    while bit >= 1:
        block = scatter_step(block.reshape(2, block.shape[0] // 2, *block.shape[1:]), axis, bit)
        bit //= 2
    return block


def reduce_weights(parts):
    owners = parts.shape[0]
    shape = parts.shape[1:]
    current = parts.reshape(owners // 2, 2, *shape).transpose(1, 0, 2, 3)
    current = scatter_step(current, "fsdp", 1)
    bit = 2
    while bit < owners:
        current = current.reshape(-1, 2, *shape).transpose(1, 0, 2, 3)
        current = scatter_step(current, "fsdp", bit)
        bit *= 2
    current = current.reshape(shape)
    bit = 1
    bits = []
    while bit < lax.axis_size("ctx"):
        current = scatter_step(current.reshape(2, current.shape[0] // 2, shape[1]), "ctx", bit)
        bits.append(bit)
        bit *= 2
    for bit in reversed(bits):
        current = gather_step(current, "ctx", bit)
    return current.astype(f32)


def shards(
    layer_input,
    doc_lengths,
    ln1_gain,
    ln1_bias,
    qkv_weight,
    query_bias,
    value_bias,
    out_weight,
    out_bias,
    ln2_gain,
    ln2_bias,
    up_weight,
    up_bias,
    down_weight,
    down_bias,
    cotangent,
):
    owners = lax.axis_size("fsdp")
    devices = lax.axis_size("ctx")
    x, cot = layer_input[0], cotangent[0]
    rows = x.shape[0]
    total = rows * devices
    far = far_levels(total)
    here = lax.axis_index("ctx")
    part = WIDTH // owners

    small = jnp.concatenate(
        [ln1_gain, ln1_bias, query_bias, value_bias, out_bias, ln2_gain, ln2_bias, down_bias, up_bias]
    )
    gathered = lax.all_gather(small, "fsdp", axis=0, tiled=False)
    vectors = [gathered[:, at * part : (at + 1) * part].reshape(1, WIDTH).astype(f32) for at in range(8)]
    up_shift = gathered[:, 8 * part :].reshape(1, -1).astype(f32)
    gain_first, shift_first, query_shift, value_shift = vectors[:4]
    feed_vectors = jnp.concatenate(vectors[4:] + [jnp.zeros((4, WIDTH), f32)], axis=0)
    qkv_shift = jnp.concatenate([query_shift, jnp.zeros_like(query_shift), value_shift], axis=1)

    qkv_full = lax.all_gather(qkv_weight, "fsdp", axis=0, tiled=True)
    out_full = lax.all_gather(out_weight, "fsdp", axis=0, tiled=True)
    up_full = lax.all_gather(up_weight, "fsdp", axis=0, tiled=True)
    down_full = lax.all_gather(down_weight, "fsdp", axis=0, tiled=True)

    starts = jnp.cumsum(doc_lengths[0]) - doc_lengths[0]
    bias = score_bias(rows, total, here * rows, starts, far)

    normed, queries, *levels = qkv_call(rows, x, qkv_full, qkv_shift, gain_first, shift_first)
    levels, tail, head = levels[:LOCAL], levels[LOCAL], levels[LOCAL + 1]
    left = shifted(tail, "ctx", 1)
    right = shifted(head, "ctx", -1)
    base = gather_ctx(levels[LOCAL - 1], "ctx")

    here_array = here.reshape(1).astype(jnp.int32)
    attended, logs = attend_call(rows, devices, far, here_array, queries, bias, levels, left, right, base)
    output, grad_middle, grad_attended, feed_grads, vec_grads, up_bias_grad = feed_call(
        owners, x, attended, cot, out_full, up_full, down_full, feed_vectors, up_shift
    )
    extra = jnp.zeros((owners, 32, WIDTH), bf16)
    extra = extra.at[:, 0, :].set(vec_grads[:4].reshape(4, owners, part).transpose(1, 0, 2).reshape(owners, -1).astype(bf16))
    extra = extra.at[:, 1, :].set(up_bias_grad.reshape(owners, -1).astype(bf16))
    feed_sum = reduce_weights(jnp.concatenate([feed_grads, extra], axis=1))

    dq, local, to_left, to_right, to_far = attend_back_call(
        rows, devices, far, here_array, queries, grad_attended, bias, logs, levels, left, right, base
    )
    back_right = shifted(to_left, "ctx", -1)
    back_left = shifted(to_right, "ctx", 1)
    back_far = scatter_ctx(to_far, "ctx").astype(f32)
    input_grad, qkv_grads, first_grads = project_back_call(
        owners, x, normed, dq, local, grad_middle, back_right, back_left, back_far, qkv_full, gain_first
    )
    extra = jnp.zeros((owners, 32, WIDTH), bf16)
    extra = extra.at[:, 0, :].set(first_grads[:4].reshape(4, owners, part).transpose(1, 0, 2).reshape(owners, -1).astype(bf16))
    qkv_sum = reduce_weights(jnp.concatenate([qkv_grads, extra], axis=1))

    wide = up_weight.shape[1]
    wide_rows = wide // owners
    down_grad = feed_sum[:wide_rows]
    up_grad = jnp.concatenate(
        [feed_sum[wide_rows + at * part : wide_rows + (at + 1) * part] for at in range(wide // WIDTH)], axis=1
    )
    out_grad = feed_sum[2 * wide_rows : 2 * wide_rows + part]
    feed_row = feed_sum[2 * wide_rows + part]
    up_row = feed_sum[2 * wide_rows + part + 1]
    qkv_grad = jnp.concatenate([qkv_sum[at * part : (at + 1) * part] for at in range(3)], axis=1)
    first_row = qkv_sum[3 * part]
    pick = lambda row, at: row[at * part : (at + 1) * part]
    return (
        output[None],
        input_grad[None],
        pick(first_row, 0),
        pick(first_row, 1),
        qkv_grad,
        pick(first_row, 2),
        pick(first_row, 3),
        out_grad,
        pick(feed_row, 0),
        pick(feed_row, 1),
        pick(feed_row, 2),
        up_grad,
        up_row,
        down_grad,
        pick(feed_row, 3),
    )


def solution(mesh):
    row, vector = P("fsdp", None), P("fsdp")
    tokens = P("fsdp", "ctx", None)
    return jax.shard_map(
        shards,
        mesh=mesh,
        in_specs=(
            tokens,
            row,
            vector,
            vector,
            row,
            vector,
            vector,
            row,
            vector,
            vector,
            vector,
            row,
            vector,
            row,
            vector,
            tokens,
        ),
        out_specs=(
            tokens,
            tokens,
            vector,
            vector,
            row,
            vector,
            vector,
            row,
            vector,
            vector,
            vector,
            row,
            vector,
            row,
            vector,
        ),
        check_vma=False,
    )
```

time: 1200 us -> 345 us (0.29); the launches traced: 1180 us -> 344 us
  matrix products: 304 us -> 0 us
  other arithmetic: 341 us -> 37.7 us
  local copies, waits for them, and re-layouts: 184 us -> 21.7 us
  waiting for transfers between devices: 239 us -> 103 us
  Pallas kernels: 0 us -> 106 us
  blocking collectives: 88.1 us -> 13.9 us
  starting transfers between devices: 11.6 us -> 47.1 us
    dot_general x40 -> x0, matrix products: 304 us -> none  [the longest x8 96.7 us: group_scores(): jnp.einsum('cse,jse->scj', query_group.reshape(query_group.shape[0], 2, h...]
    and x1 -> x0, other arithmetic: 206 us -> none  [allowed(): return level_ok & (key_doc[None, :] == query_doc[:, None])]
    reduce_scatter x5 -> x0, waiting for transfers between devices: 161 us -> none  [the longest x1 47 us: shards(): lax.psum_scatter(grads[9], 'fsdp', scatter_dimension=0, tiled=True)]
    pallas_call x0 -> x5, Pallas kernels: none -> 106 us  [the longest x1 31.2 us: feed_call(): pl.pallas_call(partial(feed_kernel, hidden_width), grid=(rows // tile,),...]
    ppermute x0 -> x22, waiting for transfers between devices: none -> 88.4 us  [swap(): lax.ppermute(block, axis, [(i, i ^ bit) for i in range(lax.axis_size(axis...]
    psum x1 -> x0, waiting for transfers between devices: 64.2 us -> none  [shards(): lax.psum((owned[0], owned[1], owned[2], owned[3], owned[4], owned[5], own...]
    convert_element_type x19 -> x16, other arithmetic: 63.4 us -> 10.1 us  [the longest x11 7.78 us: add_low(): return (left.astype(f32) + right.astype(f32)).astype(bf16)]
    reshape x17 -> x2, local copies, waits for them, and re-layouts: 46.4 us -> 0.09 us  [reduce_weights(): current.reshape(2, current.shape[0] // 2, shape[1])]
  transfers between devices with their start and end apart: 14 -> 29, of which waited for: 7 -> 19; matrix products, arithmetic and copies ran while one was open for 40% -> 13% of each run, Pallas kernels for 0% -> 22%
where the time goes in v1:
time: 345 us; the launch traced here: 344 us
  Pallas kernels  106 us (31%)
  waiting for transfers between devices  103 us (30%)
  starting transfers between devices  47.1 us (14%)
  other arithmetic  37.7 us (11%)
  local copies, waits for them, and re-layouts  21.7 us (6%)
  between operations  14.4 us (4%)
  blocking collectives  13.9 us (4%)
    ppermute x22, waiting for transfers between devices, swap(): lax.ppermute(block, axis, [(i, i ^ bit) for i in range(lax.axis_size(axis...  88.4 us
    ppermute x22, starting transfers between devices, swap(): lax.ppermute(block, axis, [(i, i ^ bit) for i in range(lax.axis_size(axis...  37 us
    pallas_call x1, Pallas kernels, feed_call(): pl.pallas_call(partial(feed_kernel, hidden_width), grid=(rows // tile,),...  31.2 us
    pallas_call x1, Pallas kernels, attend_back_call(): pl.pallas_call(partial(attend_back_kernel, rows, devices, far), grid=(chu...  30.3 us
    pallas_call x1, Pallas kernels, attend_call(): pl.pallas_call(partial(attend_kernel, rows, devices, far), grid=(chunks,)...  20.9 us
    pallas_call x1, Pallas kernels, project_back_call(): pl.pallas_call(partial(project_back_kernel, rows), out_shape=[jax.ShapeDt...  13.8 us
    ppermute x4, waiting for transfers between devices, shifted(): return lax.ppermute(block, axis, route)  12.8 us
    unnamed x41, local copies, waits for them, and re-layouts  12.8 us
  transfers between devices with their start and end apart: 29, of which 19 were waited for; matrix products, arithmetic and copies ran while one was open for 13% of the time, Pallas kernels for 22%

profile of v1, /device:TPU:0, one launch (start us, length us, event | category | flops | bytes accessed | tf_op | source)
XLA Modules:
  0.0 343.9 jit_solution(2592759506919567426)
XLA Ops:
  17.0 6.2 %all-gather.1 = bf16[4,1,1536]{2,1,0:T(2,128)(2,1)S(1)} all-gather(bf16[1,1,1536]{2,1,0:T(2,128)(2,1)S(1)} %reshape.2718), channel_id=2, replica_groups=mesh['ctx'=8,'fsdp'=4] {'fsdp'}, dimensions={0}, use_global_device_ids=true | all-gather | bytes 15360 | tf_op jit(solution)/shard_map/all_gather | solution.py:722
  27.2 5.3 %iota_add_fusion = (s32[8,128]{1,0:T(8,128)S(1)}, s32[8,128]{1,0:T(8,128)S(1)}) fusion(s32[8]{0:T(128)S(1)} %multiply_add_fusion, s32[]{:T(128)} %bitcast.16, s32[]{:T(128)} %bitcast.15, s32[]{:T(128)} %bitcast.14, s32[]{:T(128)} %bitcast.13, s32[]{:T(128)} %bitcast.12, s32[]{:T(128)} %bitcast.11, s32[]{:T(128)} %bitcast.10, s32[]{:T(128)} %bitcast.9), kind=kLoop, calls=%fused_computation.100 | loop fusion | flops 25600 | bytes 8256 | tf_op jit(solution)/shard_map/add | solution.py:101
  32.5 5.9 %broadcast_shift-right-arithmetic_fusion.1 = (s32[8,528]{1,0:T(8,128)S(1)}, s32[8,528]{1,0:T(8,128)S(1)}, s32[8,528]{1,0:T(8,128)S(1)}) fusion(s32[8,528]{1,0:T(8,128)S(1)} %concatenate.101, s32[528]{0:T(1024)} %constant.441, s32[528]{0:T(1024)} %constant.431.clone, s32[]{:T(128)} %bitcast.16, s32[]{:T(128)} %bitcast.15, s32[]{:T(128)} %bitcast.14, ...), kind=kLoop, calls=%fused_computation.88 | loop fusion | flops 244992 | bytes 73952 | tf_op jit(solution)/shard_map/shift_right_arithmetic | solution.py:111
  38.5 9.4 %qkv_levels.1 = (bf16[1024,512]{1,0:T(8,128)(2,1)}, bf16[1024,512]{1,0:T(8,128)(2,1)}, bf16[1024,1024]{1,0:T(8,128)(2,1)}, bf16[512,1024]{1,0:T(8,128)(2,1)}, bf...) custom-call(bf16[1024,512]{1,0:T(8,128)(2,1)} %bitcast.156, ...), custom_call_target="tpu_custom_call" | custom-call | flops 1610612736 | bytes 10485760 | tf_op jit(solution)/shard_map/qkv_levels/pallas_call | solution.py:220
  50.0 3.9 %fusion.7.bias_ref = f32[8,528,128]{2,1,0:T(8,128)} fusion(f32[528]{0:T(1024)S(1)} %copy-done.7, s32[8,128]{1,0:T(8,128)S(1)} %get-tuple-element.150, s32[8,528]{1,0:T(8,128)S(1)} %get-tuple-element.139, s32[528]{0:T(1024)S(1)} %copy-done.6, s32[8,528]{1,0:T(8,128)S(1)} %get-tuple-element.140, s32[528]{0:T(1024)S(1)} %copy-done.5, ...), kind=kLoop, calls=%fused_computation.14 | loop fusion | flops 7569408 | bytes 2228432 | tf_op jit(solution)/shard_map/jit(_where)/select_n | solution.py:115
  61.0 7.7 %all_gather.21.out_w_ref = bf16[512,512]{1,0:T(8,128)(2,1)} all-gather(bf16[128,512]{1,0:T(8,128)(2,1)S(1)} %copy-done.3), channel_id=1, replica_groups=mesh['ctx'=8,'fsdp'=4] {'fsdp'}, dimensions={0}, use_global_device_ids=true | all-gather | bytes 655360 | tf_op jit(solution)/shard_map/all_gather | solution.py:730
  76.5 4.9 %collective-permute-done.1.refs_8_ = bf16[112,1024]{1,0:T(8,128)(2,1)S(1)} collective-permute-done((bf16[112,1024]{1,0:T(8,128)(2,1)S(1)}, bf16[112,1024]{1,0:T(8,128)(2,1)S(1)}, u32[]{:S(2)}, u32[]{:S(2)}) %collective-permute-start.1) | collective-permute-done | bytes 229408 | tf_op jit(solution)/shard_map/ppermute | solution.py:628
  82.1 20.9 %attend.1 = (bf16[1024,512]{1,0:T(8,128)(2,1)}, f32[8,8,256]{2,1,0:T(8,128)}) custom-call(s32[1]{0:T(128)} %bitcast.1.here_ref, bf16[1024,512]{1,0:T(8,128)(2,1)} %get-tuple-element.78.q_ref, f32[8,528,128]{2,1,0:T(8,128)} %fusion.7.bias_ref, bf16[1024,1024]{1,0:T(8,128)(2,1)} %get-tuple-element.79.refs_0_, bf16[512,1024]{1,0:T(8,128)(2,1)} %get-tuple-element.80.refs_1_, ...), custom_call_target="tpu_custom_call" | custom-call | flops 17179869184 | bytes 12582912 | tf_op jit(solution)/shard_map/attend/pallas_call | solution.py:290
  103.1 31.2 %feed_forward.1 = (bf16[1024,512]{1,0:T(8,128)(2,1)}, f32[1024,512]{1,0:T(8,128)}, bf16[1024,512]{1,0:T(8,128)(2,1)}, bf16[4,1152,512]{2,1,0:T(8,128)(2,1)}, f32[8,512]{1,0:T(8,128)}, /*index=5*/f32[1,2048]{1,0:T(1,128)}) custom-call(bf16[1024,512]{1,0:T(8,128)(2,1)} %bitcast.157, bf16[1024,512]{1,0:T(8,128)(2,1)} %get-tuple-element.88.attended_ref, ...), custom_call_target="tpu_custom_call" | custom-call | flops 16106127360 | bytes 20971520 | tf_op jit(solution)/shard_map/feed_forward/pallas_call | solution.py:523
  141.0 30.3 %attend_back.1 = (bf16[1024,512]{1,0:T(8,128)(2,1)}, f32[1024,1024]{1,0:T(8,128)}, bf16[112,1024]{1,0:T(8,128)(2,1)}, bf16[112,1024]{1,0:T(8,128)(2,1)}, f32[64,1024]{1,0:T(8,128)}) custom-call(s32[1]{0:T(128)} %bitcast.1.here_ref, bf16[1024,512]{1,0:T(8,128)(2,1)} %get-tuple-element.78.q_ref, bf16[1024,512]{1,0:T(8,128)(2,1)} %get-tuple-element.91.grad_ref, ...), custom_call_target="tpu_custom_call" | custom-call | flops 42949672960 | bytes 25165824 | tf_op jit(solution)/shard_map/attend_back/pallas_call | solution.py:395
  175.6 4.1 %collective-permute-done.7 = f32[32,1024]{1,0:T(8,128)S(1)} collective-permute-done((f32[32,1024]{1,0:T(8,128)S(1)}, f32[32,1024]{1,0:T(8,128)S(1)}, u32[]{:S(2)}, u32[]{:S(2)}) %collective-permute-start.7) | collective-permute-done | bytes 131104 | tf_op jit(solution)/shard_map/ppermute | solution.py:632
  180.7 3.9 %collective-permute-start.8 = (bf16[16,1024]{1,0:T(8,128)(2,1)S(1)}, bf16[16,1024]{1,0:T(8,128)(2,1)S(1)}, u32[]{:S(2)}, u32[]{:S(2)}) collective-permute-start(bf16[16,1024]{1,0:T(8,128)(2,1)S(1)} %dynamic-slice_bitcast_fusion.9), channel_id=1, source_target_pairs={{0,8},{4,12},{8,0},{12,4},{16,24},{20,28},{24,16},{28,20},{1,9},{5... | collective-permute-start | bytes 98312 | tf_op jit(solution)/shard_map/ppermute | solution.py:632
  190.9 4.8 %collective-permute-start.6 = (bf16[112,1024]{1,0:T(8,128)(2,1)}, bf16[112,1024]{1,0:T(8,128)(2,1)S(1)}, u32[]{:S(2)}, u32[]{:S(2)}) collective-permute-start(bf16[112,1024]{1,0:T(8,128)(2,1)} %get-tuple-element.97), channel_id=1, source_target_pairs={{0,4},{4,8},{8,12},{12,16},{16,20},{20,24},{24,28},{1,5},{5,9},{9,... | collective-permute-start | bytes 688136 | tf_op jit(solution)/shard_map/ppermute | solution.py:628
  197.7 3.5 %collective-permute-done.6.from_left_ref = bf16[112,1024]{1,0:T(8,128)(2,1)S(1)} collective-permute-done((bf16[112,1024]{1,0:T(8,128)(2,1)}, bf16[112,1024]{1,0:T(8,128)(2,1)S(1)}, u32[]{:S(2)}, u32[]{:S(2)}) %collective-permute-start.6) | collective-permute-done | bytes 229408 | tf_op jit(solution)/shard_map/ppermute | solution.py:628
  201.9 13.8 %project_back.1 = (f32[1024,512]{1,0:T(8,128)}, bf16[4,384,512]{2,1,0:T(8,128)(2,1)}, f32[8,512]{1,0:T(8,128)}) custom-call(bf16[1024,512]{1,0:T(8,128)(2,1)} %bitcast.158, bf16[1024,512]{1,0:T(8,128)(2,1)} %get-tuple-element.90.normed_ref, bf16[1024,512]{1,0:T(8,128)(2,1)} %get-tuple-element.93.dq_ref, f32[1024,1024]{1,0:T(8,128)} %get-tuple-element.94.local_ref, ...), custom_call_target="tpu_custom_call" | custom-call | flops 4294967296 | bytes 20971520 | tf_op jit(solution)/shard_map/project_back/pallas_call | solution.py:609
  225.9 34.5 %collective-permute-done.11 = bf16[1,416,512]{2,1,0:T(8,128)(2,1)} collective-permute-done((bf16[1,416,512]{2,1,0:T(8,128)(2,1)}, bf16[1,416,512]{2,1,0:T(8,128)(2,1)}, u32[]{:S(2)}, u32[]{:S(2)}) %collective-permute-start.11) | collective-permute-done | bytes 426016 | tf_op jit(solution)/shard_map/ppermute | solution.py:632
  274.1 6.9 %collective-permute-done.20 = bf16[592,512]{1,0:T(8,128)(2,1)S(1)} collective-permute-done((bf16[592,512]{1,0:T(8,128)(2,1)S(1)}, bf16[592,512]{1,0:T(8,128)(2,1)S(1)}, u32[]{:S(2)}, u32[]{:S(2)}) %collective-permute-start.20) | collective-permute-done | bytes 606240 | tf_op jit(solution)/shard_map/ppermute | solution.py:632
  285.9 4.0 %collective-permute-done.14 = bf16[52,512]{1,0:T(8,128)(2,1)S(1)} collective-permute-done((bf16[52,512]{1,0:T(8,128)(2,1)S(1)}, bf16[52,512]{1,0:T(8,128)(2,1)S(1)}, u32[]{:S(2)}, u32[]{:S(2)}) %collective-permute-start.14) | collective-permute-done | bytes 53280 | tf_op jit(solution)/shard_map/ppermute | solution.py:632
  289.9 3.4 %collective-permute-start.15 = (bf16[52,512]{1,0:T(8,128)(2,1)S(1)}, bf16[52,512]{1,0:T(8,128)(2,1)S(1)}, u32[]{:S(2)}, u32[]{:S(2)}) collective-permute-start(bf16[52,512]{1,0:T(8,128)(2,1)S(1)} %fusion.16), channel_id=1, source_target_pairs={{0,16},{4,20},{8,24},{12,28},{16,0},{20,4},{24,8},{28,12},{1,17},{... | collective-permute-start | bytes 159752 | tf_op jit(solution)/shard_map/ppermute | solution.py:632
  294.0 4.2 %collective-permute-done.15 = bf16[52,512]{1,0:T(8,128)(2,1)S(1)} collective-permute-done((bf16[52,512]{1,0:T(8,128)(2,1)S(1)}, bf16[52,512]{1,0:T(8,128)(2,1)S(1)}, u32[]{:S(2)}, u32[]{:S(2)}) %collective-permute-start.15) | collective-permute-done | bytes 53280 | tf_op jit(solution)/shard_map/ppermute | solution.py:632
  305.8 4.0 %collective-permute-done.23 = bf16[148,512]{1,0:T(8,128)(2,1)S(1)} collective-permute-done((bf16[148,512]{1,0:T(8,128)(2,1)S(1)}, bf16[148,512]{1,0:T(8,128)(2,1)S(1)}, u32[]{:S(2)}, u32[]{:S(2)}) %collective-permute-start.23) | collective-permute-done | bytes 151584 | tf_op jit(solution)/shard_map/ppermute | solution.py:632
  311.0 5.7 %collective-permute-done.24 = bf16[296,512]{1,0:T(8,128)(2,1)S(1)} collective-permute-done((bf16[296,512]{1,0:T(8,128)(2,1)S(1)}, bf16[296,512]{1,0:T(8,128)(2,1)S(1)}, u32[]{:S(2)}, u32[]{:S(2)}) %collective-permute-start.24) | collective-permute-done | bytes 303136 | tf_op jit(solution)/shard_map/ppermute | solution.py:632
  316.9 3.8 %collective-permute-start.25 = (bf16[592,512]{1,0:T(8,128)(2,1)S(1)}, bf16[592,512]{1,0:T(8,128)(2,1)S(1)}, u32[]{:S(2)}, u32[]{:S(2)}) collective-permute-start(bf16[592,512]{1,0:T(8,128)(2,1)S(1)} %pad_maximum_fusion.3), channel_id=1, source_target_pairs={{0,4},{4,0},{8,12},{12,8},{16,20},{20,16},{24,28},{28,24},{1,5},{5... | collective-permute-start | bytes 1818632 | tf_op jit(solution)/shard_map/ppermute | solution.py:632
  322.2 10.5 %collective-permute-done.25 = bf16[592,512]{1,0:T(8,128)(2,1)S(1)} collective-permute-done((bf16[592,512]{1,0:T(8,128)(2,1)S(1)}, bf16[592,512]{1,0:T(8,128)(2,1)S(1)}, u32[]{:S(2)}, u32[]{:S(2)}) %collective-permute-start.25) | collective-permute-done | bytes 606240 | tf_op jit(solution)/shard_map/ppermute | solution.py:632
  (189 shorter events, 96.4 us)
Async XLA Ops:
  7.2 31.3 %all-gather.6.cloned.1.call-start = ((), (), s32[]{:S(2)}) async-start(), calls=%async_computation | async-start | bytes 1966080 | tf_op jit(solution)/shard_map/all_gather | solution.py:729
  7.9 95.2 %all-gather.10.cloned.1.call-start = ((), (), s32[]{:S(2)}) async-start(), calls=%async_computation.2 | async-start | bytes 2621440 | tf_op jit(solution)/shard_map/all_gather | solution.py:732
  8.7 94.4 %all-gather.8.cloned.1.call-start = ((), (), s32[]{:S(2)}) async-start(), calls=%async_computation.1 | async-start | bytes 2621440 | tf_op jit(solution)/shard_map/all_gather | solution.py:731
  48.0 5.9 %collective-permute-start.2 = (bf16[16,1024]{1,0:T(8,128)(2,1)}, bf16[16,1024]{1,0:T(8,128)(2,1)S(1)}, u32[]{:S(2)}, u32[]{:S(2)}) collective-permute-start(bf16[16,1024]{1,0:T(8,128)(2,1)} %get-tuple-element.85.refs_6_), channel_id=1, source_target_pairs={{0,4},{4,0},{8,12},{12,8},{16,20},{20,16},{24,28},{28,24},{1,5},{5... | collective-permute-start | bytes 98312 | tf_op jit(solution)/shard_map/ppermute | solution.py:632
  58.3 14.3 %collective-permute-start.4 = (bf16[64,1024]{1,0:T(8,128)(2,1)S(1)}, bf16[64,1024]{1,0:T(8,128)(2,1)S(1)}, u32[]{:S(2)}, u32[]{:S(2)}) collective-permute-start(bf16[64,1024]{1,0:T(8,128)(2,1)S(1)} %pad_maximum_fusion.7), channel_id=1, source_target_pairs={{0,16},{4,20},{8,24},{12,28},{16,0},{20,4},{24,8},{28,12},{1,17},{... | collective-permute-start | bytes 393224 | tf_op jit(solution)/shard_map/ppermute | solution.py:632
  68.7 7.8 %collective-permute-start = (bf16[112,1024]{1,0:T(8,128)(2,1)S(1)}, bf16[112,1024]{1,0:T(8,128)(2,1)S(1)}, u32[]{:S(2)}, u32[]{:S(2)}) collective-permute-start(bf16[112,1024]{1,0:T(8,128)(2,1)S(1)} %copy-done.10), channel_id=1, source_target_pairs={{0,4},{4,8},{8,12},{12,16},{16,20},{20,24},{24,28},{1,5},{5,9},{9,... | collective-permute-start | bytes 688136 | tf_op jit(solution)/shard_map/ppermute | solution.py:628
  71.1 10.3 %collective-permute-start.1 = (bf16[112,1024]{1,0:T(8,128)(2,1)S(1)}, bf16[112,1024]{1,0:T(8,128)(2,1)S(1)}, u32[]{:S(2)}, u32[]{:S(2)}) collective-permute-start(bf16[112,1024]{1,0:T(8,128)(2,1)S(1)} %copy-done.9), channel_id=1, source_target_pairs={{4,0},{8,4},{12,8},{16,12},{20,16},{24,20},{28,24},{5,1},{9,5},{13... | collective-permute-start | bytes 688136 | tf_op jit(solution)/shard_map/ppermute | solution.py:628
  141.0 77.3 %collective-permute-start.18 = (bf16[2,1184,512]{2,1,0:T(8,128)(2,1)S(1)}, bf16[2,1184,512]{2,1,0:T(8,128)(2,1)}, u32[]{:S(2)}, u32[]{:S(2)}) collective-permute-start(bf16[2,1184,512]{2,1,0:T(8,128)(2,1)S(1)} %dynamic-slice_bitcast_fusion), channel_id=1, source_target_pairs={{0,1},{1,0},{2,3},{3,2},{4,5},{5,4},{6,7},{7,6},{8,9},{9,8},{10,11... | collective-permute-start | bytes 7274504 | tf_op jit(solution)/shard_map/ppermute | solution.py:632
  172.3 7.5 %collective-permute-start.7 = (f32[32,1024]{1,0:T(8,128)S(1)}, f32[32,1024]{1,0:T(8,128)S(1)}, u32[]{:S(2)}, u32[]{:S(2)}) collective-permute-start(f32[32,1024]{1,0:T(8,128)S(1)} %dynamic-slice_bitcast_fusion.6), channel_id=1, source_target_pairs={{0,16},{4,20},{8,24},{12,28},{16,0},{20,4},{24,8},{28,12},{1,17},{... | collective-permute-start | bytes 393224 | tf_op jit(solution)/shard_map/ppermute | solution.py:632
  186.5 9.3 %collective-permute-start.9 = (bf16[8,1024]{1,0:T(8,128)(2,1)S(1)}, bf16[8,1024]{1,0:T(8,128)(2,1)S(1)}, u32[]{:S(2)}, u32[]{:S(2)}) collective-permute-start(bf16[8,1024]{1,0:T(8,128)(2,1)S(1)} %dynamic-slice_bitcast_fusion.10), channel_id=1, source_target_pairs={{0,4},{4,0},{8,12},{12,8},{16,20},{20,16},{24,28},{28,24},{1,5},{5... | collective-permute-start | bytes 49160 | tf_op jit(solution)/shard_map/ppermute | solution.py:632
  189.6 8.1 %collective-permute-start.5 = (bf16[112,1024]{1,0:T(8,128)(2,1)}, bf16[112,1024]{1,0:T(8,128)(2,1)S(1)}, u32[]{:S(2)}, u32[]{:S(2)}) collective-permute-start(bf16[112,1024]{1,0:T(8,128)(2,1)} %get-tuple-element.96), channel_id=1, source_target_pairs={{4,0},{8,4},{12,8},{16,12},{20,16},{24,20},{28,24},{5,1},{9,5},{13... | collective-permute-start | bytes 688136 | tf_op jit(solution)/shard_map/ppermute | solution.py:628
  190.9 10.4 %collective-permute-start.6 = (bf16[112,1024]{1,0:T(8,128)(2,1)}, bf16[112,1024]{1,0:T(8,128)(2,1)S(1)}, u32[]{:S(2)}, u32[]{:S(2)}) collective-permute-start(bf16[112,1024]{1,0:T(8,128)(2,1)} %get-tuple-element.97), channel_id=1, source_target_pairs={{0,4},{4,8},{8,12},{12,16},{16,20},{20,24},{24,28},{1,5},{5,9},{9,... | collective-permute-start | bytes 688136 | tf_op jit(solution)/shard_map/ppermute | solution.py:628
  222.8 41.2 %collective-permute-start.19 = (bf16[1,1184,512]{2,1,0:T(8,128)(2,1)}, bf16[1,1184,512]{2,1,0:T(8,128)(2,1)}, u32[]{:S(2)}, u32[]{:S(2)}) collective-permute-start(bf16[1,1184,512]{2,1,0:T(8,128)(2,1)} %constant_dynamic-slice_fusion), channel_id=1, source_target_pairs={{0,2},{1,3},{2,0},{3,1},{4,6},{5,7},{6,4},{7,5},{8,10},{9,11},{10,... | collective-permute-start | bytes 3637256 | tf_op jit(solution)/shard_map/ppermute | solution.py:632
  224.7 35.7 %collective-permute-start.11 = (bf16[1,416,512]{2,1,0:T(8,128)(2,1)}, bf16[1,416,512]{2,1,0:T(8,128)(2,1)}, u32[]{:S(2)}, u32[]{:S(2)}) collective-permute-start(bf16[1,416,512]{2,1,0:T(8,128)(2,1)} %constant_dynamic-slice_fusion.1), channel_id=1, source_target_pairs={{0,2},{1,3},{2,0},{3,1},{4,6},{5,7},{6,4},{7,5},{8,10},{9,11},{10,... | collective-permute-start | bytes 1277960 | tf_op jit(solution)/shard_map/ppermute | solution.py:632
  261.5 7.7 %collective-permute-start.12 = (bf16[208,512]{1,0:T(8,128)(2,1)S(1)}, bf16[208,512]{1,0:T(8,128)(2,1)S(1)}, u32[]{:S(2)}, u32[]{:S(2)}) collective-permute-start(bf16[208,512]{1,0:T(8,128)(2,1)S(1)} %dynamic-slice_bitcast_fusion.4), channel_id=1, source_target_pairs={{0,4},{4,0},{8,12},{12,8},{16,20},{20,16},{24,28},{28,24},{1,5},{5... | collective-permute-start | bytes 638984 | tf_op jit(solution)/shard_map/ppermute | solution.py:632
  266.7 14.3 %collective-permute-start.20 = (bf16[592,512]{1,0:T(8,128)(2,1)S(1)}, bf16[592,512]{1,0:T(8,128)(2,1)S(1)}, u32[]{:S(2)}, u32[]{:S(2)}) collective-permute-start(bf16[592,512]{1,0:T(8,128)(2,1)S(1)} %dynamic-slice_bitcast_fusion.2), channel_id=1, source_target_pairs={{0,4},{4,0},{8,12},{12,8},{16,20},{20,16},{24,28},{28,24},{1,5},{5... | collective-permute-start | bytes 1818632 | tf_op jit(solution)/shard_map/ppermute | solution.py:632
  282.3 11.1 %collective-permute-start.21 = (bf16[296,512]{1,0:T(8,128)(2,1)S(1)}, bf16[296,512]{1,0:T(8,128)(2,1)S(1)}, u32[]{:S(2)}, u32[]{:S(2)}) collective-permute-start(bf16[296,512]{1,0:T(8,128)(2,1)S(1)} %dynamic-slice_bitcast_fusion.3), channel_id=1, source_target_pairs={{0,8},{4,12},{8,0},{12,4},{16,24},{20,28},{24,16},{28,20},{1,9},{5... | collective-permute-start | bytes 909320 | tf_op jit(solution)/shard_map/ppermute | solution.py:632
  283.9 6.0 %collective-permute-start.14 = (bf16[52,512]{1,0:T(8,128)(2,1)S(1)}, bf16[52,512]{1,0:T(8,128)(2,1)S(1)}, u32[]{:S(2)}, u32[]{:S(2)}) collective-permute-start(bf16[52,512]{1,0:T(8,128)(2,1)S(1)} %dynamic-slice_bitcast_fusion.8), channel_id=1, source_target_pairs={{0,16},{4,20},{8,24},{12,28},{16,0},{20,4},{24,8},{28,12},{1,17},{... | collective-permute-start | bytes 159752 | tf_op jit(solution)/shard_map/ppermute | solution.py:632
  289.9 8.3 %collective-permute-start.15 = (bf16[52,512]{1,0:T(8,128)(2,1)S(1)}, bf16[52,512]{1,0:T(8,128)(2,1)S(1)}, u32[]{:S(2)}, u32[]{:S(2)}) collective-permute-start(bf16[52,512]{1,0:T(8,128)(2,1)S(1)} %fusion.16), channel_id=1, source_target_pairs={{0,16},{4,20},{8,24},{12,28},{16,0},{20,4},{24,8},{28,12},{1,17},{... | collective-permute-start | bytes 159752 | tf_op jit(solution)/shard_map/ppermute | solution.py:632
  293.5 8.9 %collective-permute-start.22 = (bf16[148,512]{1,0:T(8,128)(2,1)S(1)}, bf16[148,512]{1,0:T(8,128)(2,1)S(1)}, u32[]{:S(2)}, u32[]{:S(2)}) collective-permute-start(bf16[148,512]{1,0:T(8,128)(2,1)S(1)} %dynamic-slice_bitcast_fusion.5), channel_id=1, source_target_pairs={{0,16},{4,20},{8,24},{12,28},{16,0},{20,4},{24,8},{28,12},{1,17},{... | collective-permute-start | bytes 454664 | tf_op jit(solution)/shard_map/ppermute | solution.py:632
  298.2 6.7 %collective-permute-start.16 = (bf16[104,512]{1,0:T(8,128)(2,1)S(1)}, bf16[104,512]{1,0:T(8,128)(2,1)S(1)}, u32[]{:S(2)}, u32[]{:S(2)}) collective-permute-start(bf16[104,512]{1,0:T(8,128)(2,1)S(1)} %pad_maximum_fusion.8), channel_id=1, source_target_pairs={{0,8},{4,12},{8,0},{12,4},{16,24},{20,28},{24,16},{28,20},{1,9},{5... | collective-permute-start | bytes 319496 | tf_op jit(solution)/shard_map/ppermute | solution.py:632
  302.5 7.3 %collective-permute-start.23 = (bf16[148,512]{1,0:T(8,128)(2,1)S(1)}, bf16[148,512]{1,0:T(8,128)(2,1)S(1)}, u32[]{:S(2)}, u32[]{:S(2)}) collective-permute-start(bf16[148,512]{1,0:T(8,128)(2,1)S(1)} %fusion.13), channel_id=1, source_target_pairs={{0,16},{4,20},{8,24},{12,28},{16,0},{20,4},{24,8},{28,12},{1,17},{... | collective-permute-start | bytes 454664 | tf_op jit(solution)/shard_map/ppermute | solution.py:632
  309.9 6.9 %collective-permute-start.24 = (bf16[296,512]{1,0:T(8,128)(2,1)S(1)}, bf16[296,512]{1,0:T(8,128)(2,1)S(1)}, u32[]{:S(2)}, u32[]{:S(2)}) collective-permute-start(bf16[296,512]{1,0:T(8,128)(2,1)S(1)} %pad_maximum_fusion.4), channel_id=1, source_target_pairs={{0,8},{4,12},{8,0},{12,4},{16,24},{20,28},{24,16},{28,20},{1,9},{5... | collective-permute-start | bytes 909320 | tf_op jit(solution)/shard_map/ppermute | solution.py:632
  316.9 15.8 %collective-permute-start.25 = (bf16[592,512]{1,0:T(8,128)(2,1)S(1)}, bf16[592,512]{1,0:T(8,128)(2,1)S(1)}, u32[]{:S(2)}, u32[]{:S(2)}) collective-permute-start(bf16[592,512]{1,0:T(8,128)(2,1)S(1)} %pad_maximum_fusion.3), channel_id=1, source_target_pairs={{0,4},{4,0},{8,12},{12,8},{16,20},{20,16},{24,28},{28,24},{1,5},{5... | collective-permute-start | bytes 1818632 | tf_op jit(solution)/shard_map/ppermute | solution.py:632
  (20 other events, 150.9 us)
Sparse Core Ops, SparseCore 0:
  9.6 22.4 all-gather.5
  33.6 22.6 all-gather.9
  57.8 22.5 all-gather.7

commit v2 on v1

v2 whole, which is shorter than its diff:
```python
from functools import partial
import math

import jax
import jax.numpy as jnp
from jax import lax
from jax.experimental import pallas as pl
from jax.experimental.pallas import tpu as pltpu
from jax.sharding import PartitionSpec as P

HEADS = 8
BLOCK = 16
LEVELS = 10
NEAR = 4
LOCAL = 7
CHUNK = 128
WIDTH = 512
PAIRS = HEADS // 2
ENTRY = 3 * WIDTH
SMALL = 16
MASKED = -1e30
EPSILON = 1e-05
VMEM_LIMIT = 56 * 1024 * 1024

f32 = jnp.float32
bf16 = jnp.bfloat16


def level_rows(rows, level):
    return rows // 2**level


def far_levels(total):
    return [l for l in range(LOCAL, LEVELS) if total // (BLOCK * 2**l) >= 2]


def extended_offsets(rows, far):
    offsets, cursor = [], 0
    for level in range(LOCAL):
        offsets.append(cursor)
        cursor += level_rows(rows, level) + 2 * BLOCK
    for _ in far:
        offsets.append(cursor)
        cursor += 2 * BLOCK
    return offsets, cursor


def slot_layout(far):
    parts = [(level, CHUNK // 2**level + 2 * BLOCK) for level in range(NEAR)]
    parts += [(level, BLOCK) for level in list(range(NEAR, LOCAL)) + far for _ in range(2)]
    return parts, sum(count for _, count in parts)


def slot_sources(rows, far, chunk):
    offsets, _ = extended_offsets(rows, far)
    sources = []
    for level in range(NEAR):
        sources.append((offsets[level] + chunk * (CHUNK // 2**level), CHUNK // 2**level + 2 * BLOCK))
    for level in range(NEAR, LOCAL):
        block = chunk // (BLOCK * 2**level // CHUNK)
        sources.append((offsets[level] + block * BLOCK, BLOCK))
        sources.append((offsets[level] + block * BLOCK + 2 * BLOCK, BLOCK))
    for at in range(len(far)):
        sources.append((offsets[LOCAL + at], BLOCK))
        sources.append((offsets[LOCAL + at] + BLOCK, BLOCK))
    return sources


def count_starts(positions, starts):
    total = jnp.full(positions.shape, -1, jnp.int32)
    for start in starts:
        total = total + (start <= positions).astype(jnp.int32)
    return total


def mask_kernel(rows, total, far, here_ref, lengths_ref, bias_ref):
    starts, start = [], jnp.int32(0)
    for at in range(lengths_ref.shape[1]):
        starts.append(start)
        start = start + lengths_ref[0, at]
    base = here_ref[0] * rows + pl.program_id(0) * CHUNK
    query = base + lax.broadcasted_iota(jnp.int32, (1, CHUNK), 1)
    query_doc = count_starts(query, starts)

    def part(at, count, first_row, level):
        span = 2**level
        shift = level + 4
        first = first_row + span * lax.broadcasted_iota(jnp.int32, (count, CHUNK), 0)
        gap = jnp.abs((first >> shift) - (query >> shift))
        if level == 0:
            seen = gap <= 1
        else:
            seen = (gap == 1) & (jnp.abs((first >> (shift - 1)) - (query >> (shift - 1))) > 1)
        doc = count_starts(first, starts)
        seen = seen & (first >= 0) & (first < total) & (doc == query_doc)
        if level:
            seen = seen & (count_starts(first + (span - 1), starts) == doc)
        bias_ref[0, at : at + count, :] = jnp.where(seen, level * math.log(2.0), MASKED)

    at = 0
    for level in range(NEAR):
        count = CHUNK // 2**level + 2 * BLOCK
        part(at, count, base - BLOCK * 2**level, level)
        at += count
    for level in list(range(NEAR, LOCAL)) + far:
        block = base >> (level + 4)
        for side in (-1, 1):
            part(at, BLOCK, (block + side) * (BLOCK * 2**level), level)
            at += BLOCK


def mask_call(rows, total, far, meta, lengths):
    chunks = rows // CHUNK
    _, slots = slot_layout(far)
    return pl.pallas_call(
        partial(mask_kernel, rows, total, far),
        grid=(chunks,),
        out_shape=jax.ShapeDtypeStruct((chunks, slots, CHUNK), f32),
        in_specs=[pl.BlockSpec(memory_space=pltpu.SMEM)] * 2,
        out_specs=pl.BlockSpec((1, slots, CHUNK), lambda i: (i, 0, 0)),
        cost_estimate=pl.CostEstimate(flops=4 << 30, bytes_accessed=3 << 20, transcendentals=0),
        name="mask",
    )(meta, lengths)


def dot_nt(left, right):
    return lax.dot_general(left, right, (((1,), (1,)), ((), ())), preferred_element_type=f32)


def dot_tn(left, right):
    return lax.dot_general(left, right, (((0,), (0,)), ((), ())), preferred_element_type=f32)


def dot_nn(left, right):
    return jnp.dot(left, right, preferred_element_type=f32)


def pool_matrix(count):
    row = lax.broadcasted_iota(jnp.int32, (count // 2, count), 0)
    column = lax.broadcasted_iota(jnp.int32, (count // 2, count), 1)
    return jnp.where((column >> 1) == row, 0.5, 0.0).astype(bf16)


def spread_matrix(count):
    row = lax.broadcasted_iota(jnp.int32, (2 * count, count), 0)
    column = lax.broadcasted_iota(jnp.int32, (2 * count, count), 1)
    return jnp.where((row >> 1) == column, 0.5, 0.0).astype(bf16)


def spread(values):
    count = values.shape[0]
    tile = min(count, 128)
    matrix = spread_matrix(tile)
    high = values.astype(bf16)
    low = (values - high.astype(f32)).astype(bf16)
    parts = [
        dot_nn(matrix, high[at : at + tile]) + dot_nn(matrix, low[at : at + tile])
        for at in range(0, count, tile)
    ]
    return parts[0] if len(parts) == 1 else jnp.concatenate(parts, axis=0)


def norm_rows(values):
    mean = jnp.mean(values, axis=-1, keepdims=True)
    centred = values - mean
    variance = jnp.mean(centred * centred, axis=-1, keepdims=True)
    inverse = lax.rsqrt(variance + EPSILON)
    return centred * inverse, inverse


def norm_back(grad_out, scaled, inverse, gain):
    grad_scaled = grad_out * gain
    first = jnp.mean(grad_scaled, axis=-1, keepdims=True)
    second = jnp.mean(grad_scaled * scaled, axis=-1, keepdims=True)
    return inverse * (grad_scaled - first - scaled * second)


def split_heads(pair):
    lane = lax.broadcasted_iota(jnp.int32, pair.shape, 1)
    zero = jnp.zeros_like(pair)
    return jnp.concatenate([jnp.where(lane < 64, pair, zero), jnp.where(lane < 64, zero, pair)], axis=0)


def join_heads(stacked):
    rows = stacked.shape[0] // 2
    lane = lax.broadcasted_iota(jnp.int32, (rows, stacked.shape[1]), 1)
    return jnp.where(lane < 64, stacked[:rows], stacked[rows:])


def pack_kernel(w_ref, *refs):
    out_ref = refs[-1]
    part = w_ref.shape[0]
    out_ref[0:part, :] = w_ref[...]
    row = jnp.concatenate([ref[...].reshape(1, -1) for ref in refs[:-1]], axis=1)
    out_ref[part : part + SMALL, :] = jnp.broadcast_to(row.astype(f32), (SMALL, row.shape[1])).astype(bf16)


def pack_call(weight, vectors):
    return pl.pallas_call(
        pack_kernel,
        out_shape=jax.ShapeDtypeStruct((weight.shape[0] + SMALL, weight.shape[1]), bf16),
        in_specs=vmem_specs(1 + len(vectors)),
        out_specs=vmem_specs(1)[0],
        name="pack",
    )(weight, *vectors)


def vmem_specs(count):
    return [pl.BlockSpec(memory_space=pltpu.VMEM)] * count


def qkv_kernel(rows, owners, meta_ref, x_ref, *refs):
    shard_refs, refs = refs[:owners], refs[owners:]
    w_ref, vec_ref, up_bias_ref, q_ref = refs[:4]
    kv_refs, scaled_refs = refs[4 : 4 + LOCAL], refs[4 + LOCAL : 4 + 2 * LOCAL]
    tail_ref, head_ref = refs[4 + 2 * LOCAL : 6 + 2 * LOCAL]
    keep_ref = refs[6 + 2 * LOCAL]
    part = WIDTH // owners
    step = pl.program_id(0)

    @pl.when(step == 0)
    def _():
        for at, ref in enumerate(shard_refs):
            owner = meta_ref[1 + at]
            w_ref[pl.ds(pl.multiple_of(owner * part, part), part), :] = ref[0:part, :]
            row = ref[part : part + 1, :].astype(f32)
            for vector in range(8):
                vec_ref[vector : vector + 1, pl.ds(pl.multiple_of(owner * part, part), part)] = row[
                    :, vector * part : (vector + 1) * part
                ]
            wide = row.shape[1] - 8 * part
            up_bias_ref[:, pl.ds(pl.multiple_of(owner * wide, wide), wide)] = row[:, 8 * part :]

    tile = x_ref.shape[0]
    scaled, _ = norm_rows(x_ref[...].astype(f32))
    normed = (scaled * vec_ref[0:1, :] + vec_ref[1:2, :]).astype(bf16)
    queries = (dot_nn(normed, w_ref[:, :WIDTH]) + vec_ref[2:3, :]).astype(bf16)
    q_ref[...] = queries * jnp.asarray(0.125, bf16)
    keys = dot_nn(normed, w_ref[:, WIDTH : 2 * WIDTH]).astype(bf16)
    values = (dot_nn(normed, w_ref[:, 2 * WIDTH :]) + vec_ref[3:4, :]).astype(bf16)
    current = jnp.concatenate([keys, values, scaled.astype(bf16)], axis=1)

    def edges(level, block):
        @pl.when(step == 0)
        def _():
            head_ref[BLOCK * level : BLOCK * (level + 1), :] = block[:BLOCK]

        @pl.when(step == pl.num_programs(0) - 1)
        def _():
            tail_ref[BLOCK * level : BLOCK * (level + 1), :] = block[block.shape[0] - BLOCK :]

    for level in range(5):
        if level:
            current = dot_nn(pool_matrix(current.shape[0]), current).astype(bf16)
        kv_refs[level][...] = current[:, : 2 * WIDTH]
        scaled_refs[level][...] = current[:, 2 * WIDTH :]
        edges(level, current)
    count = tile // 16
    keep_ref[pl.ds(pl.multiple_of(step * count, count), count), :] = current

    @pl.when(step == pl.num_programs(0) - 1)
    def _():
        current = keep_ref[...]
        for level in range(5, LOCAL):
            current = dot_nn(pool_matrix(current.shape[0]), current).astype(bf16)
            kv_refs[level][...] = current[:, : 2 * WIDTH]
            scaled_refs[level][...] = current[:, 2 * WIDTH :]
            tail_ref[BLOCK * level : BLOCK * (level + 1), :] = current[current.shape[0] - BLOCK :]
            head_ref[BLOCK * level : BLOCK * (level + 1), :] = current[:BLOCK]


def qkv_call(rows, hidden_width, meta, x, pieces):
    owners = len(pieces)
    tile = 256

    def tiled(count, width):
        return pl.BlockSpec((count, width), lambda i: (i, 0))

    def leveled(width):
        shapes, specs = [], []
        for level in range(LOCAL):
            shapes.append(jax.ShapeDtypeStruct((level_rows(rows, level), width), bf16))
            specs.append(tiled(tile // 2**level, width) if level < 5 else vmem_specs(1)[0])
        return shapes, specs

    kv_shapes, kv_specs = leveled(2 * WIDTH)
    scaled_shapes, scaled_specs = leveled(WIDTH)
    edge = jax.ShapeDtypeStruct((BLOCK * LOCAL, ENTRY), bf16)
    outs = pl.pallas_call(
        partial(qkv_kernel, rows, owners),
        grid=(rows // tile,),
        out_shape=[
            jax.ShapeDtypeStruct((WIDTH, 3 * WIDTH), bf16),
            jax.ShapeDtypeStruct((8, WIDTH), f32),
            jax.ShapeDtypeStruct((1, hidden_width), f32),
            jax.ShapeDtypeStruct((rows, WIDTH), bf16),
        ]
        + kv_shapes
        + scaled_shapes
        + [edge, edge],
        in_specs=[pl.BlockSpec(memory_space=pltpu.SMEM), tiled(tile, WIDTH)] + vmem_specs(owners),
        out_specs=vmem_specs(3) + [tiled(tile, WIDTH)] + kv_specs + scaled_specs + vmem_specs(2),
        scratch_shapes=[pltpu.VMEM((level_rows(rows, 4), ENTRY), bf16)],
        compiler_params=pltpu.CompilerParams(vmem_limit_bytes=VMEM_LIMIT),
        cost_estimate=pl.CostEstimate(flops=9 << 30, bytes_accessed=12 << 20, transcendentals=0),
        name="qkv_levels",
    )(meta, x, *pieces)
    weight, vectors, up_bias, queries = outs[:4]
    return weight, vectors, up_bias, queries, outs[4 : 4 + LOCAL], outs[4 + LOCAL : 4 + 2 * LOCAL], outs[-2], outs[-1]


def far_level(entries):
    return dot_nn(pool_matrix(entries.shape[0]), entries).astype(bf16)


def assemble(rows, far, here, columns, level_refs, left_ref, right_ref, base_ref, ext_ref, far_ref):
    offsets, _ = extended_offsets(rows, far)
    for inner, outer, target, width in columns:
        lanes, edge_lanes = slice(target, target + width), slice(outer, outer + width)
        for level in range(LOCAL):
            at, count = offsets[level], level_rows(rows, level)
            edge = slice(BLOCK * level, BLOCK * (level + 1))
            ext_ref[at : at + BLOCK, lanes] = left_ref[edge, edge_lanes]
            ext_ref[at + BLOCK : at + BLOCK + count, lanes] = level_refs[level][:, inner : inner + width]
            ext_ref[at + BLOCK + count : at + 2 * BLOCK + count, lanes] = right_ref[edge, edge_lanes]
        current = base_ref[:, edge_lanes]
        for index, level in enumerate(far):
            current = far_level(current)
            count = current.shape[0]
            far_ref[0:count, 0:width] = current
            for side, start in enumerate(far_starts(here, level, count)):
                at = offsets[LOCAL + index] + side * BLOCK
                ext_ref[at : at + BLOCK, lanes] = far_ref[pl.ds(start, BLOCK), 0:width]


def far_starts(here, level, count):
    block = here >> (level - 6)
    last = count // BLOCK - 1
    return [pl.multiple_of(jnp.clip(at, 0, last) * BLOCK, BLOCK) for at in (block - 1, block + 1)]


def load_slots(rows, far, chunk, ext_ref, slots_ref):
    at = 0
    for start, count in slot_sources(rows, far, chunk):
        if not isinstance(start, int):
            start = pl.multiple_of(start, BLOCK)
        slots_ref[at : at + count, :] = ext_ref[pl.ds(start, count), :]
        at += count


def attend_kernel(rows, far, meta_ref, q_ref, bias_ref, *refs):
    level_refs, refs = refs[:LOCAL], refs[LOCAL:]
    left_ref, right_ref, base_ref, out_ref, log_ref, ext_ref, far_ref, slots_ref = refs
    chunk = pl.program_id(0)

    @pl.when(chunk == 0)
    def _():
        columns = [(0, 0, 0, 2 * WIDTH)]
        assemble(rows, far, meta_ref[0], columns, level_refs, left_ref, right_ref, base_ref, ext_ref, far_ref)

    load_slots(rows, far, chunk, ext_ref, slots_ref)
    bias = bias_ref[0]
    bias = jnp.concatenate([bias, bias], axis=1)
    for pair in range(PAIRS):
        lanes = slice(128 * pair, 128 * (pair + 1))
        values = slots_ref[:, WIDTH + 128 * pair : WIDTH + 128 * (pair + 1)]
        scores = dot_nt(slots_ref[:, lanes], split_heads(q_ref[:, lanes])) + bias
        top = jnp.max(scores, axis=0, keepdims=True)
        exponent = jnp.exp(scores - top)
        total = jnp.sum(exponent, axis=0, keepdims=True)
        probs = (exponent * (1.0 / total)).astype(bf16)
        out_ref[:, lanes] = join_heads(dot_tn(probs, values)).astype(bf16)
        log_ref[0, pair : pair + 1, :] = top + jnp.log(total)


def attend_call(rows, devices, far, meta, q, bias, levels, left, right, base):
    chunks = rows // CHUNK
    _, entries = extended_offsets(rows, far)
    _, slots = slot_layout(far)
    return pl.pallas_call(
        partial(attend_kernel, rows, far),
        grid=(chunks,),
        out_shape=[
            jax.ShapeDtypeStruct((rows, WIDTH), bf16),
            jax.ShapeDtypeStruct((chunks, 8, 2 * CHUNK), f32),
        ],
        in_specs=[
            pl.BlockSpec(memory_space=pltpu.SMEM),
            pl.BlockSpec((CHUNK, WIDTH), lambda i: (i, 0)),
            pl.BlockSpec((1, slots, CHUNK), lambda i: (i, 0, 0)),
        ]
        + vmem_specs(LOCAL + 3),
        out_specs=[
            pl.BlockSpec((CHUNK, WIDTH), lambda i: (i, 0)),
            pl.BlockSpec((1, 8, 2 * CHUNK), lambda i: (i, 0, 0)),
        ],
        scratch_shapes=[
            pltpu.VMEM((entries, 2 * WIDTH), bf16),
            pltpu.VMEM((8 * devices, 2 * WIDTH), bf16),
            pltpu.VMEM((slots, 2 * WIDTH), bf16),
        ],
        compiler_params=pltpu.CompilerParams(vmem_limit_bytes=VMEM_LIMIT),
        cost_estimate=pl.CostEstimate(flops=20 << 30, bytes_accessed=12 << 20, transcendentals=4 << 20),
        name="attend",
    )(meta, q, bias, *levels, left, right, base)


def column_sum(values):
    return jnp.sum(values, axis=0, keepdims=True)


def matrix_row(left, right):
    total = None
    for a in two_parts(left):
        for b in two_parts(right):
            term = dot_nt(a, b)
            total = term if total is None else total + term
    return total[0:1]


def two_parts(values):
    if values.dtype == bf16:
        return [values]
    high = values.astype(bf16)
    return [high, (values - high.astype(f32)).astype(bf16)]


def attend_back_kernel(rows, far, first, count_pairs, combine, *refs):
    refs = list(refs)
    take = lambda count: [refs.pop(0) for _ in range(count)]
    meta_ref, q_ref, grad_ref, bias_ref, log_ref = take(5)
    level_refs, scaled_refs = take(LOCAL), take(LOCAL)
    left_ref, right_ref, base_ref, w_ref, vec_ref = take(5)
    if combine:
        before_left, before_right, before_far, before_weights, before_vec = take(5)
    dq_ref, local_ref, to_left_ref, to_right_ref, to_far_ref, weights_ref = take(6)
    vec_grad_ref = None if combine else take(1)[0]
    ext_ref, far_ref, slots_ref, acc_ref, tree_ref, scaled_ref, dq_keep_ref = take(7)
    chunk = pl.program_id(0)
    offsets, entries = extended_offsets(rows, far)
    half = 128 * count_pairs
    lane = 128 * first

    @pl.when(chunk == 0)
    def _():
        columns = [(lane, lane, 0, half), (WIDTH + lane, WIDTH + lane, half, half)]
        common = (left_ref, right_ref, base_ref)
        assemble(rows, far, meta_ref[0], columns, level_refs, *common, ext_ref, far_ref)
        assemble(rows, far, meta_ref[0], [(0, 2 * WIDTH, 0, WIDTH)], scaled_refs, *common, scaled_ref, far_ref)
        acc_ref[...] = jnp.zeros_like(acc_ref)

    load_slots(rows, far, chunk, ext_ref, slots_ref)
    bias = bias_ref[0]
    bias = jnp.concatenate([bias, bias], axis=1)
    sources = slot_sources(rows, far, chunk)
    for pair in range(count_pairs):
        lanes = slice(128 * pair, 128 * (pair + 1))
        value_lanes = slice(half + 128 * pair, half + 128 * (pair + 1))
        keys, values = slots_ref[:, lanes], slots_ref[:, value_lanes]
        queries, grads = split_heads(q_ref[:, lanes]), split_heads(grad_ref[:, lanes])
        logs = log_ref[0, first + pair : first + pair + 1, :]
        probs = jnp.exp(dot_nt(keys, queries) + bias - logs)
        grad_probs = dot_nt(values, grads)
        delta = jnp.sum(probs * grad_probs, axis=0, keepdims=True)
        grad_scores = (probs * (grad_probs - delta)).astype(bf16)
        dq = (join_heads(dot_tn(grad_scores, keys)) * 0.125).astype(bf16)
        dq_ref[:, lanes] = dq
        dq_keep_ref[pl.ds(pl.multiple_of(chunk * CHUNK, CHUNK), CHUNK), lanes] = dq
        grad_keys = dot_nn(grad_scores, queries)
        grad_values = dot_nn(probs.astype(bf16), grads)
        at = 0
        for start, count in sources:
            if not isinstance(start, int):
                start = pl.multiple_of(start, BLOCK)
            acc_ref[pl.ds(start, count), lanes] += grad_keys[at : at + count]
            acc_ref[pl.ds(start, count), value_lanes] += grad_values[at : at + count]
            at += count

    @pl.when(chunk == pl.num_programs(0) - 1)
    def _():
        dq = dq_keep_ref[...]
        sums = [column_sum(dq.astype(f32)), column_sum(acc_ref[:, :half]), column_sum(acc_ref[:, half:])]
        parts = [
            dot_tn(scaled_refs[0][...], dq),
            dot_tn(scaled_ref[...], acc_ref[:, :half].astype(bf16)),
            dot_tn(scaled_ref[...], acc_ref[:, half:].astype(bf16)),
        ]
        first_row = lax.broadcasted_iota(jnp.int32, (16, 1), 0) == 0
        ones = jnp.where(first_row, jnp.ones((16, half), f32), 0.0).astype(bf16)
        as_column = lambda row: dot_tn(jnp.where(first_row, row, 0.0).astype(bf16), ones)
        gain, shift = as_column(vec_ref[0:1, :]), as_column(vec_ref[1:2, :])
        gain_grad, shift_grad = jnp.zeros((1, WIDTH), f32), jnp.zeros((1, WIDTH), f32)
        owners = weights_ref.shape[0]
        part = WIDTH // owners
        for block in range(3):
            weight = w_ref[:, block * WIDTH + lane : block * WIDTH + lane + half]
            wide = weight.astype(f32)
            gain_grad += matrix_row(jnp.ones((16, half), bf16), wide * parts[block])
            shift_grad += matrix_row(jnp.broadcast_to(sums[block], (16, half)), weight)
            grad = (gain * parts[block] + shift * sums[block]).astype(bf16)
            for owner in range(owners):
                weights_ref[owner, block * part : (block + 1) * part, lane * combine : lane * combine + half] = grad[
                    owner * part : (owner + 1) * part
                ]
        if combine:
            for owner in range(owners):
                weights_ref[owner, 0 : 3 * part, 0:lane] = before_weights[owner, 0 : 3 * part, :]
            extend = lambda row, at: jnp.concatenate([before_vec[at : at + 1, 0:lane], row], axis=1)
            rows_out = [
                before_vec[0:1, :] + gain_grad,
                before_vec[1:2, :] + shift_grad,
                extend(sums[0], 2),
                extend(sums[2], 3),
            ]
            extra = weights_ref.shape[1] - 3 * part
            top_row = lax.broadcasted_iota(jnp.int32, (extra, 1), 0) == 0
            for owner in range(owners):
                row = jnp.concatenate([r[:, owner * part : (owner + 1) * part] for r in rows_out], axis=1)
                weights_ref[owner, 3 * part :, :] = jnp.where(top_row, row, 0.0).astype(bf16)
        else:
            vec_grad_ref[...] = jnp.zeros_like(vec_grad_ref)
            vec_grad_ref[0:1, :] = gain_grad
            vec_grad_ref[1:2, :] = shift_grad
            vec_grad_ref[2:3, 0:half] = sums[0]
            vec_grad_ref[3:4, 0:half] = sums[2]

        def put(target, values, before):
            if combine:
                target[:, 0:lane] = before[:, 0:lane]
                target[:, WIDTH : WIDTH + lane] = before[:, lane:]
                target[:, lane : lane + half] = values[:, :half].astype(bf16)
                target[:, WIDTH + lane : WIDTH + lane + half] = values[:, half:].astype(bf16)
            else:
                target[...] = values.astype(bf16)

        lefts, rights = [], []
        for level in range(LOCAL):
            at, count = offsets[level], level_rows(rows, level)
            lefts.append(acc_ref[at : at + BLOCK, :])
            rights.append(acc_ref[at + BLOCK + count : at + 2 * BLOCK + count, :])
        put(to_left_ref, jnp.concatenate(lefts, axis=0), before_left if combine else None)
        put(to_right_ref, jnp.concatenate(rights, axis=0), before_right if combine else None)
        carry = None
        for index in range(len(far) - 1, -1, -1):
            level = far[index]
            count = base_ref.shape[0] // 2 ** (level - LOCAL + 1)
            tree_ref[0:count, :] = jnp.zeros((count, 2 * half), f32) if carry is None else spread(carry)
            for side, start in enumerate(far_starts(meta_ref[0], level, count)):
                at = offsets[LOCAL + index] + side * BLOCK
                tree_ref[pl.ds(start, BLOCK), :] += acc_ref[at : at + BLOCK, :]
            carry = tree_ref[0:count, :]
        put(to_far_ref, carry, before_far if combine else None)
        for level in range(LOCAL - 1, 0, -1):
            at, count = offsets[level] + BLOCK, level_rows(rows, level)
            below = offsets[level - 1] + BLOCK
            tile = min(count, 128)
            for row in range(0, count, tile):
                carry = spread(acc_ref[at + row : at + row + tile, :])
                target = slice(below + 2 * row, below + 2 * (row + tile))
                total = acc_ref[target, :] + carry
                if level == 1:
                    local_ref[2 * row : 2 * (row + tile), :] = total
                else:
                    acc_ref[target, :] = total


def attend_back_call(rows, devices, far, owners, first, count_pairs, before, meta, q, grads, bias, logs, levels, scaled, left, right, base, weight, vectors):
    chunks = rows // CHUNK
    _, entries = extended_offsets(rows, far)
    _, slots = slot_layout(far)
    combine = before is not None
    half = 128 * count_pairs
    side = 2 * WIDTH if combine else 2 * half
    part = WIDTH // owners
    lanes = first // count_pairs
    outs = [
        jax.ShapeDtypeStruct((rows, half), bf16),
        jax.ShapeDtypeStruct((rows, 2 * half), f32),
        jax.ShapeDtypeStruct((BLOCK * LOCAL, side), bf16),
        jax.ShapeDtypeStruct((BLOCK * LOCAL, side), bf16),
        jax.ShapeDtypeStruct((8 * devices, side), bf16),
        jax.ShapeDtypeStruct((owners, 3 * part + 64, WIDTH) if combine else (owners, 3 * part, half), bf16),
    ]
    if not combine:
        outs.append(jax.ShapeDtypeStruct((8, WIDTH), f32))
    return pl.pallas_call(
        partial(attend_back_kernel, rows, far, first, count_pairs, combine),
        grid=(chunks,),
        out_shape=outs,
        in_specs=[
            pl.BlockSpec(memory_space=pltpu.SMEM),
            pl.BlockSpec((CHUNK, half), lambda i: (i, lanes)),
            pl.BlockSpec((CHUNK, half), lambda i: (i, lanes)),
            pl.BlockSpec((1, slots, CHUNK), lambda i: (i, 0, 0)),
            pl.BlockSpec((1, 8, 2 * CHUNK), lambda i: (i, 0, 0)),
        ]
        + vmem_specs(2 * LOCAL + 5 + (5 if combine else 0)),
        out_specs=[pl.BlockSpec((CHUNK, half), lambda i: (i, 0))] + vmem_specs(len(outs) - 1),
        scratch_shapes=[
            pltpu.VMEM((entries, 2 * half), bf16),
            pltpu.VMEM((8 * devices, WIDTH), bf16),
            pltpu.VMEM((slots, 2 * half), bf16),
            pltpu.VMEM((entries, 2 * half), f32),
            pltpu.VMEM((8 * devices, 2 * half), f32),
            pltpu.VMEM((entries, WIDTH), bf16),
            pltpu.VMEM((rows, half), bf16),
        ],
        compiler_params=pltpu.CompilerParams(vmem_limit_bytes=VMEM_LIMIT),
        cost_estimate=pl.CostEstimate(flops=(40 << 30) * count_pairs // PAIRS, bytes_accessed=12 << 20, transcendentals=4 << 20),
        name="attend_back",
    )(meta, q, grads, bias, logs, *levels, *scaled, left, right, base, weight, vectors, *(before or []))


def normal_parts(values):
    size = jnp.abs(values)
    bell = jnp.exp(-0.5 * values * values)
    t = 1.0 / (1.0 + (0.3275911 / math.sqrt(2.0)) * size)
    poly = t * (
        0.5 * 0.254829592
        + t * (0.5 * -0.284496736 + t * (0.5 * 1.421413741 + t * (0.5 * -1.453152027 + t * (0.5 * 1.061405429))))
    )
    tail = poly * bell
    return jnp.where(values < 0, tail, 1.0 - tail), bell * (1.0 / math.sqrt(2.0 * math.pi))


def feed_kernel(
    hidden_width,
    x_ref,
    attended_ref,
    cot_ref,
    rest_ref,
    up_w_ref,
    vec_ref,
    up_bias_ref,
    y_ref,
    grad_middle_ref,
    grad_attended_ref,
    weights_ref,
    out_w_ref,
    vec_grad_ref,
    up_bias_grad_ref,
    down_acc,
    up_acc,
    out_acc,
):
    step = pl.program_id(0)
    owners = rest_ref.shape[0]
    rows = WIDTH // owners
    wide_rows = hidden_width // owners

    @pl.when(step == 0)
    def _():
        for owner in range(owners):
            out_w_ref[owner * rows : (owner + 1) * rows, :] = rest_ref[owner, wide_rows:, :]
        down_acc[...] = jnp.zeros_like(down_acc)
        up_acc[...] = jnp.zeros_like(up_acc)
        out_acc[...] = jnp.zeros_like(out_acc)
        vec_grad_ref[...] = jnp.zeros_like(vec_grad_ref)
        up_bias_grad_ref[...] = jnp.zeros_like(up_bias_grad_ref)

    out_bias, gain, shift, down_bias = (vec_ref[4 + at : 5 + at, :] for at in range(4))
    attended = attended_ref[...]
    middle = x_ref[...].astype(f32) + dot_nn(attended, out_w_ref[...]) + out_bias
    scaled, inverse = norm_rows(middle)
    normed = (scaled * gain + shift).astype(bf16)
    cot = cot_ref[...]
    wide = cot.astype(f32)
    lowered = jnp.zeros_like(middle)
    grad_normed = jnp.zeros_like(middle)
    for owner in range(owners):
        columns = slice(owner * wide_rows, (owner + 1) * wide_rows)
        down = rest_ref[owner, 0:wide_rows, :]
        pre = dot_nn(normed, up_w_ref[:, columns]) + up_bias_ref[:, columns]
        phi, bell = normal_parts(pre)
        hidden = (pre * phi).astype(bf16)
        lowered += dot_nn(hidden, down)
        grad_pre = (dot_nt(cot, down) * (phi + pre * bell)).astype(bf16)
        up_bias_grad_ref[:, columns] += column_sum(grad_pre.astype(f32))
        grad_normed += dot_nt(grad_pre, up_w_ref[:, columns])
        down_acc[columns, :] += dot_tn(hidden, cot)
        up_acc[:, columns] += dot_tn(normed, grad_pre)
    y_ref[...] = (middle + lowered + down_bias).astype(bf16)
    grad_middle = wide + norm_back(grad_normed, scaled, inverse, gain)
    grad_middle_ref[...] = grad_middle
    grad_proj = grad_middle.astype(bf16)
    grad_attended_ref[...] = dot_nt(grad_proj, out_w_ref[...]).astype(bf16)
    out_acc[...] += dot_tn(attended, grad_proj)
    vec_grad_ref[0:1, :] += column_sum(grad_proj.astype(f32))
    vec_grad_ref[1:2, :] += column_sum(grad_normed * scaled)
    vec_grad_ref[2:3, :] += column_sum(grad_normed)
    vec_grad_ref[3:4, :] += column_sum(wide)

    @pl.when(step == pl.num_programs(0) - 1)
    def _():
        extra = weights_ref.shape[1] - 2 * wide_rows - rows
        row_at = lax.broadcasted_iota(jnp.int32, (extra, 1), 0)
        for owner in range(owners):
            wide_span, span = slice(owner * wide_rows, (owner + 1) * wide_rows), slice(owner * rows, (owner + 1) * rows)
            weights_ref[owner, 0:wide_rows, :] = down_acc[wide_span, :].astype(bf16)
            at = wide_rows
            for block in range(hidden_width // WIDTH):
                weights_ref[owner, at : at + rows, :] = up_acc[span, block * WIDTH : (block + 1) * WIDTH].astype(bf16)
                at += rows
            weights_ref[owner, at : at + rows, :] = out_acc[span, :].astype(bf16)
            first = jnp.concatenate([vec_grad_ref[i : i + 1, span] for i in range(4)], axis=1)
            second = up_bias_grad_ref[:, wide_span]
            weights_ref[owner, at + rows :, :] = jnp.where(
                row_at == 0, first, jnp.where(row_at == 1, second, 0.0)
            ).astype(bf16)


def feed_call(owners, x, attended, cot, rest, up_w, vectors, up_bias):
    rows, hidden_width = x.shape[0], up_w.shape[1]
    tile = 256
    row_spec = pl.BlockSpec((tile, WIDTH), lambda i: (i, 0))
    packed = 2 * (hidden_width // owners) + WIDTH // owners + 64
    return pl.pallas_call(
        partial(feed_kernel, hidden_width),
        grid=(rows // tile,),
        out_shape=[
            jax.ShapeDtypeStruct((rows, WIDTH), bf16),
            jax.ShapeDtypeStruct((rows, WIDTH), f32),
            jax.ShapeDtypeStruct((rows, WIDTH), bf16),
            jax.ShapeDtypeStruct((owners, packed, WIDTH), bf16),
        ],
        in_specs=[row_spec, row_spec, row_spec] + vmem_specs(4),
        out_specs=[row_spec, row_spec, row_spec] + vmem_specs(1),
        scratch_shapes=[
            pltpu.VMEM((WIDTH, WIDTH), bf16),
            pltpu.VMEM((8, WIDTH), f32),
            pltpu.VMEM((1, hidden_width), f32),
            pltpu.VMEM((hidden_width, WIDTH), f32),
            pltpu.VMEM((WIDTH, hidden_width), f32),
            pltpu.VMEM((WIDTH, WIDTH), f32),
        ],
        compiler_params=pltpu.CompilerParams(vmem_limit_bytes=VMEM_LIMIT),
        cost_estimate=pl.CostEstimate(flops=32 << 30, bytes_accessed=20 << 20, transcendentals=4 << 20),
        name="feed_forward",
    )(x, attended, cot, rest, up_w, vectors, up_bias)


def input_grad_kernel(
    x_ref,
    dq_refs,
    local_refs,
    grad_middle_ref,
    from_right_ref,
    from_left_ref,
    base_ref,
    w_ref,
    vec_ref,
    out_ref,
    tree_ref,
):
    rows = tree_ref.shape[0]
    step = pl.program_id(0)
    tile = x_ref.shape[0]

    @pl.when(step == 0)
    def _():
        carry = spread(base_ref[...].astype(f32))
        for level in range(LOCAL - 1, -1, -1):
            count = level_rows(rows, level)
            edge = slice(BLOCK * level, BLOCK * (level + 1))
            if level == LOCAL - 1:
                tree_ref[0:count, :] = carry
            tree_ref[0:BLOCK, :] += from_left_ref[edge, :].astype(f32)
            tree_ref[count - BLOCK : count, :] += from_right_ref[edge, :].astype(f32)
            if level:
                part = min(count, 128)
                for row in range(count - part, -1, -part):
                    tree_ref[2 * row : 2 * (row + part), :] = spread(tree_ref[row : row + part, :])

    span = pl.ds(pl.multiple_of(step * tile, tile), tile)
    scaled, inverse = norm_rows(x_ref[...].astype(f32))
    grad = jnp.zeros((tile, WIDTH), f32)
    half = dq_refs[0].shape[1]
    for index, (dq_ref, local_ref) in enumerate(zip(dq_refs, local_refs)):
        lane = index * half
        grad += dot_nt(dq_ref[...], w_ref[:, lane : lane + half])
        for block in range(2):
            column = block * WIDTH + lane
            dkv = (local_ref[:, block * half : (block + 1) * half] + tree_ref[span, column : column + half]).astype(bf16)
            grad += dot_nt(dkv, w_ref[:, WIDTH + column : WIDTH + column + half])
    out_ref[...] = grad_middle_ref[...] + norm_back(grad, scaled, inverse, vec_ref[0:1, :])


def input_grad_call(x, dqs, locals_, grad_middle, from_right, from_left, base, weight, vectors):
    rows = x.shape[0]
    tile = 256
    count = len(dqs)
    tiled = lambda width: pl.BlockSpec((tile, width), lambda i: (i, 0))

    def kernel(x_ref, *refs):
        input_grad_kernel(x_ref, refs[:count], refs[count : 2 * count], *refs[2 * count :])

    return pl.pallas_call(
        kernel,
        grid=(rows // tile,),
        out_shape=jax.ShapeDtypeStruct((rows, WIDTH), f32),
        in_specs=[tiled(WIDTH)]
        + [tiled(d.shape[1]) for d in dqs]
        + [tiled(d.shape[1]) for d in locals_]
        + [tiled(WIDTH)]
        + vmem_specs(5),
        out_specs=tiled(WIDTH),
        scratch_shapes=[pltpu.VMEM((rows, 2 * WIDTH), f32)],
        compiler_params=pltpu.CompilerParams(vmem_limit_bytes=VMEM_LIMIT),
        cost_estimate=pl.CostEstimate(flops=8 << 30, bytes_accessed=14 << 20, transcendentals=0),
        name="input_grad",
    )(x, *dqs, *locals_, grad_middle, from_right, from_left, base, weight, vectors)


def shifted(block, axis, distance):
    devices = range(lax.axis_size(axis))
    route = [(i - distance, i) for i in devices if i - distance in devices]
    return lax.ppermute(block, axis, route)


def swap(block, axis, bit):
    return lax.ppermute(block, axis, [(i, i ^ bit) for i in range(lax.axis_size(axis))])


def add_low(left, right):
    return (left.astype(f32) + right.astype(f32)).astype(bf16)


def scatter_step(parts, axis, bit):
    mine = (lax.axis_index(axis) // bit) % 2
    keep = lax.dynamic_index_in_dim(parts, mine, 0, keepdims=False)
    send = lax.dynamic_index_in_dim(parts, 1 - mine, 0, keepdims=False)
    return add_low(keep, swap(send, axis, bit))


def gather_step(part, axis, bit, rows_axis=0):
    mine = (lax.axis_index(axis) // bit) % 2
    other = swap(part, axis, bit)
    first = jnp.where(mine == 0, part, other)
    second = jnp.where(mine == 0, other, part)
    return jnp.concatenate([first, second], axis=rows_axis)


def together(*values):
    return lax.optimization_barrier(values)


def bits_of(axis):
    size = lax.axis_size(axis)
    return [1 << at for at in range(size.bit_length() - 1)]


class Reduction:
    def __init__(self, parts):
        self.shape = parts.shape[1:]
        self.value = parts
        self.done = []
        self.todo = [self.low, self.cross_one, self.cross_two]
        self.todo += [partial(self.scatter, bit) for bit in bits_of("ctx")[1:]]
        self.todo += [partial(self.gather, bit) for bit in reversed(bits_of("ctx")[1:])]
        self.todo += [self.last]

    def step(self, count=1):
        for _ in range(count):
            if self.todo:
                self.todo.pop(0)()
        return self

    def after(self, *others):
        tied = together(self.value, *others)
        self.value = tied[0]
        return tied[1:]

    def low(self):
        owners = self.value.shape[0]
        self.value = scatter_step(self.value.reshape(owners // 2, 2, *self.shape).transpose(1, 0, 2, 3), "fsdp", 1)

    def over_owners(self, current):
        for bit in bits_of("fsdp")[1:]:
            current = current.reshape(-1, 2, *current.shape[1:]).transpose(1, 0, 2, 3)
            current = scatter_step(current, "fsdp", bit)
        return current.reshape(current.shape[1:])

    def over_ctx(self, current):
        outer, rows, width = current.shape
        return scatter_step(current.reshape(outer, 2, rows // 2, width).transpose(1, 0, 2, 3), "ctx", 1)

    def cross_one(self):
        half = self.shape[0] // 2
        one, two = self.value[:, :half], self.value[:, half:]
        self.value = (self.over_owners(one)[None], self.over_ctx(two))

    def cross_two(self):
        one, two = self.value
        self.value = jnp.concatenate([self.over_ctx(one)[0], self.over_owners(two)], axis=0)

    def scatter(self, bit):
        rows, width = self.value.shape
        self.value = scatter_step(self.value.reshape(2, rows // 2, width), "ctx", bit)

    def gather(self, bit):
        self.value = gather_step(self.value, "ctx", bit)

    def last(self):
        rows, width = self.value.shape
        both = gather_step(self.value.reshape(2, 1, rows // 2, width), "ctx", 1, 1)
        self.value = both.reshape(2 * rows, width)


def shards(
    layer_input,
    doc_lengths,
    ln1_gain,
    ln1_bias,
    qkv_weight,
    query_bias,
    value_bias,
    out_weight,
    out_bias,
    ln2_gain,
    ln2_bias,
    up_weight,
    up_bias,
    down_weight,
    down_bias,
    cotangent,
):
    owners = lax.axis_size("fsdp")
    devices = lax.axis_size("ctx")
    x, cot = layer_input[0], cotangent[0]
    rows = x.shape[0]
    total = rows * devices
    far = far_levels(total)
    here, owner = lax.axis_index("ctx"), lax.axis_index("fsdp")
    part = WIDTH // owners
    hidden_width = up_weight.shape[1]
    meta = jnp.stack([here] + [owner ^ at for at in range(owners)]).astype(jnp.int32)

    vectors = [ln1_gain, ln1_bias, query_bias, value_bias, out_bias, ln2_gain, ln2_bias, down_bias, up_bias]
    pieces = {0: pack_call(qkv_weight, vectors)}
    for bit in reversed(bits_of("fsdp")):
        for at in list(pieces):
            pieces[at ^ bit] = swap(pieces[at], "fsdp", bit)
    rest_shard = jnp.concatenate([down_weight, out_weight], axis=0)
    tied = together(up_weight, rest_shard, *(pieces[at] for at in range(owners)))
    pieces = tied[2:]
    rest = lax.all_gather(tied[1], "fsdp", axis=0, tiled=False)
    up_full = lax.all_gather(tied[0], "fsdp", axis=0, tiled=True)

    bias = mask_call(rows, total, far, meta, doc_lengths)
    qkv_full, vec, up_shift, queries, levels, scaled, tail, head = qkv_call(rows, hidden_width, meta, x, pieces)
    left = shifted(tail, "ctx", 1)
    right = shifted(head, "ctx", -1)
    base = tail[BLOCK * (LOCAL - 1) :]
    for at, bit in enumerate(bits_of("ctx")):
        base = gather_step(base, "ctx", bit)
        if at == 0:
            base, left, right = together(base, left, right)

    attended, logs = attend_call(rows, devices, far, meta, queries, bias, levels, left, right, base)
    output, grad_middle, grad_attended, feed_grads = feed_call(
        owners, x, attended, cot, rest, up_full, vec, up_shift
    )
    feed = Reduction(feed_grads).step()
    back = partial(attend_back_call, rows, devices, far, owners)
    count = PAIRS // 2
    common = (bias, logs, levels, scaled, left, right, base, qkv_full, vec)
    (grad_attended,) = feed.after(grad_attended)
    dq_one, local_one, *before = back(0, count, None, meta, queries, grad_attended, *common)
    feed.step()
    tied = together(*feed.value, *before)
    feed.value, before = tied[:2], tied[2:]
    dq_two, local_two, to_left, to_right, to_far, qkv_grads = back(
        count, count, before, meta, queries, grad_attended, *common
    )
    feed.step()
    first = Reduction(qkv_grads)

    back_right = shifted(to_left, "ctx", -1)
    back_left = shifted(to_right, "ctx", 1)
    back_far = to_far
    for at, bit in enumerate(reversed(bits_of("ctx"))):
        back_far = scatter_step(back_far.reshape(2, -1, 2 * WIDTH), "ctx", bit)
        if at == 0:
            back_far, back_right, back_left = together(back_far, back_right, back_left)
    input_grad = input_grad_call(
        x, [dq_one, dq_two], [local_one, local_two], grad_middle, back_right, back_left, back_far, qkv_full, vec
    )
    while feed.todo or first.todo:
        first.step()
        feed.step()
    feed_sum, qkv_sum = feed.value.astype(f32), first.value.astype(f32)

    wide_rows = hidden_width // owners
    down_grad = feed_sum[:wide_rows]
    up_grad = jnp.concatenate(
        [feed_sum[wide_rows + at * part : wide_rows + (at + 1) * part] for at in range(hidden_width // WIDTH)], axis=1
    )
    out_grad = feed_sum[2 * wide_rows : 2 * wide_rows + part]
    feed_row = feed_sum[2 * wide_rows + part]
    up_row = feed_sum[2 * wide_rows + part + 1]
    qkv_grad = jnp.concatenate([qkv_sum[at * part : (at + 1) * part] for at in range(3)], axis=1)
    first_row = qkv_sum[3 * part]
    pick = lambda row, at: row[at * part : (at + 1) * part]
    return (
        output[None],
        input_grad[None],
        pick(first_row, 0),
        pick(first_row, 1),
        qkv_grad,
        pick(first_row, 2),
        pick(first_row, 3),
        out_grad,
        pick(feed_row, 0),
        pick(feed_row, 1),
        pick(feed_row, 2),
        up_grad,
        up_row,
        down_grad,
        pick(feed_row, 3),
    )


def solution(mesh):
    row, vector = P("fsdp", None), P("fsdp")
    tokens = P("fsdp", "ctx", None)
    return jax.shard_map(
        shards,
        mesh=mesh,
        in_specs=(
            tokens,
            row,
            vector,
            vector,
            row,
            vector,
            vector,
            row,
            vector,
            vector,
            vector,
            row,
            vector,
            row,
            vector,
            tokens,
        ),
        out_specs=(
            tokens,
            tokens,
            vector,
            vector,
            row,
            vector,
            vector,
            row,
            vector,
            vector,
            vector,
            row,
            vector,
            row,
            vector,
        ),
        check_vma=False,
    )
```

time: 345 us -> 303 us (0.88)
  other arithmetic: 37.7 us -> 12.8 us
  Pallas kernels: 106 us -> 128 us
  blocking collectives: 13.9 us -> 0 us
  local copies, waits for them, and re-layouts: 21.7 us -> 9.99 us
  waiting for transfers between devices: 103 us -> 92.9 us
    pallas_call x4 -> x7, Pallas kernels: 74.5 us -> 96.3 us  [the longest x2 46.1 us: attend_back_call(): pl.pallas_call(partial(attend_back_kernel, rows, far, first, count_pairs,...]
    ppermute x22 -> x29, waiting for transfers between devices: 88.4 us -> 71.8 us  [swap(): lax.ppermute(block, axis, [(i, i ^ bit) for i in range(lax.axis_size(axis...]
    all_gather x2 -> x0, blocking collectives: 13.9 us -> none  [the longest x1 7.67 us: shards(): out_full = lax.all_gather(out_weight, 'fsdp', axis=0, tiled=True)]
    unnamed x41 -> x16, local copies, waits for them, and re-layouts: 12.8 us -> 0.94 us
    ppermute x4, waiting for transfers between devices: 12.8 us -> 21.1 us  [shifted(): return lax.ppermute(block, axis, route)]
    shift_right_arithmetic x1 -> x0, other arithmetic: 5.94 us -> none  [score_bias(): gap = jnp.abs((first3 >> shift3) - (query3 >> shift3))]
    add x11 -> x0, other arithmetic: 5.9 us -> none  [the longest x1 5.26 us: score_bias(): query = bases[:, None] + jnp.arange(CHUNK, dtype=jnp.int32)[None, :]]
    select_n x1 -> x0, other arithmetic: 3.92 us -> none  [score_bias(): jnp.where(seen, level[:, :, None].astype(f32) * math.log(2.0), MASKED)]
  transfers between devices with their start and end apart: 29 -> 35, of which waited for: 19 -> 20; matrix products, arithmetic and copies ran while one was open for 13% -> 4% of each run, Pallas kernels for 22% -> 23%
where the time goes in v2:
time: 303 us; the launch traced here: 302 us
  Pallas kernels  128 us (42%)
  waiting for transfers between devices  92.9 us (31%)
  starting transfers between devices  44.1 us (15%)
  between operations  14.7 us (5%)
  other arithmetic  12.8 us (4%)
  local copies, waits for them, and re-layouts  9.99 us (3%)
    ppermute x29, waiting for transfers between devices, swap(): lax.ppermute(block, axis, [(i, i ^ bit) for i in range(lax.axis_size(axis...  71.8 us
    pallas_call x2, Pallas kernels, attend_back_call(): pl.pallas_call(partial(attend_back_kernel, rows, far, first, count_pairs,...  46.1 us
    ppermute x29, starting transfers between devices, swap(): lax.ppermute(block, axis, [(i, i ^ bit) for i in range(lax.axis_size(axis...  34.7 us
    pallas_call x1, Pallas kernels, feed_call(): pl.pallas_call(partial(feed_kernel, hidden_width), grid=(rows // tile,),...  31.4 us
    pallas_call x1, Pallas kernels, attend_call(): pl.pallas_call(partial(attend_kernel, rows, far), grid=(chunks,), out_sha...  21.2 us
    ppermute x4, waiting for transfers between devices, shifted(): return lax.ppermute(block, axis, route)  21.1 us
    pallas_call x1, Pallas kernels, qkv_call(): pl.pallas_call(partial(qkv_kernel, rows, owners), grid=(rows // tile,), o...  10.5 us
    pallas_call x1, Pallas kernels, input_grad_call(): pl.pallas_call(kernel, grid=(rows // tile,), out_shape=jax.ShapeDtypeStru...  10.4 us
  transfers between devices with their start and end apart: 35, of which 20 were waited for; matrix products, arithmetic and copies ran while one was open for 4% of the time, Pallas kernels for 23%

profile of v2, /device:TPU:0, one launch (start us, length us, event | category | flops | bytes accessed | tf_op | source)
XLA Modules:
  0.0 302.2 jit_solution(6328887351238545585)
XLA Ops:
  12.1 10.4 %collective-permute-done.1.refs_2_ = bf16[144,1536]{1,0:T(8,128)(2,1)S(1)} collective-permute-done((bf16[144,1536]{1,0:T(8,128)(2,1)}, bf16[144,1536]{1,0:T(8,128)(2,1)S(1)}, u32[]{:S(2)}, u32[]{:S(2)}) %collective-permute-start.1) | collective-permute-done | bytes 442400 | tf_op jit(solution)/shard_map/ppermute | solution.py:821
  25.5 10.5 %qkv_levels.1 = (bf16[512,1536]{1,0:T(8,128)(2,1)}, f32[8,512]{1,0:T(8,128)}, f32[1,2048]{1,0:T(1,128)}, bf16[1024,512]{1,0:T(8,128)(2,1)}, bf16[1024,1024]{1,0:...) custom-call(s32[5]{0:T(128)} %stack.23.meta_ref.here_ref.refs_0_, ...), custom_call_target="tpu_custom_call" | custom-call | flops 9663676416 | bytes 12582912 | tf_op jit(solution)/shard_map/qkv_levels/pallas_call | solution.py:289
  43.0 13.0 %collective-permute-done.4.refs_7_.refs_19_ = bf16[112,1536]{1,0:T(8,128)(2,1)S(1)} collective-permute-done((bf16[112,1536]{1,0:T(8,128)(2,1)}, bf16[112,1536]{1,0:T(8,128)(2,1)S(1)}, u32[]{:S(2)}, u32[]{:S(2)}) %collective-permute-start.4) | collective-permute-done | bytes 344096 | tf_op jit(solution)/shard_map/ppermute | solution.py:817
  56.0 4.5 %collective-permute-start.6 = (bf16[32,1536]{1,0:T(8,128)(2,1)S(1)}, bf16[32,1536]{1,0:T(8,128)(2,1)S(1)}, u32[]{:S(2)}, u32[]{:S(2)}) collective-permute-start(bf16[32,1536]{1,0:T(8,128)(2,1)S(1)} %pad_maximum_fusion.13), channel_id=1, source_target_pairs={{0,8},{4,12},{8,0},{12,4},{16,24},{20,28},{24,16},{28,20},{1,9},{5... | collective-permute-start | bytes 294920 | tf_op jit(solution)/shard_map/ppermute | solution.py:821
  60.6 3.0 collective-permute-done.6
  66.4 6.2 %mask.1.bias_ref.refs_3_ = f32[8,528,128]{2,1,0:T(8,128)} custom-call(s32[5]{0:T(128)} %stack.23.meta_ref.here_ref.refs_0_, s32[1,8]{1,0:T(1,128)} %lengths_ref.1), custom_call_target="tpu_custom_call" | custom-call | flops 4294967296 | bytes 3145728 | tf_op jit(solution)/shard_map/mask/pallas_call | solution.py:115
  76.0 21.2 %attend.1 = (bf16[1024,512]{1,0:T(8,128)(2,1)}, f32[8,8,256]{2,1,0:T(8,128)}) custom-call(s32[5]{0:T(128)} %stack.23.meta_ref.here_ref.refs_0_, bf16[1024,512]{1,0:T(8,128)(2,1)} %get-tuple-element.79.q_ref.refs_1_, f32[8,528,128]{2,1,0:T(8,128)} %mask.1.bias_ref.refs_3_, bf16[1024,1024]{1,0:T(8,128)(2,1)} %get-tuple-element.80.refs_0_.refs_5_, ...), custom_call_target="tpu_custom_call" | custom-call | flops 21474836480 | bytes 12582912 | tf_op jit(solution)/shard_map/attend/pallas_call | solution.py:380
  97.2 31.4 %feed_forward.1 = (bf16[1024,512]{1,0:T(8,128)(2,1)}, f32[1024,512]{1,0:T(8,128)}, bf16[1024,512]{1,0:T(8,128)(2,1)}, bf16[4,1216,512]{2,1,0:T(8,128)(2,1)}) custom-call(bf16[1024,512]{1,0:T(8,128)(2,1)} %bitcast.158, bf16[1024,512]{1,0:T(8,128)(2,1)} %get-tuple-element.92.attended_ref, bf16[1024,512]{1,0:T(8,128)(2,1)} %bitcast.156, ...), custom_call_target="tpu_custom_call" | custom-call | flops 34359738368 | bytes 20971520 | tf_op jit(solution)/shard_map/feed_forward/pallas_call | solution.py:717
  130.7 4.8 %collective-permute-done.8 = bf16[2,1216,512]{2,1,0:T(8,128)(2,1)} collective-permute-done((bf16[2,1216,512]{2,1,0:T(8,128)(2,1)S(1)}, bf16[2,1216,512]{2,1,0:T(8,128)(2,1)}, u32[]{:S(2)}, u32[]{:S(2)}) %collective-permute-start.8) | collective-permute-done | bytes 2490400 | tf_op jit(solution)/shard_map/ppermute | solution.py:821
  135.5 3.2 %fusion = bf16[2,1216,512]{2,1,0:T(8,128)(2,1)S(1)} fusion(bf16[2,1216,512]{2,1,0:T(8,128)(2,1)} %collective-permute-done.8, bf16[2,2,1216,512]{3,2,1,0:T(8,128)(2,1)} %bitcast.129, s32[]{:T(128)S(6)} %select_n.290), kind=kLoop, calls=%fused_computation.1 | loop fusion | flops 4980736 | bytes 7471108 | tf_op jit(solution)/shard_map/convert_element_type | solution.py:825
  140.6 22.6 %attend_back.2 = (bf16[1024,256]{1,0:T(8,128)(2,1)}, f32[1024,512]{1,0:T(8,128)}, bf16[112,512]{1,0:T(8,128)(2,1)}, bf16[112,512]{1,0:T(8,128)(2,1)}, bf16[64,51...) custom-call(s32[5]{0:T(128)} %stack.23.meta_ref.here_ref.refs_0_, ...), custom_call_target="tpu_custom_call" | custom-call | flops 21474836480 | bytes 12582912 | tf_op jit(solution)/shard_map/attend_back/pallas_call | solution.py:586
  163.5 23.5 %attend_back.3 = (bf16[1024,256]{1,0:T(8,128)(2,1)}, f32[1024,512]{1,0:T(8,128)}, bf16[112,1024]{1,0:T(8,128)(2,1)}, bf16[112,1024]{1,0:T(8,128)(2,1)}, bf16[64,...) custom-call(s32[5]{0:T(128)} %stack.23.meta_ref.here_ref.refs_0_, bf16[1024,512]{1,0:T(8,128)(2,1)} %get-tuple-element.79.q_ref.refs_1_, ...), custom_call_target="tpu_custom_call" | custom-call | flops 21474836480 | bytes 12582912 | tf_op jit(solution)/shard_map/attend_back/pallas_call | solution.py:586
  189.2 4.6 %collective-permute-start.13 = (bf16[112,1024]{1,0:T(8,128)(2,1)}, bf16[112,1024]{1,0:T(8,128)(2,1)S(1)}, u32[]{:S(2)}, u32[]{:S(2)}) collective-permute-start(bf16[112,1024]{1,0:T(8,128)(2,1)} %get-tuple-element.128), channel_id=1, source_target_pairs={{0,4},{4,8},{8,12},{12,16},{16,20},{20,24},{24,28},{1,5},{5,9},{9,... | collective-permute-start | bytes 688136 | tf_op jit(solution)/shard_map/ppermute | solution.py:817
  197.3 5.9 %collective-permute-done.13.refs_6_ = bf16[112,1024]{1,0:T(8,128)(2,1)S(1)} collective-permute-done((bf16[112,1024]{1,0:T(8,128)(2,1)}, bf16[112,1024]{1,0:T(8,128)(2,1)S(1)}, u32[]{:S(2)}, u32[]{:S(2)}) %collective-permute-start.13) | collective-permute-done | bytes 229408 | tf_op jit(solution)/shard_map/ppermute | solution.py:817
  211.8 4.4 %collective-permute-done.15 = bf16[8,1024]{1,0:T(8,128)(2,1)S(1)} collective-permute-done((bf16[8,1024]{1,0:T(8,128)(2,1)S(1)}, bf16[8,1024]{1,0:T(8,128)(2,1)S(1)}, u32[]{:S(2)}, u32[]{:S(2)}) %collective-permute-start.15) | collective-permute-done | bytes 16416 | tf_op jit(solution)/shard_map/ppermute | solution.py:821
  216.8 10.4 %input_grad.1 = f32[1024,512]{1,0:T(8,128)} custom-call(bf16[1024,512]{1,0:T(8,128)(2,1)} %bitcast.159, bf16[1024,256]{1,0:T(8,128)(2,1)} %get-tuple-element.110.refs_0_, bf16[1024,256]{1,0:T(8,128)(2,1)} %get-tuple-element.122.refs_1_, f32[1024,512]{1,0:T(8,128)} %get-tuple-element.123.refs_2_, f32[1024,512]{1,0:T(8,128)} %get-tuple-element.124.refs_3_, ...), custom_call_target="tpu_custom_call" | custom-call | flops 8589934592 | bytes 14680064 | tf_op jit(solution)/shard_map/input_grad/pallas_call | solution.py:797
  230.9 5.2 %collective-permute-done.28 = bf16[304,512]{1,0:T(8,128)(2,1)S(1)} collective-permute-done((bf16[304,512]{1,0:T(8,128)(2,1)S(1)}, bf16[304,512]{1,0:T(8,128)(2,1)S(1)}, u32[]{:S(2)}, u32[]{:S(2)}) %collective-permute-start.28) | collective-permute-done | bytes 311328 | tf_op jit(solution)/shard_map/ppermute | solution.py:821
  238.4 4.8 %collective-permute-done.17 = bf16[1,224,512]{2,1,0:T(8,128)(2,1)S(1)} collective-permute-done((bf16[1,224,512]{2,1,0:T(8,128)(2,1)S(1)}, bf16[1,224,512]{2,1,0:T(8,128)(2,1)S(1)}, u32[]{:S(2)}, u32[]{:S(2)}) %collective-permute-start.17) | collective-permute-done | bytes 229408 | tf_op jit(solution)/shard_map/ppermute | solution.py:821
  244.5 3.7 %collective-permute-done.18 = bf16[1,112,512]{2,1,0:T(8,128)(2,1)S(1)} collective-permute-done((bf16[1,112,512]{2,1,0:T(8,128)(2,1)S(1)}, bf16[1,112,512]{2,1,0:T(8,128)(2,1)S(1)}, u32[]{:S(2)}, u32[]{:S(2)}) %collective-permute-start.18) | collective-permute-done | bytes 114720 | tf_op jit(solution)/shard_map/ppermute | solution.py:821
  249.3 3.8 %collective-permute-done.21 = bf16[112,512]{1,0:T(8,128)(2,1)S(1)} collective-permute-done((bf16[112,512]{1,0:T(8,128)(2,1)S(1)}, bf16[112,512]{1,0:T(8,128)(2,1)S(1)}, u32[]{:S(2)}, u32[]{:S(2)}) %collective-permute-start.21) | collective-permute-done | bytes 114720 | tf_op jit(solution)/shard_map/ppermute | solution.py:821
  253.3 8.0 %collective-permute-done.29 = bf16[152,512]{1,0:T(8,128)(2,1)S(1)} collective-permute-done((bf16[152,512]{1,0:T(8,128)(2,1)S(1)}, bf16[152,512]{1,0:T(8,128)(2,1)S(1)}, u32[]{:S(2)}, u32[]{:S(2)}) %collective-permute-start.29) | collective-permute-done | bytes 155680 | tf_op jit(solution)/shard_map/ppermute | solution.py:821
  264.5 3.7 %collective-permute-done.30 = bf16[152,512]{1,0:T(8,128)(2,1)S(1)} collective-permute-done((bf16[152,512]{1,0:T(8,128)(2,1)S(1)}, bf16[152,512]{1,0:T(8,128)(2,1)S(1)}, u32[]{:S(2)}, u32[]{:S(2)}) %collective-permute-start.30) | collective-permute-done | bytes 155680 | tf_op jit(solution)/shard_map/ppermute | solution.py:821
  278.4 4.0 %collective-permute-done.25 = bf16[2,1,112,512]{3,2,1,0:T(8,128)(2,1)S(1)} collective-permute-done((bf16[2,1,112,512]{3,2,1,0:T(8,128)(2,1)S(1)}, bf16[2,1,112,512]{3,2,1,0:T(8,128)(2,1)S(1)}, u32[]{:S(2)}, u32[]{:S(2)}) %collective-permute-start.25) | collective-permute-done | bytes 229408 | tf_op jit(solution)/shard_map/ppermute | solution.py:821
  283.6 7.1 %collective-permute-done.32 = bf16[2,1,304,512]{3,2,1,0:T(8,128)(2,1)S(1)} collective-permute-done((bf16[2,1,304,512]{3,2,1,0:T(8,128)(2,1)S(1)}, bf16[2,1,304,512]{3,2,1,0:T(8,128)(2,1)S(1)}, u32[]{:S(2)}, u32[]{:S(2)}) %collective-permute-start.32) | collective-permute-done | bytes 622624 | tf_op jit(solution)/shard_map/ppermute | solution.py:821
  (140 shorter events, 67.8 us)
Async XLA Ops:
  7.2 90.0 %all-gather.4.cloned.1.call-start = ((), (), s32[]{:S(2)}) async-start(), calls=%async_computation | async-start | bytes 2621440 | tf_op jit(solution)/shard_map/all_gather | solution.py:947
  9.1 13.3 %collective-permute-start.1 = (bf16[144,1536]{1,0:T(8,128)(2,1)}, bf16[144,1536]{1,0:T(8,128)(2,1)S(1)}, u32[]{:S(2)}, u32[]{:S(2)}) collective-permute-start(bf16[144,1536]{1,0:T(8,128)(2,1)} %pack.1.refs_0_), channel_id=1, source_target_pairs={{0,2},{1,3},{2,0},{3,1},{4,6},{5,7},{6,4},{7,5},{8,10},{9,11},{10,... | collective-permute-start | bytes 1327112 | tf_op jit(solution)/shard_map/ppermute | solution.py:821
  12.1 12.5 %collective-permute-start = (bf16[144,1536]{1,0:T(8,128)(2,1)}, bf16[144,1536]{1,0:T(8,128)(2,1)S(1)}, u32[]{:S(2)}, u32[]{:S(2)}) collective-permute-start(bf16[144,1536]{1,0:T(8,128)(2,1)} %pack.1.refs_0_), channel_id=1, source_target_pairs={{0,1},{1,0},{2,3},{3,2},{4,5},{5,4},{6,7},{7,6},{8,9},{9,8},{10,11... | collective-permute-start | bytes 1327112 | tf_op jit(solution)/shard_map/ppermute | solution.py:821
  24.6 72.6 %all-gather.6.cloned.1.call-start = ((), (), s32[]{:S(2)}) async-start(), calls=%async_computation.1 | async-start | bytes 3276800 | tf_op jit(solution)/shard_map/all_gather | solution.py:946
  38.6 17.4 %collective-permute-start.4 = (bf16[112,1536]{1,0:T(8,128)(2,1)}, bf16[112,1536]{1,0:T(8,128)(2,1)S(1)}, u32[]{:S(2)}, u32[]{:S(2)}) collective-permute-start(bf16[112,1536]{1,0:T(8,128)(2,1)} %get-tuple-element.87), channel_id=1, source_target_pairs={{0,4},{4,8},{8,12},{12,16},{16,20},{20,24},{24,28},{1,5},{5,9},{9,... | collective-permute-start | bytes 1032200 | tf_op jit(solution)/shard_map/ppermute | solution.py:817
  40.8 15.2 %collective-permute-start.5 = (bf16[112,1536]{1,0:T(8,128)(2,1)}, bf16[112,1536]{1,0:T(8,128)(2,1)S(1)}, u32[]{:S(2)}, u32[]{:S(2)}) collective-permute-start(bf16[112,1536]{1,0:T(8,128)(2,1)} %get-tuple-element.88), channel_id=1, source_target_pairs={{4,0},{8,4},{12,8},{16,12},{20,16},{24,20},{28,24},{5,1},{9,5},{13... | collective-permute-start | bytes 1032200 | tf_op jit(solution)/shard_map/ppermute | solution.py:817
  56.0 7.5 %collective-permute-start.6 = (bf16[32,1536]{1,0:T(8,128)(2,1)S(1)}, bf16[32,1536]{1,0:T(8,128)(2,1)S(1)}, u32[]{:S(2)}, u32[]{:S(2)}) collective-permute-start(bf16[32,1536]{1,0:T(8,128)(2,1)S(1)} %pad_maximum_fusion.13), channel_id=1, source_target_pairs={{0,8},{4,12},{8,0},{12,4},{16,24},{20,28},{24,16},{28,20},{1,9},{5... | collective-permute-start | bytes 294920 | tf_op jit(solution)/shard_map/ppermute | solution.py:821
  63.6 11.6 %collective-permute-start.7 = (bf16[64,1536]{1,0:T(8,128)(2,1)S(1)}, bf16[64,1536]{1,0:T(8,128)(2,1)S(1)}, u32[]{:S(2)}, u32[]{:S(2)}) collective-permute-start(bf16[64,1536]{1,0:T(8,128)(2,1)S(1)} %pad_maximum_fusion.11), channel_id=1, source_target_pairs={{0,16},{4,20},{8,24},{12,28},{16,0},{20,4},{24,8},{28,12},{1,17},{... | collective-permute-start | bytes 589832 | tf_op jit(solution)/shard_map/ppermute | solution.py:821
  138.9 24.3 %collective-permute-start.9 = (bf16[1,608,512]{2,1,0:T(8,128)(2,1)S(1)}, bf16[1,608,512]{2,1,0:T(8,128)(2,1)S(1)}, u32[]{:S(2)}, u32[]{:S(2)}) collective-permute-start(bf16[1,608,512]{2,1,0:T(8,128)(2,1)S(1)} %constant_dynamic-slice_fusion.3), channel_id=1, source_target_pairs={{0,2},{1,3},{2,0},{3,1},{4,6},{5,7},{6,4},{7,5},{8,10},{9,11},{10,... | collective-permute-start | bytes 1867784 | tf_op jit(solution)/shard_map/ppermute | solution.py:821
  140.5 22.8 %collective-permute-start.10 = (bf16[2,304,512]{2,1,0:T(8,128)(2,1)S(1)}, bf16[2,304,512]{2,1,0:T(8,128)(2,1)S(1)}, u32[]{:S(2)}, u32[]{:S(2)}) collective-permute-start(bf16[2,304,512]{2,1,0:T(8,128)(2,1)S(1)} %dynamic-slice_bitcast_fusion.2), channel_id=1, source_target_pairs={{0,4},{4,0},{8,12},{12,8},{16,20},{20,16},{24,28},{28,24},{1,5},{5... | collective-permute-start | bytes 1867784 | tf_op jit(solution)/shard_map/ppermute | solution.py:821
  187.9 9.5 %collective-permute-start.12 = (bf16[112,1024]{1,0:T(8,128)(2,1)}, bf16[112,1024]{1,0:T(8,128)(2,1)S(1)}, u32[]{:S(2)}, u32[]{:S(2)}) collective-permute-start(bf16[112,1024]{1,0:T(8,128)(2,1)} %get-tuple-element.127), channel_id=1, source_target_pairs={{4,0},{8,4},{12,8},{16,12},{20,16},{24,20},{28,24},{5,1},{9,5},{13... | collective-permute-start | bytes 688136 | tf_op jit(solution)/shard_map/ppermute | solution.py:817
  189.2 14.1 %collective-permute-start.13 = (bf16[112,1024]{1,0:T(8,128)(2,1)}, bf16[112,1024]{1,0:T(8,128)(2,1)S(1)}, u32[]{:S(2)}, u32[]{:S(2)}) collective-permute-start(bf16[112,1024]{1,0:T(8,128)(2,1)} %get-tuple-element.128), channel_id=1, source_target_pairs={{0,4},{4,8},{8,12},{12,16},{16,20},{20,24},{24,28},{1,5},{5,9},{9,... | collective-permute-start | bytes 688136 | tf_op jit(solution)/shard_map/ppermute | solution.py:817
  193.8 33.4 %collective-permute-start.27 = (bf16[1,304,512]{2,1,0:T(8,128)(2,1)S(1)}, bf16[1,304,512]{2,1,0:T(8,128)(2,1)S(1)}, u32[]{:S(2)}, u32[]{:S(2)}) collective-permute-start(bf16[1,304,512]{2,1,0:T(8,128)(2,1)S(1)} %constant_dynamic-slice_fusion), channel_id=1, source_target_pairs={{0,2},{1,3},{2,0},{3,1},{4,6},{5,7},{6,4},{7,5},{8,10},{9,11},{10,... | collective-permute-start | bytes 933896 | tf_op jit(solution)/shard_map/ppermute | solution.py:821
  206.1 21.2 %collective-permute-start.26 = (bf16[1,304,512]{2,1,0:T(8,128)(2,1)S(1)}, bf16[1,304,512]{2,1,0:T(8,128)(2,1)S(1)}, u32[]{:S(2)}, u32[]{:S(2)}) collective-permute-start(bf16[1,304,512]{2,1,0:T(8,128)(2,1)S(1)} %dynamic-slice_bitcast_fusion.4), channel_id=1, source_target_pairs={{0,4},{4,0},{8,12},{12,8},{16,20},{20,16},{24,28},{28,24},{1,5},{5... | collective-permute-start | bytes 933896 | tf_op jit(solution)/shard_map/ppermute | solution.py:821
  208.6 7.6 %collective-permute-start.15 = (bf16[8,1024]{1,0:T(8,128)(2,1)S(1)}, bf16[8,1024]{1,0:T(8,128)(2,1)S(1)}, u32[]{:S(2)}, u32[]{:S(2)}) collective-permute-start(bf16[8,1024]{1,0:T(8,128)(2,1)S(1)} %dynamic-slice_bitcast_fusion.12), channel_id=1, source_target_pairs={{0,4},{4,0},{8,12},{12,8},{16,20},{20,16},{24,28},{28,24},{1,5},{5... | collective-permute-start | bytes 49160 | tf_op jit(solution)/shard_map/ppermute | solution.py:821
  211.7 16.2 %collective-permute-start.16 = (bf16[2,448,512]{2,1,0:T(8,128)(2,1)S(1)}, bf16[2,448,512]{2,1,0:T(8,128)(2,1)S(1)}, u32[]{:S(2)}, u32[]{:S(2)}) collective-permute-start(bf16[2,448,512]{2,1,0:T(8,128)(2,1)S(1)} %dynamic-slice_bitcast_fusion.1), channel_id=1, source_target_pairs={{0,1},{1,0},{2,3},{3,2},{4,5},{5,4},{6,7},{7,6},{8,9},{9,8},{10,11... | collective-permute-start | bytes 2752520 | tf_op jit(solution)/shard_map/ppermute | solution.py:821
  227.5 8.5 %collective-permute-start.28 = (bf16[304,512]{1,0:T(8,128)(2,1)S(1)}, bf16[304,512]{1,0:T(8,128)(2,1)S(1)}, u32[]{:S(2)}, u32[]{:S(2)}) collective-permute-start(bf16[304,512]{1,0:T(8,128)(2,1)S(1)} %dynamic-slice_bitcast_fusion.3), channel_id=1, source_target_pairs={{0,8},{4,12},{8,0},{12,4},{16,24},{20,28},{24,16},{28,20},{1,9},{5... | collective-permute-start | bytes 933896 | tf_op jit(solution)/shard_map/ppermute | solution.py:821
  229.1 7.7 %collective-permute-start.19 = (bf16[2,112,512]{2,1,0:T(8,128)(2,1)S(1)}, bf16[2,112,512]{2,1,0:T(8,128)(2,1)S(1)}, u32[]{:S(2)}, u32[]{:S(2)}) collective-permute-start(bf16[2,112,512]{2,1,0:T(8,128)(2,1)S(1)} %dynamic-slice_bitcast_fusion.5), channel_id=1, source_target_pairs={{0,4},{4,0},{8,12},{12,8},{16,20},{20,16},{24,28},{28,24},{1,5},{5... | collective-permute-start | bytes 688136 | tf_op jit(solution)/shard_map/ppermute | solution.py:821
  236.8 7.6 %collective-permute-start.20 = (bf16[1,112,512]{2,1,0:T(8,128)(2,1)S(1)}, bf16[1,112,512]{2,1,0:T(8,128)(2,1)S(1)}, u32[]{:S(2)}, u32[]{:S(2)}) collective-permute-start(bf16[1,112,512]{2,1,0:T(8,128)(2,1)S(1)} %constant_dynamic-slice_fusion.1), channel_id=1, source_target_pairs={{0,2},{1,3},{2,0},{3,1},{4,6},{5,7},{6,4},{7,5},{8,10},{9,11},{10,... | collective-permute-start | bytes 344072 | tf_op jit(solution)/shard_map/ppermute | solution.py:821
  249.3 12.1 %collective-permute-start.29 = (bf16[152,512]{1,0:T(8,128)(2,1)S(1)}, bf16[152,512]{1,0:T(8,128)(2,1)S(1)}, u32[]{:S(2)}, u32[]{:S(2)}) collective-permute-start(bf16[152,512]{1,0:T(8,128)(2,1)S(1)} %dynamic-slice_bitcast_fusion.6), channel_id=1, source_target_pairs={{0,16},{4,20},{8,24},{12,28},{16,0},{20,4},{24,8},{28,12},{1,17},{... | collective-permute-start | bytes 466952 | tf_op jit(solution)/shard_map/ppermute | solution.py:821
  253.3 9.3 %collective-permute-start.22 = (bf16[56,512]{1,0:T(8,128)(2,1)S(1)}, bf16[56,512]{1,0:T(8,128)(2,1)S(1)}, u32[]{:S(2)}, u32[]{:S(2)}) collective-permute-start(bf16[56,512]{1,0:T(8,128)(2,1)S(1)} %dynamic-slice_bitcast_fusion.10), channel_id=1, source_target_pairs={{0,16},{4,20},{8,24},{12,28},{16,0},{20,4},{24,8},{28,12},{1,17},{... | collective-permute-start | bytes 172040 | tf_op jit(solution)/shard_map/ppermute | solution.py:821
  269.0 8.1 %collective-permute-start.31 = (bf16[304,512]{1,0:T(8,128)(2,1)S(1)}, bf16[304,512]{1,0:T(8,128)(2,1)S(1)}, u32[]{:S(2)}, u32[]{:S(2)}) collective-permute-start(bf16[304,512]{1,0:T(8,128)(2,1)S(1)} %pad_maximum_fusion.8), channel_id=1, source_target_pairs={{0,8},{4,12},{8,0},{12,4},{16,24},{20,28},{24,16},{28,20},{1,9},{5... | collective-permute-start | bytes 933896 | tf_op jit(solution)/shard_map/ppermute | solution.py:821
  273.8 8.6 %collective-permute-start.25 = (bf16[2,1,112,512]{3,2,1,0:T(8,128)(2,1)S(1)}, bf16[2,1,112,512]{3,2,1,0:T(8,128)(2,1)S(1)}, u32[]{:S(2)}, u32[]{:S(2)}) collective-permute-start(bf16[2,1,112,512]{3,2,1,0:T(8,128)(2,1)S(1)} %bitcast.142), channel_id=1, source_target_pairs={{0,4},{4,0},{8,12},{12,8},{16,20},{20,16},{24,28},{28,24},{1,5},{5... | collective-permute-start | bytes 688136 | tf_op jit(solution)/shard_map/ppermute | solution.py:821
  277.2 13.5 %collective-permute-start.32 = (bf16[2,1,304,512]{3,2,1,0:T(8,128)(2,1)S(1)}, bf16[2,1,304,512]{3,2,1,0:T(8,128)(2,1)S(1)}, u32[]{:S(2)}, u32[]{:S(2)}) collective-permute-start(bf16[2,1,304,512]{3,2,1,0:T(8,128)(2,1)S(1)} %bitcast.132), channel_id=1, source_target_pairs={{0,4},{4,0},{8,12},{12,8},{16,20},{20,16},{24,28},{28,24},{1,5},{5... | collective-permute-start | bytes 1867784 | tf_op jit(solution)/shard_map/ppermute | solution.py:821
  (19 other events, 131.2 us)
Sparse Core Ops, SparseCore 0:
  24.8 24.0 all-gather.3
  51.0 25.5 all-gather.5

commit v3 on v2

--- a/solution.py
+++ b/solution.py
@@ -66,21 +66,16 @@
     return sources
 
 
-def count_starts(positions, starts):
-    total = jnp.full(positions.shape, -1, jnp.int32)
-    for start in starts:
-        total = total + (start <= positions).astype(jnp.int32)
-    return total
-
-
 def mask_kernel(rows, total, far, here_ref, lengths_ref, bias_ref):
-    starts, start = [], jnp.int32(0)
-    for at in range(lengths_ref.shape[1]):
-        starts.append(start)
-        start = start + lengths_ref[0, at]
     base = here_ref[0] * rows + pl.program_id(0) * CHUNK
     query = base + lax.broadcasted_iota(jnp.int32, (1, CHUNK), 1)
-    query_doc = count_starts(query, starts)
+    first_token = jnp.zeros((1, CHUNK), jnp.int32)
+    end_token = jnp.full((1, CHUNK), total, jnp.int32)
+    start = jnp.int32(0)
+    for at in range(lengths_ref.shape[1]):
+        first_token = jnp.where(start <= query, start, first_token)
+        start = start + lengths_ref[0, at]
+        end_token = jnp.where(start > query, jnp.minimum(end_token, start), end_token)
 
     def part(at, count, first_row, level):
         span = 2**level
@@ -91,10 +86,7 @@
             seen = gap <= 1
         else:
             seen = (gap == 1) & (jnp.abs((first >> (shift - 1)) - (query >> (shift - 1))) > 1)
-        doc = count_starts(first, starts)
-        seen = seen & (first >= 0) & (first < total) & (doc == query_doc)
-        if level:
-            seen = seen & (count_starts(first + (span - 1), starts) == doc)
+        seen = seen & (first >= first_token) & (first + (span - 1) < end_token)
         bias_ref[0, at : at + count, :] = jnp.where(seen, level * math.log(2.0), MASKED)
 
     at = 0
@@ -205,16 +197,39 @@
     )(weight, *vectors)
 
 
+def pack_rest_kernel(down_ref, up_ref, out_w_ref, one_ref, two_ref):
+    rows = up_ref.shape[0]
+    blocks = up_ref.shape[1] // WIDTH
+    for block in range(blocks - 1):
+        one_ref[block * rows : (block + 1) * rows, :] = up_ref[:, block * WIDTH : (block + 1) * WIDTH]
+    two_ref[0:rows, :] = up_ref[:, (blocks - 1) * WIDTH :]
+    two_ref[rows : 2 * rows, :] = out_w_ref[...]
+    two_ref[2 * rows :, :] = down_ref[...]
+
+
+def pack_rest_call(down, up, out_w):
+    rows, blocks = up.shape[0], up.shape[1] // WIDTH
+    return pl.pallas_call(
+        pack_rest_kernel,
+        out_shape=[
+            jax.ShapeDtypeStruct(((blocks - 1) * rows, WIDTH), bf16),
+            jax.ShapeDtypeStruct((2 * rows + down.shape[0], WIDTH), bf16),
+        ],
+        in_specs=vmem_specs(3),
+        out_specs=vmem_specs(2),
+        name="pack_rest",
+    )(down, up, out_w)
+
+
 def vmem_specs(count):
     return [pl.BlockSpec(memory_space=pltpu.VMEM)] * count
 
 
 def qkv_kernel(rows, owners, meta_ref, x_ref, *refs):
-    shard_refs, refs = refs[:owners], refs[owners:]
+    shard_refs, refs = refs[:owners], refs[owners + 1 :]
     w_ref, vec_ref, up_bias_ref, q_ref = refs[:4]
     kv_refs, scaled_refs = refs[4 : 4 + LOCAL], refs[4 + LOCAL : 4 + 2 * LOCAL]
-    tail_ref, head_ref = refs[4 + 2 * LOCAL : 6 + 2 * LOCAL]
-    keep_ref = refs[6 + 2 * LOCAL]
+    tail_ref, head_ref, top_ref, keep_ref = refs[4 + 2 * LOCAL :]
     part = WIDTH // owners
     step = pl.program_id(0)
 
@@ -267,9 +282,10 @@
             scaled_refs[level][...] = current[:, 2 * WIDTH :]
             tail_ref[BLOCK * level : BLOCK * (level + 1), :] = current[current.shape[0] - BLOCK :]
             head_ref[BLOCK * level : BLOCK * (level + 1), :] = current[:BLOCK]
-
-
-def qkv_call(rows, hidden_width, meta, x, pieces):
+        top_ref[...] = current
+
+
+def qkv_call(rows, hidden_width, meta, x, pieces, earlier):
     owners = len(pieces)
     tile = 256
 
@@ -297,16 +313,17 @@
         ]
         + kv_shapes
         + scaled_shapes
-        + [edge, edge],
-        in_specs=[pl.BlockSpec(memory_space=pltpu.SMEM), tiled(tile, WIDTH)] + vmem_specs(owners),
-        out_specs=vmem_specs(3) + [tiled(tile, WIDTH)] + kv_specs + scaled_specs + vmem_specs(2),
+        + [edge, edge, jax.ShapeDtypeStruct((BLOCK, ENTRY), bf16)],
+        in_specs=[pl.BlockSpec(memory_space=pltpu.SMEM), tiled(tile, WIDTH)]
+        + vmem_specs(owners)
+        + [pl.BlockSpec(memory_space=pl.ANY)],
+        out_specs=vmem_specs(3) + [tiled(tile, WIDTH)] + kv_specs + scaled_specs + vmem_specs(3),
         scratch_shapes=[pltpu.VMEM((level_rows(rows, 4), ENTRY), bf16)],
         compiler_params=pltpu.CompilerParams(vmem_limit_bytes=VMEM_LIMIT),
         cost_estimate=pl.CostEstimate(flops=9 << 30, bytes_accessed=12 << 20, transcendentals=0),
         name="qkv_levels",
-    )(meta, x, *pieces)
-    weight, vectors, up_bias, queries = outs[:4]
-    return weight, vectors, up_bias, queries, outs[4 : 4 + LOCAL], outs[4 + LOCAL : 4 + 2 * LOCAL], outs[-2], outs[-1]
+    )(meta, x, *pieces, earlier)
+    return outs
 
 
 def far_level(entries):
@@ -425,27 +442,30 @@
     return [high, (values - high.astype(f32)).astype(bf16)]
 
 
-def attend_back_kernel(rows, far, first, count_pairs, combine, *refs):
+def choose(flag, zero, one):
+    return jnp.where(flag == 0, zero, one), jnp.where(flag == 0, one, zero)
+
+
+def choose_groups(flag, folded):
+    groups = folded.reshape(-1, 2, 8, folded.shape[1])
+    return [part.reshape(-1, folded.shape[1]) for part in choose(flag, groups[:, 0], groups[:, 1])]
+
+
+def attend_back_kernel(rows, far, *refs):
     refs = list(refs)
     take = lambda count: [refs.pop(0) for _ in range(count)]
     meta_ref, q_ref, grad_ref, bias_ref, log_ref = take(5)
     level_refs, scaled_refs = take(LOCAL), take(LOCAL)
     left_ref, right_ref, base_ref, w_ref, vec_ref = take(5)
-    if combine:
-        before_left, before_right, before_far, before_weights, before_vec = take(5)
-    dq_ref, local_ref, to_left_ref, to_right_ref, to_far_ref, weights_ref = take(6)
-    vec_grad_ref = None if combine else take(1)[0]
+    dq_ref, local_ref, to_left_ref, to_right_ref, far_keep_ref, far_send_ref, keep_ref, send_ref = take(8)
     ext_ref, far_ref, slots_ref, acc_ref, tree_ref, scaled_ref, dq_keep_ref = take(7)
     chunk = pl.program_id(0)
     offsets, entries = extended_offsets(rows, far)
-    half = 128 * count_pairs
-    lane = 128 * first
 
     @pl.when(chunk == 0)
     def _():
-        columns = [(lane, lane, 0, half), (WIDTH + lane, WIDTH + lane, half, half)]
         common = (left_ref, right_ref, base_ref)
-        assemble(rows, far, meta_ref[0], columns, level_refs, *common, ext_ref, far_ref)
+        assemble(rows, far, meta_ref[0], [(0, 0, 0, 2 * WIDTH)], level_refs, *common, ext_ref, far_ref)
         assemble(rows, far, meta_ref[0], [(0, 2 * WIDTH, 0, WIDTH)], scaled_refs, *common, scaled_ref, far_ref)
         acc_ref[...] = jnp.zeros_like(acc_ref)
 
@@ -453,13 +473,12 @@
     bias = bias_ref[0]
     bias = jnp.concatenate([bias, bias], axis=1)
     sources = slot_sources(rows, far, chunk)
-    for pair in range(count_pairs):
+    for pair in range(PAIRS):
         lanes = slice(128 * pair, 128 * (pair + 1))
-        value_lanes = slice(half + 128 * pair, half + 128 * (pair + 1))
+        value_lanes = slice(WIDTH + 128 * pair, WIDTH + 128 * (pair + 1))
         keys, values = slots_ref[:, lanes], slots_ref[:, value_lanes]
         queries, grads = split_heads(q_ref[:, lanes]), split_heads(grad_ref[:, lanes])
-        logs = log_ref[0, first + pair : first + pair + 1, :]
-        probs = jnp.exp(dot_nt(keys, queries) + bias - logs)
+        probs = jnp.exp(dot_nt(keys, queries) + bias - log_ref[0, pair : pair + 1, :])
         grad_probs = dot_nt(values, grads)
         delta = jnp.sum(probs * grad_probs, axis=0, keepdims=True)
         grad_scores = (probs * (grad_probs - delta)).astype(bf16)
@@ -479,77 +498,53 @@
     @pl.when(chunk == pl.num_programs(0) - 1)
     def _():
         dq = dq_keep_ref[...]
-        sums = [column_sum(dq.astype(f32)), column_sum(acc_ref[:, :half]), column_sum(acc_ref[:, half:])]
-        parts = [
-            dot_tn(scaled_refs[0][...], dq),
-            dot_tn(scaled_ref[...], acc_ref[:, :half].astype(bf16)),
-            dot_tn(scaled_ref[...], acc_ref[:, half:].astype(bf16)),
-        ]
+        sums = [column_sum(dq.astype(f32)), column_sum(acc_ref[:, :WIDTH]), column_sum(acc_ref[:, WIDTH:])]
+        both = dot_tn(scaled_ref[...], acc_ref[...].astype(bf16))
+        parts = [dot_tn(scaled_refs[0][...], dq), both[:, :WIDTH], both[:, WIDTH:]]
         first_row = lax.broadcasted_iota(jnp.int32, (16, 1), 0) == 0
-        ones = jnp.where(first_row, jnp.ones((16, half), f32), 0.0).astype(bf16)
+        ones = jnp.where(first_row, jnp.ones((16, WIDTH), f32), 0.0).astype(bf16)
         as_column = lambda row: dot_tn(jnp.where(first_row, row, 0.0).astype(bf16), ones)
         gain, shift = as_column(vec_ref[0:1, :]), as_column(vec_ref[1:2, :])
         gain_grad, shift_grad = jnp.zeros((1, WIDTH), f32), jnp.zeros((1, WIDTH), f32)
-        owners = weights_ref.shape[0]
+        owners = 2 * keep_ref.shape[0]
         part = WIDTH // owners
+        low_bit = meta_ref[1] & 1
         for block in range(3):
-            weight = w_ref[:, block * WIDTH + lane : block * WIDTH + lane + half]
-            wide = weight.astype(f32)
-            gain_grad += matrix_row(jnp.ones((16, half), bf16), wide * parts[block])
-            shift_grad += matrix_row(jnp.broadcast_to(sums[block], (16, half)), weight)
-            grad = (gain * parts[block] + shift * sums[block]).astype(bf16)
-            for owner in range(owners):
-                weights_ref[owner, block * part : (block + 1) * part, lane * combine : lane * combine + half] = grad[
-                    owner * part : (owner + 1) * part
-                ]
-        if combine:
-            for owner in range(owners):
-                weights_ref[owner, 0 : 3 * part, 0:lane] = before_weights[owner, 0 : 3 * part, :]
-            extend = lambda row, at: jnp.concatenate([before_vec[at : at + 1, 0:lane], row], axis=1)
-            rows_out = [
-                before_vec[0:1, :] + gain_grad,
-                before_vec[1:2, :] + shift_grad,
-                extend(sums[0], 2),
-                extend(sums[2], 3),
-            ]
-            extra = weights_ref.shape[1] - 3 * part
-            top_row = lax.broadcasted_iota(jnp.int32, (extra, 1), 0) == 0
-            for owner in range(owners):
-                row = jnp.concatenate([r[:, owner * part : (owner + 1) * part] for r in rows_out], axis=1)
-                weights_ref[owner, 3 * part :, :] = jnp.where(top_row, row, 0.0).astype(bf16)
-        else:
-            vec_grad_ref[...] = jnp.zeros_like(vec_grad_ref)
-            vec_grad_ref[0:1, :] = gain_grad
-            vec_grad_ref[1:2, :] = shift_grad
-            vec_grad_ref[2:3, 0:half] = sums[0]
-            vec_grad_ref[3:4, 0:half] = sums[2]
-
-        def put(target, values, before):
-            if combine:
-                target[:, 0:lane] = before[:, 0:lane]
-                target[:, WIDTH : WIDTH + lane] = before[:, lane:]
-                target[:, lane : lane + half] = values[:, :half].astype(bf16)
-                target[:, WIDTH + lane : WIDTH + lane + half] = values[:, half:].astype(bf16)
-            else:
-                target[...] = values.astype(bf16)
-
-        lefts, rights = [], []
+            weight = w_ref[:, block * WIDTH : (block + 1) * WIDTH]
+            gain_grad += matrix_row(jnp.ones((16, WIDTH), bf16), weight.astype(f32) * parts[block])
+            shift_grad += matrix_row(jnp.broadcast_to(sums[block], (16, WIDTH)), weight)
+            grad = gain * parts[block] + shift * sums[block]
+            for high in range(owners // 2):
+                at = 2 * high * part
+                mine, other = choose(low_bit, grad[at : at + part], grad[at + part : at + 2 * part])
+                keep_ref[high, block * part : (block + 1) * part, :] = mine.astype(bf16)
+                send_ref[high, block * part : (block + 1) * part, :] = other.astype(bf16)
+        extra = keep_ref.shape[1] - 3 * part
+        top_row = lax.broadcasted_iota(jnp.int32, (extra, 1), 0) == 0
+        vectors = [gain_grad, shift_grad, sums[0], sums[2]]
+        owner_row = lambda owner: jnp.concatenate([v[:, owner * part : (owner + 1) * part] for v in vectors], axis=1)
+        for high in range(owners // 2):
+            mine, other = choose(low_bit, owner_row(2 * high), owner_row(2 * high + 1))
+            keep_ref[high, 3 * part :, :] = jnp.where(top_row, mine, 0.0).astype(bf16)
+            send_ref[high, 3 * part :, :] = jnp.where(top_row, other, 0.0).astype(bf16)
+
         for level in range(LOCAL):
             at, count = offsets[level], level_rows(rows, level)
-            lefts.append(acc_ref[at : at + BLOCK, :])
-            rights.append(acc_ref[at + BLOCK + count : at + 2 * BLOCK + count, :])
-        put(to_left_ref, jnp.concatenate(lefts, axis=0), before_left if combine else None)
-        put(to_right_ref, jnp.concatenate(rights, axis=0), before_right if combine else None)
+            edge = slice(BLOCK * level, BLOCK * (level + 1))
+            to_left_ref[edge, :] = acc_ref[at : at + BLOCK, :].astype(bf16)
+            to_right_ref[edge, :] = acc_ref[at + BLOCK + count : at + 2 * BLOCK + count, :].astype(bf16)
         carry = None
         for index in range(len(far) - 1, -1, -1):
             level = far[index]
             count = base_ref.shape[0] // 2 ** (level - LOCAL + 1)
-            tree_ref[0:count, :] = jnp.zeros((count, 2 * half), f32) if carry is None else spread(carry)
+            tree_ref[0:count, :] = jnp.zeros((count, 2 * WIDTH), f32) if carry is None else spread(carry)
             for side, start in enumerate(far_starts(meta_ref[0], level, count)):
                 at = offsets[LOCAL + index] + side * BLOCK
                 tree_ref[pl.ds(start, BLOCK), :] += acc_ref[at : at + BLOCK, :]
             carry = tree_ref[0:count, :]
-        put(to_far_ref, carry, before_far if combine else None)
+        mine, other = choose_groups(meta_ref[0] & 1, jnp.concatenate([carry[:, :WIDTH], carry[:, WIDTH:]], axis=0))
+        far_keep_ref[...] = mine.astype(bf16)
+        far_send_ref[...] = other.astype(bf16)
         for level in range(LOCAL - 1, 0, -1):
             at, count = offsets[level] + BLOCK, level_rows(rows, level)
             below = offsets[level - 1] + BLOCK
@@ -564,51 +559,52 @@
                     acc_ref[target, :] = total
 
 
-def attend_back_call(rows, devices, far, owners, first, count_pairs, before, meta, q, grads, bias, logs, levels, scaled, left, right, base, weight, vectors):
+def chain_rows(rows, devices):
+    unit = 8 * devices
+    return -(-(rows + 16) // unit) * unit
+
+
+def attend_back_call(rows, devices, far, owners, meta, q, grads, bias, logs, levels, scaled, left, right, base, weight, vectors):
     chunks = rows // CHUNK
     _, entries = extended_offsets(rows, far)
     _, slots = slot_layout(far)
-    combine = before is not None
-    half = 128 * count_pairs
-    side = 2 * WIDTH if combine else 2 * half
-    part = WIDTH // owners
-    lanes = first // count_pairs
+    chain = (owners // 2, chain_rows(3 * WIDTH // owners, devices), WIDTH)
     outs = [
-        jax.ShapeDtypeStruct((rows, half), bf16),
-        jax.ShapeDtypeStruct((rows, 2 * half), f32),
-        jax.ShapeDtypeStruct((BLOCK * LOCAL, side), bf16),
-        jax.ShapeDtypeStruct((BLOCK * LOCAL, side), bf16),
-        jax.ShapeDtypeStruct((8 * devices, side), bf16),
-        jax.ShapeDtypeStruct((owners, 3 * part + 64, WIDTH) if combine else (owners, 3 * part, half), bf16),
+        jax.ShapeDtypeStruct((rows, WIDTH), bf16),
+        jax.ShapeDtypeStruct((rows, 2 * WIDTH), f32),
+        jax.ShapeDtypeStruct((BLOCK * LOCAL, 2 * WIDTH), bf16),
+        jax.ShapeDtypeStruct((BLOCK * LOCAL, 2 * WIDTH), bf16),
+        jax.ShapeDtypeStruct((8 * devices, WIDTH), bf16),
+        jax.ShapeDtypeStruct((8 * devices, WIDTH), bf16),
+        jax.ShapeDtypeStruct(chain, bf16),
+        jax.ShapeDtypeStruct(chain, bf16),
     ]
-    if not combine:
-        outs.append(jax.ShapeDtypeStruct((8, WIDTH), f32))
     return pl.pallas_call(
-        partial(attend_back_kernel, rows, far, first, count_pairs, combine),
+        partial(attend_back_kernel, rows, far),
         grid=(chunks,),
         out_shape=outs,
         in_specs=[
             pl.BlockSpec(memory_space=pltpu.SMEM),
-            pl.BlockSpec((CHUNK, half), lambda i: (i, lanes)),
-            pl.BlockSpec((CHUNK, half), lambda i: (i, lanes)),
+            pl.BlockSpec((CHUNK, WIDTH), lambda i: (i, 0)),
+            pl.BlockSpec((CHUNK, WIDTH), lambda i: (i, 0)),
             pl.BlockSpec((1, slots, CHUNK), lambda i: (i, 0, 0)),
             pl.BlockSpec((1, 8, 2 * CHUNK), lambda i: (i, 0, 0)),
         ]
-        + vmem_specs(2 * LOCAL + 5 + (5 if combine else 0)),
-        out_specs=[pl.BlockSpec((CHUNK, half), lambda i: (i, 0))] + vmem_specs(len(outs) - 1),
+        + vmem_specs(2 * LOCAL + 5),
+        out_specs=[pl.BlockSpec((CHUNK, WIDTH), lambda i: (i, 0))] + vmem_specs(len(outs) - 1),
         scratch_shapes=[
-            pltpu.VMEM((entries, 2 * half), bf16),
-            pltpu.VMEM((8 * devices, WIDTH), bf16),
-            pltpu.VMEM((slots, 2 * half), bf16),
-            pltpu.VMEM((entries, 2 * half), f32),
-            pltpu.VMEM((8 * devices, 2 * half), f32),
+            pltpu.VMEM((entries, 2 * WIDTH), bf16),
+            pltpu.VMEM((8 * devices, 2 * WIDTH), bf16),
+            pltpu.VMEM((slots, 2 * WIDTH), bf16),
+            pltpu.VMEM((entries, 2 * WIDTH), f32),
+            pltpu.VMEM((8 * devices, 2 * WIDTH), f32),
             pltpu.VMEM((entries, WIDTH), bf16),
-            pltpu.VMEM((rows, half), bf16),
+            pltpu.VMEM((rows, WIDTH), bf16),
         ],
         compiler_params=pltpu.CompilerParams(vmem_limit_bytes=VMEM_LIMIT),
-        cost_estimate=pl.CostEstimate(flops=(40 << 30) * count_pairs // PAIRS, bytes_accessed=12 << 20, transcendentals=4 << 20),
+        cost_estimate=pl.CostEstimate(flops=36 << 30, bytes_accessed=24 << 20, transcendentals=4 << 20),
         name="attend_back",
-    )(meta, q, grads, bias, logs, *levels, *scaled, left, right, base, weight, vectors, *(before or []))
+    )(meta, q, grads, bias, logs, *levels, *scaled, left, right, base, weight, vectors)
 
 
 def normal_parts(values):
@@ -625,33 +621,33 @@
 
 def feed_kernel(
     hidden_width,
+    owners,
+    meta_ref,
     x_ref,
     attended_ref,
     cot_ref,
-    rest_ref,
-    up_w_ref,
     vec_ref,
     up_bias_ref,
-    y_ref,
-    grad_middle_ref,
-    grad_attended_ref,
-    weights_ref,
-    out_w_ref,
-    vec_grad_ref,
-    up_bias_grad_ref,
-    down_acc,
-    up_acc,
-    out_acc,
+    *refs,
 ):
+    one_refs, two_refs, refs = refs[:owners], refs[owners : 2 * owners], refs[2 * owners :]
+    y_ref, grad_middle_ref, grad_attended_ref, keep_ref, send_ref = refs[:5]
+    down_w_ref, up_w_ref, out_w_ref, vec_grad_ref, up_bias_grad_ref, down_acc, up_acc, out_acc = refs[5:]
     step = pl.program_id(0)
-    owners = rest_ref.shape[0]
     rows = WIDTH // owners
     wide_rows = hidden_width // owners
+    blocks = hidden_width // WIDTH
 
     @pl.when(step == 0)
     def _():
-        for owner in range(owners):
-            out_w_ref[owner * rows : (owner + 1) * rows, :] = rest_ref[owner, wide_rows:, :]
+        for at, (one, two) in enumerate(zip(one_refs, two_refs)):
+            owner = meta_ref[1 + at]
+            span = pl.ds(pl.multiple_of(owner * rows, rows), rows)
+            for block in range(blocks - 1):
+                up_w_ref[span, block * WIDTH : (block + 1) * WIDTH] = one[block * rows : (block + 1) * rows, :]
+            up_w_ref[span, (blocks - 1) * WIDTH :] = two[0:rows, :]
+            out_w_ref[span, :] = two[rows : 2 * rows, :]
+            down_w_ref[pl.ds(pl.multiple_of(owner * wide_rows, wide_rows), wide_rows), :] = two[2 * rows :, :]
         down_acc[...] = jnp.zeros_like(down_acc)
         up_acc[...] = jnp.zeros_like(up_acc)
         out_acc[...] = jnp.zeros_like(out_acc)
@@ -667,9 +663,9 @@
     wide = cot.astype(f32)
     lowered = jnp.zeros_like(middle)
     grad_normed = jnp.zeros_like(middle)
-    for owner in range(owners):
-        columns = slice(owner * wide_rows, (owner + 1) * wide_rows)
-        down = rest_ref[owner, 0:wide_rows, :]
+    for block in range(blocks):
+        columns = slice(block * WIDTH, (block + 1) * WIDTH)
+        down = down_w_ref[columns, :]
         pre = dot_nn(normed, up_w_ref[:, columns]) + up_bias_ref[:, columns]
         phi, bell = normal_parts(pre)
         hidden = (pre * phi).astype(bf16)
@@ -692,40 +688,52 @@
 
     @pl.when(step == pl.num_programs(0) - 1)
     def _():
-        extra = weights_ref.shape[1] - 2 * wide_rows - rows
+        extra = keep_ref.shape[1] - wide_rows - (blocks + 1) * rows
         row_at = lax.broadcasted_iota(jnp.int32, (extra, 1), 0)
-        for owner in range(owners):
-            wide_span, span = slice(owner * wide_rows, (owner + 1) * wide_rows), slice(owner * rows, (owner + 1) * rows)
-            weights_ref[owner, 0:wide_rows, :] = down_acc[wide_span, :].astype(bf16)
+        low_bit = meta_ref[1] & 1
+
+        def put(high, at, count, source):
+            mine, other = choose(low_bit, source(2 * high), source(2 * high + 1))
+            keep_ref[high, at : at + count, :] = mine.astype(bf16)
+            send_ref[high, at : at + count, :] = other.astype(bf16)
+
+        def small(owner):
+            first = [vec_grad_ref[i : i + 1, owner * rows : (owner + 1) * rows] for i in range(4)]
+            second = up_bias_grad_ref[:, owner * wide_rows : (owner + 1) * wide_rows]
+            return jnp.where(row_at == 0, jnp.concatenate(first, axis=1), jnp.where(row_at == 1, second, 0.0))
+
+        for high in range(owners // 2):
+            put(high, 0, wide_rows, lambda owner: down_acc[owner * wide_rows : (owner + 1) * wide_rows, :])
             at = wide_rows
-            for block in range(hidden_width // WIDTH):
-                weights_ref[owner, at : at + rows, :] = up_acc[span, block * WIDTH : (block + 1) * WIDTH].astype(bf16)
+            for block in range(blocks):
+                columns = slice(block * WIDTH, (block + 1) * WIDTH)
+                put(high, at, rows, lambda owner: up_acc[owner * rows : (owner + 1) * rows, columns])
                 at += rows
-            weights_ref[owner, at : at + rows, :] = out_acc[span, :].astype(bf16)
-            first = jnp.concatenate([vec_grad_ref[i : i + 1, span] for i in range(4)], axis=1)
-            second = up_bias_grad_ref[:, wide_span]
-            weights_ref[owner, at + rows :, :] = jnp.where(
-                row_at == 0, first, jnp.where(row_at == 1, second, 0.0)
-            ).astype(bf16)
-
-
-def feed_call(owners, x, attended, cot, rest, up_w, vectors, up_bias):
-    rows, hidden_width = x.shape[0], up_w.shape[1]
+            put(high, at, rows, lambda owner: out_acc[owner * rows : (owner + 1) * rows, :])
+            put(high, at + rows, extra, small)
+
+
+def feed_call(hidden_width, devices, meta, x, attended, cot, vectors, up_bias, ones, twos):
+    rows, owners = x.shape[0], len(ones)
     tile = 256
     row_spec = pl.BlockSpec((tile, WIDTH), lambda i: (i, 0))
-    packed = 2 * (hidden_width // owners) + WIDTH // owners + 64
+    chain = chain_rows(2 * (hidden_width // owners) + WIDTH // owners, devices)
+    split = jax.ShapeDtypeStruct((owners // 2, chain, WIDTH), bf16)
     return pl.pallas_call(
-        partial(feed_kernel, hidden_width),
+        partial(feed_kernel, hidden_width, owners),
         grid=(rows // tile,),
         out_shape=[
             jax.ShapeDtypeStruct((rows, WIDTH), bf16),
             jax.ShapeDtypeStruct((rows, WIDTH), f32),
             jax.ShapeDtypeStruct((rows, WIDTH), bf16),
-            jax.ShapeDtypeStruct((owners, packed, WIDTH), bf16),
+            split,
+            split,
         ],
-        in_specs=[row_spec, row_spec, row_spec] + vmem_specs(4),
-        out_specs=[row_spec, row_spec, row_spec] + vmem_specs(1),
+        in_specs=[pl.BlockSpec(memory_space=pltpu.SMEM), row_spec, row_spec, row_spec] + vmem_specs(2 + 2 * owners),
+        out_specs=[row_spec, row_spec, row_spec] + vmem_specs(2),
         scratch_shapes=[
+            pltpu.VMEM((hidden_width, WIDTH), bf16),
+            pltpu.VMEM((WIDTH, hidden_width), bf16),
             pltpu.VMEM((WIDTH, WIDTH), bf16),
             pltpu.VMEM((8, WIDTH), f32),
             pltpu.VMEM((1, hidden_width), f32),
@@ -736,7 +744,7 @@
         compiler_params=pltpu.CompilerParams(vmem_limit_bytes=VMEM_LIMIT),
         cost_estimate=pl.CostEstimate(flops=32 << 30, bytes_accessed=20 << 20, transcendentals=4 << 20),
         name="feed_forward",
-    )(x, attended, cot, rest, up_w, vectors, up_bias)
+    )(meta, x, attended, cot, vectors, up_bias, *ones, *twos)
 
 
 def input_grad_kernel(
@@ -746,7 +754,8 @@
     grad_middle_ref,
     from_right_ref,
     from_left_ref,
-    base_ref,
+    far_keep_ref,
+    far_got_ref,
     w_ref,
     vec_ref,
     out_ref,
@@ -758,7 +767,8 @@
 
     @pl.when(step == 0)
     def _():
-        carry = spread(base_ref[...].astype(f32))
+        folded = far_keep_ref[...].astype(f32) + far_got_ref[...].astype(f32)
+        carry = spread(jnp.concatenate([folded[:8], folded[8:]], axis=1))
         for level in range(LOCAL - 1, -1, -1):
             count = level_rows(rows, level)
             edge = slice(BLOCK * level, BLOCK * (level + 1))
@@ -785,7 +795,7 @@
     out_ref[...] = grad_middle_ref[...] + norm_back(grad, scaled, inverse, vec_ref[0:1, :])
 
 
-def input_grad_call(x, dqs, locals_, grad_middle, from_right, from_left, base, weight, vectors):
+def input_grad_call(x, dqs, locals_, grad_middle, from_right, from_left, far_keep, far_got, weight, vectors):
     rows = x.shape[0]
     tile = 256
     count = len(dqs)
@@ -802,13 +812,13 @@
         + [tiled(d.shape[1]) for d in dqs]
         + [tiled(d.shape[1]) for d in locals_]
         + [tiled(WIDTH)]
-        + vmem_specs(5),
+        + vmem_specs(6),
         out_specs=tiled(WIDTH),
         scratch_shapes=[pltpu.VMEM((rows, 2 * WIDTH), f32)],
         compiler_params=pltpu.CompilerParams(vmem_limit_bytes=VMEM_LIMIT),
         cost_estimate=pl.CostEstimate(flops=8 << 30, bytes_accessed=14 << 20, transcendentals=0),
         name="input_grad",
-    )(x, *dqs, *locals_, grad_middle, from_right, from_left, base, weight, vectors)
+    )(x, *dqs, *locals_, grad_middle, from_right, from_left, far_keep, far_got, weight, vectors)
 
 
 def shifted(block, axis, distance):
@@ -821,23 +831,12 @@
     return lax.ppermute(block, axis, [(i, i ^ bit) for i in range(lax.axis_size(axis))])
 
 
-def add_low(left, right):
-    return (left.astype(f32) + right.astype(f32)).astype(bf16)
-
-
-def scatter_step(parts, axis, bit):
-    mine = (lax.axis_index(axis) // bit) % 2
-    keep = lax.dynamic_index_in_dim(parts, mine, 0, keepdims=False)
-    send = lax.dynamic_index_in_dim(parts, 1 - mine, 0, keepdims=False)
-    return add_low(keep, swap(send, axis, bit))
-
-
-def gather_step(part, axis, bit, rows_axis=0):
+def gather_step(part, axis, bit):
     mine = (lax.axis_index(axis) // bit) % 2
     other = swap(part, axis, bit)
     first = jnp.where(mine == 0, part, other)
     second = jnp.where(mine == 0, other, part)
-    return jnp.concatenate([first, second], axis=rows_axis)
+    return jnp.concatenate([first, second], axis=0)
 
 
 def together(*values):
@@ -849,61 +848,109 @@
     return [1 << at for at in range(size.bit_length() - 1)]
 
 
+def step_call(name, function, meta, arrays, shapes, dtype=bf16):
+    def kernel(meta_ref, *refs):
+        values = [ref[...].astype(f32) for ref in refs[: len(arrays)]]
+        for ref, value in zip(refs[len(arrays) :], function(meta_ref[0], meta_ref[1], *values), strict=True):
+            ref[...] = value.astype(dtype)
+
+    size = sum(math.prod(a.shape) for a in arrays)
+    return pl.pallas_call(
+        kernel,
+        out_shape=[jax.ShapeDtypeStruct(shape, dtype) for shape in shapes],
+        in_specs=[pl.BlockSpec(memory_space=pltpu.SMEM)] + vmem_specs(len(arrays)),
+        out_specs=vmem_specs(len(shapes)),
+        compiler_params=pltpu.CompilerParams(vmem_limit_bytes=VMEM_LIMIT),
+        cost_estimate=pl.CostEstimate(flops=1 << 20, bytes_accessed=4 * size, transcendentals=0),
+        name=name,
+    )(meta, *arrays)
+
+
+def halves(values, axis=0):
+    return jnp.split(values, 2, axis=axis)
+
+
 class Reduction:
-    def __init__(self, parts):
-        self.shape = parts.shape[1:]
-        self.value = parts
-        self.done = []
-        self.todo = [self.low, self.cross_one, self.cross_two]
-        self.todo += [partial(self.scatter, bit) for bit in bits_of("ctx")[1:]]
-        self.todo += [partial(self.gather, bit) for bit in reversed(bits_of("ctx")[1:])]
-        self.todo += [self.last]
-
-    def step(self, count=1):
-        for _ in range(count):
-            if self.todo:
-                self.todo.pop(0)()
-        return self
-
-    def after(self, *others):
-        tied = together(self.value, *others)
-        self.value = tied[0]
-        return tied[1:]
-
-    def low(self):
-        owners = self.value.shape[0]
-        self.value = scatter_step(self.value.reshape(owners // 2, 2, *self.shape).transpose(1, 0, 2, 3), "fsdp", 1)
-
-    def over_owners(self, current):
-        for bit in bits_of("fsdp")[1:]:
-            current = current.reshape(-1, 2, *current.shape[1:]).transpose(1, 0, 2, 3)
-            current = scatter_step(current, "fsdp", bit)
-        return current.reshape(current.shape[1:])
-
-    def over_ctx(self, current):
-        outer, rows, width = current.shape
-        return scatter_step(current.reshape(outer, 2, rows // 2, width).transpose(1, 0, 2, 3), "ctx", 1)
-
-    def cross_one(self):
-        half = self.shape[0] // 2
-        one, two = self.value[:, :half], self.value[:, half:]
-        self.value = (self.over_owners(one)[None], self.over_ctx(two))
-
-    def cross_two(self):
-        one, two = self.value
-        self.value = jnp.concatenate([self.over_ctx(one)[0], self.over_owners(two)], axis=0)
-
-    def scatter(self, bit):
-        rows, width = self.value.shape
-        self.value = scatter_step(self.value.reshape(2, rows // 2, width), "ctx", bit)
-
-    def gather(self, bit):
-        self.value = gather_step(self.value, "ctx", bit)
-
-    def last(self):
-        rows, width = self.value.shape
-        both = gather_step(self.value.reshape(2, 1, rows // 2, width), "ctx", 1, 1)
-        self.value = both.reshape(2 * rows, width)
+    def __init__(self, meta, keep, send, far=None):
+        self.meta, self.rows, self.far = meta, keep.shape[1], far
+        self.bits = bits_of("ctx")[1:]
+        self.keep, self.got = keep, [swap(send, "fsdp", 1)]
+
+    def call(self, name, function, arrays, *shapes):
+        return step_call(name, function, self.meta, arrays, [(*shape, WIDTH) for shape in shapes])
+
+    def cross(self):
+        far = [self.far[1]] if self.far else []
+        extra = far[0].shape[0] if far else 0
+        half = self.rows // 2
+
+        def function(here, owner, keep, got, *far):
+            mine, other = choose(owner >> 1, *(keep + got))
+            keep, near = choose(here & 1, *halves(mine))
+            high, both = choose(here & 1, *halves(other))
+            return keep, jnp.concatenate([near, *far], axis=0), high, both
+
+        shapes = [(half,), (half + extra,), (half,), (half,)]
+        self.keep, near, high, both = self.call("cross", function, [self.keep, *self.got, *far], *shapes)
+        count = lax.axis_size("fsdp")
+        route = [(i, i ^ count ^ 2) for i in range(count * lax.axis_size("ctx"))]
+        self.got = [swap(near, "ctx", 1), swap(high, "fsdp", 2), lax.ppermute(both, ("ctx", "fsdp"), route)]
+
+    def scatter(self, at):
+        bit, last = self.bits[at], at == len(self.bits) - 1
+        rows = self.keep.shape[0]
+        far = [self.far[0]] if self.far else []
+        extra = far[0].shape[0] // 2 if far else 0
+
+        def function(here, owner, keep, *got):
+            far_keep = got[-1]
+            got = got[: len(got) - len(far)]
+            total = keep + got[0][:rows]
+            for other in got[1:]:
+                total = total + other
+            flag = (here // bit) & 1
+            keep, send = (total, total) if last else choose(flag, *halves(total))
+            if not far:
+                return [keep] if last else [keep, send]
+            far_keep, far_send = choose_groups(flag, far_keep + got[0][rows:])
+            return keep, jnp.concatenate([send, far_send], axis=0), far_keep
+
+        count = rows if last else rows // 2
+        shapes = [(count,)] if last and not far else [(count,), (count + extra,)]
+        out = self.call("scatter", function, [self.keep, *self.got, *far], *shapes, *([(extra,)] if far else []))
+        self.keep, send = out[0], out[1] if len(out) > 1 else out[0]
+        self.got = [swap(send, "ctx", bit)]
+        if far:
+            self.far = (out[2], None)
+
+    def gather(self, at):
+        rows = self.keep.shape[0]
+        bit = self.bits[at]
+        last = at == len(self.bits) - 1
+        if last and self.far:
+            self.far = (self.far[0], self.got[0][rows:])
+
+        def function(here, owner, keep, got):
+            if last:
+                return [keep + got[:rows]]
+            return [jnp.concatenate(choose((here // bit) & 1, keep, got), axis=0)]
+
+        (self.keep,) = self.call("gather", function, [self.keep, *self.got], (rows if last else 2 * rows,))
+        self.got = [swap(self.keep, "ctx", self.bits[at - 1] if at else 1)]
+
+    def steps(self):
+        count = len(self.bits)
+        return (
+            [self.cross]
+            + [partial(self.scatter, at) for at in range(count)]
+            + [partial(self.gather, at) for at in range(count - 1, -1, -1)]
+        )
+
+    def finish(self, shapes, unpack):
+        def function(here, owner, keep, got):
+            return unpack(jnp.concatenate(choose(here & 1, keep, got), axis=0))
+
+        return step_call("finish", function, self.meta, [self.keep, *self.got], shapes, f32)
 
 
 def shards(
@@ -936,71 +983,91 @@
     meta = jnp.stack([here] + [owner ^ at for at in range(owners)]).astype(jnp.int32)
 
     vectors = [ln1_gain, ln1_bias, query_bias, value_bias, out_bias, ln2_gain, ln2_bias, down_bias, up_bias]
-    pieces = {0: pack_call(qkv_weight, vectors)}
-    for bit in reversed(bits_of("fsdp")):
-        for at in list(pieces):
-            pieces[at ^ bit] = swap(pieces[at], "fsdp", bit)
-    rest_shard = jnp.concatenate([down_weight, out_weight], axis=0)
-    tied = together(up_weight, rest_shard, *(pieces[at] for at in range(owners)))
-    pieces = tied[2:]
-    rest = lax.all_gather(tied[1], "fsdp", axis=0, tiled=False)
-    up_full = lax.all_gather(tied[0], "fsdp", axis=0, tiled=True)
-
+    own = pack_call(qkv_weight, vectors)
+    across = swap(own, "fsdp", 2)
+    beside = swap(own, "fsdp", 1)
+    one, two = pack_rest_call(down_weight, up_weight, out_weight)
     bias = mask_call(rows, total, far, meta, doc_lengths)
-    qkv_full, vec, up_shift, queries, levels, scaled, tail, head = qkv_call(rows, hidden_width, meta, x, pieces)
+    across, beside, one, two, bias = together(across, beside, one, two, bias)
+    pieces = [own, beside, across, swap(across, "fsdp", 1)]
+    one_across = swap(one, "fsdp", 2)
+    *made, one_across = together(*qkv_call(rows, hidden_width, meta, x, pieces, bias), one_across)
+    qkv_full, vec, up_shift, queries = made[:4]
+    levels, scaled, (tail, head, base) = made[4 : 4 + LOCAL], made[4 + LOCAL : 4 + 2 * LOCAL], made[4 + 2 * LOCAL :]
+
+    two, one, tail, head, base = together(two, one, tail, head, base)
+    two_across = swap(two, "fsdp", 2)
+    one_beside, one_both = swap(one, "fsdp", 1), swap(one_across, "fsdp", 1)
     left = shifted(tail, "ctx", 1)
     right = shifted(head, "ctx", -1)
-    base = tail[BLOCK * (LOCAL - 1) :]
     for at, bit in enumerate(bits_of("ctx")):
         base = gather_step(base, "ctx", bit)
         if at == 0:
             base, left, right = together(base, left, right)
-
+    base, one_beside, one_both, two_across = together(base, one_beside, one_both, two_across)
+
+    two_beside, two_both = swap(two, "fsdp", 1), swap(two_across, "fsdp", 1)
     attended, logs = attend_call(rows, devices, far, meta, queries, bias, levels, left, right, base)
-    output, grad_middle, grad_attended, feed_grads = feed_call(
-        owners, x, attended, cot, rest, up_full, vec, up_shift
+    attended, logs, two_beside, two_both = together(attended, logs, two_beside, two_both)
+    output, grad_middle, grad_attended, keep, send = feed_call(
+        hidden_width,
+        devices,
+        meta,
+        x,
+        attended,
+        cot,
+        vec,
+        up_shift,
+        [one, one_beside, one_across, one_both],
+        [two, two_beside, two_across, two_both],
     )
-    feed = Reduction(feed_grads).step()
-    back = partial(attend_back_call, rows, devices, far, owners)
-    count = PAIRS // 2
-    common = (bias, logs, levels, scaled, left, right, base, qkv_full, vec)
-    (grad_attended,) = feed.after(grad_attended)
-    dq_one, local_one, *before = back(0, count, None, meta, queries, grad_attended, *common)
-    feed.step()
-    tied = together(*feed.value, *before)
-    feed.value, before = tied[:2], tied[2:]
-    dq_two, local_two, to_left, to_right, to_far, qkv_grads = back(
-        count, count, before, meta, queries, grad_attended, *common
+    feed = Reduction(meta, keep, send)
+    todo = feed.steps()
+    todo.pop(0)()
+    grad_attended, feed.keep = together(grad_attended, feed.keep)
+    made = attend_back_call(
+        rows, devices, far, owners, meta, queries, grad_attended, bias, logs, levels, scaled, left, right, base, qkv_full, vec
     )
-    feed.step()
-    first = Reduction(qkv_grads)
-
+    count = len(made)
+    made = together(*made, *feed.got)
+    feed.got = list(made[count:])
+    dq, local, to_left, to_right, far_keep, far_send, keep, send = made[:count]
+    first = Reduction(meta, keep, send, (far_keep, far_send))
     back_right = shifted(to_left, "ctx", -1)
     back_left = shifted(to_right, "ctx", 1)
-    back_far = to_far
-    for at, bit in enumerate(reversed(bits_of("ctx"))):
-        back_far = scatter_step(back_far.reshape(2, -1, 2 * WIDTH), "ctx", bit)
-        if at == 0:
-            back_far, back_right, back_left = together(back_far, back_right, back_left)
+    for one, two in zip(first.steps(), todo + [None]):
+        if two:
+            two()
+        one()
     input_grad = input_grad_call(
-        x, [dq_one, dq_two], [local_one, local_two], grad_middle, back_right, back_left, back_far, qkv_full, vec
+        x, [dq], [local], grad_middle, back_right, back_left, *first.far, qkv_full, vec
     )
-    while feed.todo or first.todo:
-        first.step()
-        feed.step()
-    feed_sum, qkv_sum = feed.value.astype(f32), first.value.astype(f32)
 
     wide_rows = hidden_width // owners
-    down_grad = feed_sum[:wide_rows]
-    up_grad = jnp.concatenate(
-        [feed_sum[wide_rows + at * part : wide_rows + (at + 1) * part] for at in range(hidden_width // WIDTH)], axis=1
+
+    def unpack_first(total):
+        blocks = [total[at * part : (at + 1) * part] for at in range(3)]
+        return [jnp.concatenate(blocks, axis=1), total[3 * part : 3 * part + 1]]
+
+    def unpack_feed(total):
+        at = wide_rows
+        blocks = []
+        for _ in range(hidden_width // WIDTH):
+            blocks.append(total[at : at + part])
+            at += part
+        return [
+            total[:wide_rows],
+            jnp.concatenate(blocks, axis=1),
+            total[at : at + part],
+            total[at + part : at + part + 1],
+            total[at + part + 1 : at + part + 2],
+        ]
+
+    qkv_grad, first_row = first.finish([(part, 3 * WIDTH), (1, WIDTH)], unpack_first)
+    down_grad, up_grad, out_grad, feed_row, up_row = feed.finish(
+        [(wide_rows, WIDTH), (part, hidden_width), (part, WIDTH), (1, WIDTH), (1, WIDTH)], unpack_feed
     )
-    out_grad = feed_sum[2 * wide_rows : 2 * wide_rows + part]
-    feed_row = feed_sum[2 * wide_rows + part]
-    up_row = feed_sum[2 * wide_rows + part + 1]
-    qkv_grad = jnp.concatenate([qkv_sum[at * part : (at + 1) * part] for at in range(3)], axis=1)
-    first_row = qkv_sum[3 * part]
-    pick = lambda row, at: row[at * part : (at + 1) * part]
+    pick = lambda row, at: row[0, at * part : (at + 1) * part]
     return (
         output[None],
         input_grad[None],
@@ -1014,7 +1081,7 @@
         pick(feed_row, 1),
         pick(feed_row, 2),
         up_grad,
-        up_row,
+        up_row[0],
         down_grad,
         pick(feed_row, 3),
     )

time: 303 us -> 263 us (0.87)
  waiting for transfers between devices: 92.9 us -> 56.4 us
  Pallas kernels: 128 us -> 149 us
  between operations: 14.7 us -> 0.98 us
  other arithmetic: 12.8 us -> 1.69 us
  local copies, waits for them, and re-layouts: 9.99 us -> 16.9 us
  starting transfers between devices: 44.1 us -> 37.9 us
    ppermute x29 -> x26, waiting for transfers between devices: 71.8 us -> 36.5 us  [swap(): lax.ppermute(block, axis, [(i, i ^ bit) for i in range(lax.axis_size(axis...]
    pallas_call x3 -> x15, Pallas kernels: 77.5 us -> 100 us  [the longest x1 38.2 us: attend_back_call(): pl.pallas_call(partial(attend_back_kernel, rows, far), grid=(chunks,), ou...]
    unnamed x16 -> x66, local copies, waits for them, and re-layouts: 0.94 us -> 12.6 us
    ppermute x29 -> x26, starting transfers between devices: 34.7 us -> 24.4 us  [swap(): lax.ppermute(block, axis, [(i, i ^ bit) for i in range(lax.axis_size(axis...]
    ppermute x4, waiting for transfers between devices: 21.1 us -> 12.7 us  [shifted(): return lax.ppermute(block, axis, route)]
    ppermute x0 -> x2, waiting for transfers between devices: none -> 7.22 us  [cross(): lax.ppermute(both, ('ctx', 'fsdp'), route)]
    convert_element_type x14 -> x0, other arithmetic: 6.07 us -> none  [the longest x12 5.54 us: add_low(): return (left.astype(f32) + right.astype(f32)).astype(bf16)]
    concatenate x14 -> x3, other arithmetic: 5.23 us -> 0.8 us  [gather_step(): return jnp.concatenate([first, second], axis=0)]
  transfers between devices with their start and end apart: 35 -> 32, of which waited for: 20 -> 14; matrix products, arithmetic and copies ran while one was open for 4% -> 2% of each run, Pallas kernels for 23% -> 41%
where the time goes in v3:
time: 263 us; the launch traced here: 262 us
  Pallas kernels  149 us (57%)
  waiting for transfers between devices  56.4 us (21%)
  starting transfers between devices  37.9 us (14%)
  local copies, waits for them, and re-layouts  16.9 us (6%)
    pallas_call x1, Pallas kernels, attend_back_call(): pl.pallas_call(partial(attend_back_kernel, rows, far), grid=(chunks,), ou...  38.2 us
    ppermute x26, waiting for transfers between devices, swap(): lax.ppermute(block, axis, [(i, i ^ bit) for i in range(lax.axis_size(axis...  36.5 us
    pallas_call x1, Pallas kernels, feed_call(): pl.pallas_call(partial(feed_kernel, hidden_width, owners), grid=(rows //...  31.9 us
    pallas_call x12, Pallas kernels, step_call(): pl.pallas_call(kernel, out_shape=[jax.ShapeDtypeStruct(shape, dtype) for...  27.7 us
    ppermute x26, starting transfers between devices, swap(): lax.ppermute(block, axis, [(i, i ^ bit) for i in range(lax.axis_size(axis...  24.4 us
    pallas_call x1, Pallas kernels, attend_call(): pl.pallas_call(partial(attend_kernel, rows, far), grid=(chunks,), out_sha...  21.4 us
    ppermute x4, waiting for transfers between devices, shifted(): return lax.ppermute(block, axis, route)  12.7 us
    unnamed x66, local copies, waits for them, and re-layouts  12.6 us
  transfers between devices with their start and end apart: 32, of which 14 were waited for; matrix products, arithmetic and copies ran while one was open for 2% of the time, Pallas kernels for 41%

profile of v3, /device:TPU:0, one launch (start us, length us, event | category | flops | bytes accessed | tf_op | source)
XLA Modules:
  0.0 262.5 jit_solution(152985403066371175)
XLA Ops:
  3.0 2.5 collective-permute-start
  8.3 4.5 %mask.1.refs_4_.bias_ref.refs_3_ = f32[8,528,128]{2,1,0:T(8,128)} custom-call(s32[5]{0:T(128)} %stack.23.here_ref.meta_ref.refs_0_, s32[1,8]{1,0:T(1,128)} %lengths_ref.1), custom_call_target="tpu_custom_call" | custom-call | flops 4294967296 | bytes 3145728 | tf_op jit(solution)/shard_map/mask/pallas_call | solution.py:107
  12.9 3.6 %collective-permute-done.refs_2_ = bf16[144,1536]{1,0:T(8,128)(2,1)S(1)} collective-permute-done((bf16[144,1536]{1,0:T(8,128)(2,1)}, bf16[144,1536]{1,0:T(8,128)(2,1)S(1)}, u32[]{:S(2)}, u32[]{:S(2)}) %collective-permute-start) | collective-permute-done | bytes 442400 | tf_op jit(solution)/shard_map/ppermute | solution.py:831
  19.1 10.6 %qkv_levels.1 = (bf16[512,1536]{1,0:T(8,128)(2,1)}, f32[8,512]{1,0:T(8,128)}, f32[1,2048]{1,0:T(1,128)}, bf16[1024,512]{1,0:T(8,128)(2,1)}, bf16[1024,1024]{1,0:...) custom-call(s32[5]{0:T(128)} %stack.23.here_ref.meta_ref.refs_0_, ...), custom_call_target="tpu_custom_call" | custom-call | flops 9663676416 | bytes 12582912 | tf_op jit(solution)/shard_map/qkv_levels/pallas_call | solution.py:305
  31.5 2.3 collective-permute-start.5
  36.1 12.7 %collective-permute-done.5.refs_7_.refs_19_ = bf16[112,1536]{1,0:T(8,128)(2,1)S(1)} collective-permute-done((bf16[112,1536]{1,0:T(8,128)(2,1)}, bf16[112,1536]{1,0:T(8,128)(2,1)S(1)}, u32[]{:S(2)}, u32[]{:S(2)}) %collective-permute-start.5) | collective-permute-done | bytes 344096 | tf_op jit(solution)/shard_map/ppermute | solution.py:827
  48.8 4.5 %collective-permute-start.7 = (bf16[32,1536]{1,0:T(8,128)(2,1)S(1)}, bf16[32,1536]{1,0:T(8,128)(2,1)S(1)}, u32[]{:S(2)}, u32[]{:S(2)}) collective-permute-start(bf16[32,1536]{1,0:T(8,128)(2,1)S(1)} %pad_maximum_fusion.2), channel_id=1, source_target_pairs={{0,8},{4,12},{8,0},{12,4},{16,24},{20,28},{24,16},{28,20},{1,9},{5... | collective-permute-start | bytes 294920 | tf_op jit(solution)/shard_map/ppermute | solution.py:831
  53.3 3.0 %collective-permute-done.7 = bf16[32,1536]{1,0:T(8,128)(2,1)S(1)} collective-permute-done((bf16[32,1536]{1,0:T(8,128)(2,1)S(1)}, bf16[32,1536]{1,0:T(8,128)(2,1)S(1)}, u32[]{:S(2)}, u32[]{:S(2)}) %collective-permute-start.7) | collective-permute-done | bytes 98336 | tf_op jit(solution)/shard_map/ppermute | solution.py:831
  56.3 2.8 %collective-permute-start.8 = (bf16[64,1536]{1,0:T(8,128)(2,1)S(1)}, bf16[64,1536]{1,0:T(8,128)(2,1)S(1)}, u32[]{:S(2)}, u32[]{:S(2)}) collective-permute-start(bf16[64,1536]{1,0:T(8,128)(2,1)S(1)} %pad_maximum_fusion.1), channel_id=1, source_target_pairs={{0,16},{4,20},{8,24},{12,28},{16,0},{20,4},{24,8},{28,12},{1,17},{... | collective-permute-start | bytes 589832 | tf_op jit(solution)/shard_map/ppermute | solution.py:831
  61.2 6.6 %collective-permute-done.8 = bf16[64,1536]{1,0:T(8,128)(2,1)S(1)} collective-permute-done((bf16[64,1536]{1,0:T(8,128)(2,1)S(1)}, bf16[64,1536]{1,0:T(8,128)(2,1)S(1)}, u32[]{:S(2)}, u32[]{:S(2)}) %collective-permute-start.8) | collective-permute-done | bytes 196640 | tf_op jit(solution)/shard_map/ppermute | solution.py:831
  68.7 8.8 %collective-permute-done.11.refs_6_ = bf16[768,512]{1,0:T(8,128)(2,1)S(1)} collective-permute-done((bf16[768,512]{1,0:T(8,128)(2,1)S(1)}, bf16[768,512]{1,0:T(8,128)(2,1)S(1)}, u32[]{:S(2)}, u32[]{:S(2)}) %collective-permute-start.11) | collective-permute-done | bytes 786464 | tf_op jit(solution)/shard_map/ppermute | solution.py:831
  77.5 21.4 %attend.1 = (bf16[1024,512]{1,0:T(8,128)(2,1)}, f32[8,8,256]{2,1,0:T(8,128)}) custom-call(s32[5]{0:T(128)} %stack.23.here_ref.meta_ref.refs_0_, bf16[1024,512]{1,0:T(8,128)(2,1)} %get-tuple-element.159.q_ref.refs_1_, f32[8,528,128]{2,1,0:T(8,128)} %mask.1.refs_4_.bias_ref.refs_3_, bf16[1024,1024]{1,0:T(8,128)(2,1)} %get-tuple-element.160.refs_0_.refs_5_, ...), custom_call_target="tpu_custom_call" | custom-call | flops 21474836480 | bytes 12582912 | tf_op jit(solution)/shard_map/attend/pallas_call | solution.py:397
  100.1 31.9 %feed_forward.1 = (bf16[1024,512]{1,0:T(8,128)(2,1)}, f32[1024,512]{1,0:T(8,128)}, bf16[1024,512]{1,0:T(8,128)(2,1)}, bf16[2,1216,512]{2,1,0:T(8,128)(2,1)}, bf16[2,1216,512]{2,1,0:T(8,128)(2,1)}) custom-call(s32[5]{0:T(128)} %stack.23.here_ref.meta_ref.refs_0_, bf16[1024,512]{1,0:T(8,128)(2,1)} %bitcast.28, ...), custom_call_target="tpu_custom_call" | custom-call | flops 34359738368 | bytes 20971520 | tf_op jit(solution)/shard_map/feed_forward/pallas_call | solution.py:722
  132.3 4.7 %collective-permute-done.14.refs_1_ = bf16[2,1216,512]{2,1,0:T(8,128)(2,1)S(1)} collective-permute-done((bf16[2,1216,512]{2,1,0:T(8,128)(2,1)}, bf16[2,1216,512]{2,1,0:T(8,128)(2,1)S(1)}, u32[]{:S(2)}, u32[]{:S(2)}) %collective-permute-start.14) | collective-permute-done | bytes 2490400 | tf_op jit(solution)/shard_map/ppermute | solution.py:831
  138.4 4.5 %cross.2 = (bf16[608,512]{1,0:T(8,128)(2,1)}, bf16[608,512]{1,0:T(8,128)(2,1)}, bf16[608,512]{1,0:T(8,128)(2,1)}, bf16[608,512]{1,0:T(8,128)(2,1)}) custom-call(s32[5]{0:T(128)} %stack.23.here_ref.meta_ref.refs_0_, bf16[2,1216,512]{2,1,0:T(8,128)(2,1)} %get-tuple-element.193.refs_0_, bf16[2,1216,512]{2,1,0:T(8,128)(2,1)} %copy-done), custom_call_target="tpu_custom_call" | custom-call | flops 1048576 | bytes 9961472 | tf_op jit(solution)/shard_map/cross/pallas_call | solution.py:858
  146.5 38.2 %attend_back.1 = (bf16[1024,512]{1,0:T(8,128)(2,1)}, f32[1024,1024]{1,0:T(8,128)}, bf16[112,1024]{1,0:T(8,128)(2,1)}, bf16[112,1024]{1,0:T(8,128)(2,1)}, bf16[64...) custom-call(s32[5]{0:T(128)} %stack.23.here_ref.meta_ref.refs_0_, ...), custom_call_target="tpu_custom_call" | custom-call | flops 38654705664 | bytes 25165824 | tf_op jit(solution)/shard_map/attend_back/pallas_call | solution.py:582
  185.9 2.8 %scatter.6 = (bf16[304,512]{1,0:T(8,128)(2,1)}, bf16[304,512]{1,0:T(8,128)(2,1)}) custom-call(s32[5]{0:T(128)} %stack.23.here_ref.meta_ref.refs_0_, bf16[608,512]{1,0:T(8,128)(2,1)} %get-tuple-element.238.refs_0_, bf16[608,512]{1,0:T(8,128)(2,1)} %copy-done.2, bf16[608,512]{1,0:T(8,128)(2,1)} %copy-done.3, bf16[608,512]{1,0:T(8,128)(2,1)} %copy-done.4), custom_call_target="tpu_custom_call" | custom-call | flops 1048576 | bytes 4980736 | tf_op jit(solution)/shard_map/scatter/pallas_call | solution.py:858
  191.2 2.6 %cross.3 = (bf16[224,512]{1,0:T(8,128)(2,1)}, bf16[288,512]{1,0:T(8,128)(2,1)}, bf16[224,512]{1,0:T(8,128)(2,1)}, bf16[224,512]{1,0:T(8,128)(2,1)}) custom-call(s32[5]{0:T(128)} %stack.23.here_ref.meta_ref.refs_0_, bf16[2,448,512]{2,1,0:T(8,128)(2,1)} %get-tuple-element.222.refs_0_, bf16[2,448,512]{2,1,0:T(8,128)(2,1)} %copy-done.1, ...), custom_call_target="tpu_custom_call" | custom-call | flops 1048576 | bytes 3801088 | tf_op jit(solution)/shard_map/cross/pallas_call | solution.py:858
  200.8 7.2 %collective-permute-done.23.refs_3_ = bf16[224,512]{1,0:T(8,128)(2,1)S(1)} collective-permute-done((bf16[224,512]{1,0:T(8,128)(2,1)}, bf16[224,512]{1,0:T(8,128)(2,1)S(1)}, u32[]{:S(2)}, u32[]{:S(2)}) %collective-permute-start.23) | collective-permute-done | bytes 229408 | tf_op jit(solution)/shard_map/ppermute | solution.py:897
  211.3 4.5 %collective-permute-done.29.refs_1_ = bf16[304,512]{1,0:T(8,128)(2,1)S(1)} collective-permute-done((bf16[304,512]{1,0:T(8,128)(2,1)}, bf16[304,512]{1,0:T(8,128)(2,1)S(1)}, u32[]{:S(2)}, u32[]{:S(2)}) %collective-permute-start.29) | collective-permute-done | bytes 311328 | tf_op jit(solution)/shard_map/ppermute | solution.py:831
  224.0 4.6 %collective-permute-start.19 = (bf16[112,1024]{1,0:T(8,128)(2,1)S(1)}, bf16[112,1024]{1,0:T(8,128)(2,1)S(1)}, u32[]{:S(2)}, u32[]{:S(2)}) collective-permute-start(bf16[112,1024]{1,0:T(8,128)(2,1)S(1)} %copy-done.29), channel_id=1, source_target_pairs={{0,4},{4,8},{8,12},{12,16},{16,20},{20,24},{24,28},{1,5},{5,9},{9,... | collective-permute-start | bytes 688136 | tf_op jit(solution)/shard_map/ppermute | solution.py:827
  228.6 3.0 %collective-permute-done.25.refs_1_ = bf16[128,512]{1,0:T(8,128)(2,1)S(1)} collective-permute-done((bf16[128,512]{1,0:T(8,128)(2,1)}, bf16[128,512]{1,0:T(8,128)(2,1)S(1)}, u32[]{:S(2)}, u32[]{:S(2)}) %collective-permute-start.25) | collective-permute-done | bytes 131104 | tf_op jit(solution)/shard_map/ppermute | solution.py:831
  243.2 10.0 %input_grad.1 = f32[1024,512]{1,0:T(8,128)} custom-call(bf16[1024,512]{1,0:T(8,128)(2,1)} %bitcast.29, bf16[1024,512]{1,0:T(8,128)(2,1)} %get-tuple-element.217.refs_0_, f32[1024,1024]{1,0:T(8,128)} %get-tuple-element.218.refs_1_, f32[1024,512]{1,0:T(8,128)} %get-tuple-element.219.refs_2_, bf16[112,1024]{1,0:T(8,128)(2,1)} %copy-done.31, ...), custom_call_target="tpu_custom_call" | custom-call | flops 8589934592 | bytes 14680064 | tf_op jit(solution)/shard_map/input_grad/pallas_call | solution.py:807
  254.6 2.8 %finish.3 = (f32[512,512]{1,0:T(8,128)}, f32[128,2048]{1,0:T(8,128)}, f32[128,512]{1,0:T(8,128)}, f32[1,512]{1,0:T(1,128)}, f32[1,512]{1,0:T(1,128)}) custom-call(s32[5]{0:T(128)} %stack.23.here_ref.meta_ref.refs_0_, bf16[608,512]{1,0:T(8,128)(2,1)} %gather.7.refs_0_, bf16[608,512]{1,0:T(8,128)(2,1)} %copy-done.5), custom_call_target="tpu_custom_call" | custom-call | flops 1048576 | bytes 2490368 | tf_op jit(solution)/shard_map/finish/pallas_call | solution.py:858
  (136 shorter events, 61.3 us)
Async XLA Ops:
  2.5 10.4 %collective-permute-start.1 = (bf16[144,1536]{1,0:T(8,128)(2,1)}, bf16[144,1536]{1,0:T(8,128)(2,1)S(1)}, u32[]{:S(2)}, u32[]{:S(2)}) collective-permute-start(bf16[144,1536]{1,0:T(8,128)(2,1)} %pack.1.refs_0_), channel_id=1, source_target_pairs={{0,1},{1,0},{2,3},{3,2},{4,5},{5,4},{6,7},{7,6},{8,9},{9,8},{10,11... | collective-permute-start | bytes 1327112 | tf_op jit(solution)/shard_map/ppermute | solution.py:831
  3.0 13.6 %collective-permute-start = (bf16[144,1536]{1,0:T(8,128)(2,1)}, bf16[144,1536]{1,0:T(8,128)(2,1)S(1)}, u32[]{:S(2)}, u32[]{:S(2)}) collective-permute-start(bf16[144,1536]{1,0:T(8,128)(2,1)} %pack.1.refs_0_), channel_id=1, source_target_pairs={{0,2},{1,3},{2,0},{3,1},{4,6},{5,7},{6,4},{7,5},{8,10},{9,11},{10,... | collective-permute-start | bytes 1327112 | tf_op jit(solution)/shard_map/ppermute | solution.py:831
  16.6 13.2 %collective-permute-start.3 = (bf16[384,512]{1,0:T(8,128)(2,1)S(1)}, bf16[384,512]{1,0:T(8,128)(2,1)S(1)}, u32[]{:S(2)}, u32[]{:S(2)}) collective-permute-start(bf16[384,512]{1,0:T(8,128)(2,1)S(1)} %copy-done.23), channel_id=1, source_target_pairs={{0,2},{1,3},{2,0},{3,1},{4,6},{5,7},{6,4},{7,5},{8,10},{9,11},{10,... | collective-permute-start | bytes 1179656 | tf_op jit(solution)/shard_map/ppermute | solution.py:831
  31.5 17.3 %collective-permute-start.5 = (bf16[112,1536]{1,0:T(8,128)(2,1)}, bf16[112,1536]{1,0:T(8,128)(2,1)S(1)}, u32[]{:S(2)}, u32[]{:S(2)}) collective-permute-start(bf16[112,1536]{1,0:T(8,128)(2,1)} %get-tuple-element.172), channel_id=1, source_target_pairs={{0,4},{4,8},{8,12},{12,16},{16,20},{20,24},{24,28},{1,5},{5,9},{9,... | collective-permute-start | bytes 1032200 | tf_op jit(solution)/shard_map/ppermute | solution.py:827
  33.8 15.0 %collective-permute-start.6 = (bf16[112,1536]{1,0:T(8,128)(2,1)}, bf16[112,1536]{1,0:T(8,128)(2,1)S(1)}, u32[]{:S(2)}, u32[]{:S(2)}) collective-permute-start(bf16[112,1536]{1,0:T(8,128)(2,1)} %get-tuple-element.173), channel_id=1, source_target_pairs={{4,0},{8,4},{12,8},{16,12},{20,16},{24,20},{28,24},{5,1},{9,5},{13... | collective-permute-start | bytes 1032200 | tf_op jit(solution)/shard_map/ppermute | solution.py:827
  56.3 11.5 %collective-permute-start.8 = (bf16[64,1536]{1,0:T(8,128)(2,1)S(1)}, bf16[64,1536]{1,0:T(8,128)(2,1)S(1)}, u32[]{:S(2)}, u32[]{:S(2)}) collective-permute-start(bf16[64,1536]{1,0:T(8,128)(2,1)S(1)} %pad_maximum_fusion.1), channel_id=1, source_target_pairs={{0,16},{4,20},{8,24},{12,28},{16,0},{20,4},{24,8},{28,12},{1,17},{... | collective-permute-start | bytes 589832 | tf_op jit(solution)/shard_map/ppermute | solution.py:831
  59.2 18.3 %collective-permute-start.11 = (bf16[768,512]{1,0:T(8,128)(2,1)S(1)}, bf16[768,512]{1,0:T(8,128)(2,1)S(1)}, u32[]{:S(2)}, u32[]{:S(2)}) collective-permute-start(bf16[768,512]{1,0:T(8,128)(2,1)S(1)} %copy-done.16), channel_id=1, source_target_pairs={{0,2},{1,3},{2,0},{3,1},{4,6},{5,7},{6,4},{7,5},{8,10},{9,11},{10,... | collective-permute-start | bytes 2359304 | tf_op jit(solution)/shard_map/ppermute | solution.py:831
  60.7 38.3 %collective-permute-start.12 = (bf16[768,512]{1,0:T(8,128)(2,1)S(1)}, bf16[768,512]{1,0:T(8,128)(2,1)S(1)}, u32[]{:S(2)}, u32[]{:S(2)}) collective-permute-start(bf16[768,512]{1,0:T(8,128)(2,1)S(1)} %copy-done.16), channel_id=1, source_target_pairs={{0,1},{1,0},{2,3},{3,2},{4,5},{5,4},{6,7},{7,6},{8,9},{9,8},{10,11... | collective-permute-start | bytes 2359304 | tf_op jit(solution)/shard_map/ppermute | solution.py:831
  60.7 8.0 %collective-permute-start.9 = (bf16[384,512]{1,0:T(8,128)(2,1)S(1)}, bf16[384,512]{1,0:T(8,128)(2,1)S(1)}, u32[]{:S(2)}, u32[]{:S(2)}) collective-permute-start(bf16[384,512]{1,0:T(8,128)(2,1)S(1)} %copy-done.23), channel_id=1, source_target_pairs={{0,1},{1,0},{2,3},{3,2},{4,5},{5,4},{6,7},{7,6},{8,9},{9,8},{10,11... | collective-permute-start | bytes 1179656 | tf_op jit(solution)/shard_map/ppermute | solution.py:831
  77.5 21.5 %collective-permute-start.13 = (bf16[768,512]{1,0:T(8,128)(2,1)S(1)}, bf16[768,512]{1,0:T(8,128)(2,1)S(1)}, u32[]{:S(2)}, u32[]{:S(2)}) collective-permute-start(bf16[768,512]{1,0:T(8,128)(2,1)S(1)} %collective-permute-done.11.refs_6_), channel_id=1, source_target_pairs={{0,1},{1,0},{2,3},{3,2},{4,5},{5,4},{6,7},{7,6},{8,9},{9,8},{10,11... | collective-permute-start | bytes 2359304 | tf_op jit(solution)/shard_map/ppermute | solution.py:831
  143.0 41.7 %collective-permute-start.15 = (bf16[608,512]{1,0:T(8,128)(2,1)}, bf16[608,512]{1,0:T(8,128)(2,1)S(1)}, u32[]{:S(2)}, u32[]{:S(2)}) collective-permute-start(bf16[608,512]{1,0:T(8,128)(2,1)} %get-tuple-element.214), channel_id=1, source_target_pairs={{0,4},{4,0},{8,12},{12,8},{16,20},{20,16},{24,28},{28,24},{1,5},{5... | collective-permute-start | bytes 1867784 | tf_op jit(solution)/shard_map/ppermute | solution.py:831
  143.0 41.7 %collective-permute-start.16 = (bf16[608,512]{1,0:T(8,128)(2,1)}, bf16[608,512]{1,0:T(8,128)(2,1)S(1)}, u32[]{:S(2)}, u32[]{:S(2)}) collective-permute-start(bf16[608,512]{1,0:T(8,128)(2,1)} %get-tuple-element.215), channel_id=1, source_target_pairs={{0,2},{1,3},{2,0},{3,1},{4,6},{5,7},{6,4},{7,5},{8,10},{9,11},{10,... | collective-permute-start | bytes 1867784 | tf_op jit(solution)/shard_map/ppermute | solution.py:831
  144.5 40.2 %collective-permute-start.17 = (bf16[608,512]{1,0:T(8,128)(2,1)}, bf16[608,512]{1,0:T(8,128)(2,1)S(1)}, u32[]{:S(2)}, u32[]{:S(2)}) collective-permute-start(bf16[608,512]{1,0:T(8,128)(2,1)} %get-tuple-element.216), channel_id=1, source_target_pairs={{0,6},{1,7},{2,4},{3,5},{4,2},{5,3},{6,0},{7,1},{8,14},{9,15},{10,... | collective-permute-start | bytes 1867784 | tf_op jit(solution)/shard_map/ppermute | solution.py:897
  188.7 8.9 %collective-permute-start.28 = (bf16[304,512]{1,0:T(8,128)(2,1)}, bf16[304,512]{1,0:T(8,128)(2,1)S(1)}, u32[]{:S(2)}, u32[]{:S(2)}) collective-permute-start(bf16[304,512]{1,0:T(8,128)(2,1)} %get-tuple-element.243), channel_id=1, source_target_pairs={{0,8},{4,12},{8,0},{12,4},{16,24},{20,28},{24,16},{28,20},{1,9},{5... | collective-permute-start | bytes 933896 | tf_op jit(solution)/shard_map/ppermute | solution.py:831
  193.9 14.1 %collective-permute-start.21 = (bf16[288,512]{1,0:T(8,128)(2,1)}, bf16[288,512]{1,0:T(8,128)(2,1)S(1)}, u32[]{:S(2)}, u32[]{:S(2)}) collective-permute-start(bf16[288,512]{1,0:T(8,128)(2,1)} %get-tuple-element.226), channel_id=1, source_target_pairs={{0,4},{4,0},{8,12},{12,8},{16,20},{20,16},{24,28},{28,24},{1,5},{5... | collective-permute-start | bytes 884744 | tf_op jit(solution)/shard_map/ppermute | solution.py:831
  195.4 12.6 %collective-permute-start.23 = (bf16[224,512]{1,0:T(8,128)(2,1)}, bf16[224,512]{1,0:T(8,128)(2,1)S(1)}, u32[]{:S(2)}, u32[]{:S(2)}) collective-permute-start(bf16[224,512]{1,0:T(8,128)(2,1)} %get-tuple-element.228), channel_id=1, source_target_pairs={{0,6},{1,7},{2,4},{3,5},{4,2},{5,3},{6,0},{7,1},{8,14},{9,15},{10,... | collective-permute-start | bytes 688136 | tf_op jit(solution)/shard_map/ppermute | solution.py:897
  200.2 15.6 %collective-permute-start.29 = (bf16[304,512]{1,0:T(8,128)(2,1)}, bf16[304,512]{1,0:T(8,128)(2,1)S(1)}, u32[]{:S(2)}, u32[]{:S(2)}) collective-permute-start(bf16[304,512]{1,0:T(8,128)(2,1)} %scatter.7.refs_0_), channel_id=1, source_target_pairs={{0,16},{4,20},{8,24},{12,28},{16,0},{20,4},{24,8},{28,12},{1,17},{... | collective-permute-start | bytes 933896 | tf_op jit(solution)/shard_map/ppermute | solution.py:831
  210.9 8.0 %collective-permute-start.24 = (bf16[144,512]{1,0:T(8,128)(2,1)}, bf16[144,512]{1,0:T(8,128)(2,1)S(1)}, u32[]{:S(2)}, u32[]{:S(2)}) collective-permute-start(bf16[144,512]{1,0:T(8,128)(2,1)} %get-tuple-element.231), channel_id=1, source_target_pairs={{0,8},{4,12},{8,0},{12,4},{16,24},{20,28},{24,16},{28,20},{1,9},{5... | collective-permute-start | bytes 442376 | tf_op jit(solution)/shard_map/ppermute | solution.py:831
  218.4 15.5 %collective-permute-start.30 = (bf16[304,512]{1,0:T(8,128)(2,1)}, bf16[304,512]{1,0:T(8,128)(2,1)S(1)}, u32[]{:S(2)}, u32[]{:S(2)}) collective-permute-start(bf16[304,512]{1,0:T(8,128)(2,1)} %gather.6.refs_0_), channel_id=1, source_target_pairs={{0,8},{4,12},{8,0},{12,4},{16,24},{20,28},{24,16},{28,20},{1,9},{5... | collective-permute-start | bytes 933896 | tf_op jit(solution)/shard_map/ppermute | solution.py:831
  221.3 10.3 %collective-permute-start.25 = (bf16[128,512]{1,0:T(8,128)(2,1)}, bf16[128,512]{1,0:T(8,128)(2,1)S(1)}, u32[]{:S(2)}, u32[]{:S(2)}) collective-permute-start(bf16[128,512]{1,0:T(8,128)(2,1)} %get-tuple-element.234), channel_id=1, source_target_pairs={{0,16},{4,20},{8,24},{12,28},{16,0},{20,4},{24,8},{28,12},{1,17},{... | collective-permute-start | bytes 393224 | tf_op jit(solution)/shard_map/ppermute | solution.py:831
  222.7 19.7 %collective-permute-start.18 = (bf16[112,1024]{1,0:T(8,128)(2,1)S(1)}, bf16[112,1024]{1,0:T(8,128)(2,1)S(1)}, u32[]{:S(2)}, u32[]{:S(2)}) collective-permute-start(bf16[112,1024]{1,0:T(8,128)(2,1)S(1)} %copy-done.30), channel_id=1, source_target_pairs={{4,0},{8,4},{12,8},{16,12},{20,16},{24,20},{28,24},{5,1},{9,5},{13... | collective-permute-start | bytes 688136 | tf_op jit(solution)/shard_map/ppermute | solution.py:827
  224.0 18.4 %collective-permute-start.19 = (bf16[112,1024]{1,0:T(8,128)(2,1)S(1)}, bf16[112,1024]{1,0:T(8,128)(2,1)S(1)}, u32[]{:S(2)}, u32[]{:S(2)}) collective-permute-start(bf16[112,1024]{1,0:T(8,128)(2,1)S(1)} %copy-done.29), channel_id=1, source_target_pairs={{0,4},{4,8},{8,12},{12,16},{16,20},{20,24},{24,28},{1,5},{5,9},{9,... | collective-permute-start | bytes 688136 | tf_op jit(solution)/shard_map/ppermute | solution.py:827
  236.7 17.0 %collective-permute-start.31 = (bf16[608,512]{1,0:T(8,128)(2,1)}, bf16[608,512]{1,0:T(8,128)(2,1)S(1)}, u32[]{:S(2)}, u32[]{:S(2)}) collective-permute-start(bf16[608,512]{1,0:T(8,128)(2,1)} %gather.7.refs_0_), channel_id=1, source_target_pairs={{0,4},{4,0},{8,12},{12,8},{16,20},{20,16},{24,28},{28,24},{1,5},{5... | collective-permute-start | bytes 1867784 | tf_op jit(solution)/shard_map/ppermute | solution.py:831
  241.3 17.3 %collective-permute-start.27 = (bf16[224,512]{1,0:T(8,128)(2,1)}, bf16[224,512]{1,0:T(8,128)(2,1)S(1)}, u32[]{:S(2)}, u32[]{:S(2)}) collective-permute-start(bf16[224,512]{1,0:T(8,128)(2,1)} %gather.5.refs_0_), channel_id=1, source_target_pairs={{0,4},{4,0},{8,12},{12,8},{16,20},{20,16},{24,28},{28,24},{1,5},{5... | collective-permute-start | bytes 688136 | tf_op jit(solution)/shard_map/ppermute | solution.py:831
  (41 other events, 380.8 us)

commit v4 on v3

--- a/solution.py
+++ b/solution.py
@@ -20,7 +20,6 @@
 SMALL = 16
 MASKED = -1e30
 EPSILON = 1e-05
-VMEM_LIMIT = 56 * 1024 * 1024
 
 f32 = jnp.float32
 bf16 = jnp.bfloat16
@@ -28,6 +27,13 @@
 
 def level_rows(rows, level):
     return rows // 2**level
+
+
+def level_offsets(rows):
+    offsets = [0]
+    for level in range(LOCAL):
+        offsets.append(offsets[-1] + level_rows(rows, level))
+    return offsets[:-1], offsets[-1]
 
 
 def far_levels(total):
@@ -110,6 +116,7 @@
         out_shape=jax.ShapeDtypeStruct((chunks, slots, CHUNK), f32),
         in_specs=[pl.BlockSpec(memory_space=pltpu.SMEM)] * 2,
         out_specs=pl.BlockSpec((1, slots, CHUNK), lambda i: (i, 0, 0)),
+        compiler_params=pltpu.CompilerParams(vmem_limit_bytes=8 << 20),
         cost_estimate=pl.CostEstimate(flops=4 << 30, bytes_accessed=3 << 20, transcendentals=0),
         name="mask",
     )(meta, lengths)
@@ -193,6 +200,7 @@
         out_shape=jax.ShapeDtypeStruct((weight.shape[0] + SMALL, weight.shape[1]), bf16),
         in_specs=vmem_specs(1 + len(vectors)),
         out_specs=vmem_specs(1)[0],
+        compiler_params=pltpu.CompilerParams(vmem_limit_bytes=56 << 20),
         name="pack",
     )(weight, *vectors)
 
@@ -217,6 +225,7 @@
         ],
         in_specs=vmem_specs(3),
         out_specs=vmem_specs(2),
+        compiler_params=pltpu.CompilerParams(vmem_limit_bytes=56 << 20),
         name="pack_rest",
     )(down, up, out_w)
 
@@ -226,10 +235,10 @@
 
 
 def qkv_kernel(rows, owners, meta_ref, x_ref, *refs):
-    shard_refs, refs = refs[:owners], refs[owners + 1 :]
+    shard_refs, refs = refs[:owners], refs[owners + 2 :]
     w_ref, vec_ref, up_bias_ref, q_ref = refs[:4]
-    kv_refs, scaled_refs = refs[4 : 4 + LOCAL], refs[4 + LOCAL : 4 + 2 * LOCAL]
-    tail_ref, head_ref, top_ref, keep_ref = refs[4 + 2 * LOCAL :]
+    kv_ref, scaled_ref, tail_ref, head_ref, top_ref, keep_ref = refs[4:]
+    places, _ = level_offsets(rows)
     part = WIDTH // owners
     step = pl.program_id(0)
 
@@ -267,10 +276,11 @@
     for level in range(5):
         if level:
             current = dot_nn(pool_matrix(current.shape[0]), current).astype(bf16)
-        kv_refs[level][...] = current[:, : 2 * WIDTH]
-        scaled_refs[level][...] = current[:, 2 * WIDTH :]
+        count = tile // 2**level
+        span = pl.ds(pl.multiple_of(places[level] + step * count, count), count)
+        kv_ref[span, :] = current[:, : 2 * WIDTH]
+        scaled_ref[span, :] = current[:, 2 * WIDTH :]
         edges(level, current)
-    count = tile // 16
     keep_ref[pl.ds(pl.multiple_of(step * count, count), count), :] = current
 
     @pl.when(step == pl.num_programs(0) - 1)
@@ -278,11 +288,12 @@
         current = keep_ref[...]
         for level in range(5, LOCAL):
             current = dot_nn(pool_matrix(current.shape[0]), current).astype(bf16)
-            kv_refs[level][...] = current[:, : 2 * WIDTH]
-            scaled_refs[level][...] = current[:, 2 * WIDTH :]
+            span = slice(places[level], places[level] + current.shape[0])
+            kv_ref[span, :] = current[:, : 2 * WIDTH]
+            scaled_ref[span, :] = current[:, 2 * WIDTH :]
             tail_ref[BLOCK * level : BLOCK * (level + 1), :] = current[current.shape[0] - BLOCK :]
             head_ref[BLOCK * level : BLOCK * (level + 1), :] = current[:BLOCK]
-        top_ref[...] = current
+        top_ref[...] = dot_nn(pool_matrix(BLOCK), current).astype(bf16)
 
 
 def qkv_call(rows, hidden_width, meta, x, pieces, earlier):
@@ -292,15 +303,7 @@
     def tiled(count, width):
         return pl.BlockSpec((count, width), lambda i: (i, 0))
 
-    def leveled(width):
-        shapes, specs = [], []
-        for level in range(LOCAL):
-            shapes.append(jax.ShapeDtypeStruct((level_rows(rows, level), width), bf16))
-            specs.append(tiled(tile // 2**level, width) if level < 5 else vmem_specs(1)[0])
-        return shapes, specs
-
-    kv_shapes, kv_specs = leveled(2 * WIDTH)
-    scaled_shapes, scaled_specs = leveled(WIDTH)
+    _, entries = level_offsets(rows)
     edge = jax.ShapeDtypeStruct((BLOCK * LOCAL, ENTRY), bf16)
     outs = pl.pallas_call(
         partial(qkv_kernel, rows, owners),
@@ -311,18 +314,17 @@
             jax.ShapeDtypeStruct((1, hidden_width), f32),
             jax.ShapeDtypeStruct((rows, WIDTH), bf16),
         ]
-        + kv_shapes
-        + scaled_shapes
-        + [edge, edge, jax.ShapeDtypeStruct((BLOCK, ENTRY), bf16)],
+        + [jax.ShapeDtypeStruct((entries, 2 * WIDTH), bf16), jax.ShapeDtypeStruct((entries, WIDTH), bf16)]
+        + [edge, edge, jax.ShapeDtypeStruct((BLOCK // 2, ENTRY), bf16)],
         in_specs=[pl.BlockSpec(memory_space=pltpu.SMEM), tiled(tile, WIDTH)]
         + vmem_specs(owners)
-        + [pl.BlockSpec(memory_space=pl.ANY)],
-        out_specs=vmem_specs(3) + [tiled(tile, WIDTH)] + kv_specs + scaled_specs + vmem_specs(3),
+        + [pl.BlockSpec(memory_space=pl.ANY)] * 2,
+        out_specs=vmem_specs(3) + [tiled(tile, WIDTH)] + vmem_specs(5),
         scratch_shapes=[pltpu.VMEM((level_rows(rows, 4), ENTRY), bf16)],
-        compiler_params=pltpu.CompilerParams(vmem_limit_bytes=VMEM_LIMIT),
+        compiler_params=pltpu.CompilerParams(vmem_limit_bytes=56 << 20),
         cost_estimate=pl.CostEstimate(flops=9 << 30, bytes_accessed=12 << 20, transcendentals=0),
         name="qkv_levels",
-    )(meta, x, *pieces, earlier)
+    )(meta, x, *pieces, *earlier)
     return outs
 
 
@@ -330,19 +332,23 @@
     return dot_nn(pool_matrix(entries.shape[0]), entries).astype(bf16)
 
 
-def assemble(rows, far, here, columns, level_refs, left_ref, right_ref, base_ref, ext_ref, far_ref):
+def assemble(rows, far, here, columns, own_ref, left_ref, right_ref, base_ref, ext_ref, far_ref):
     offsets, _ = extended_offsets(rows, far)
+    places, _ = level_offsets(rows)
     for inner, outer, target, width in columns:
         lanes, edge_lanes = slice(target, target + width), slice(outer, outer + width)
         for level in range(LOCAL):
             at, count = offsets[level], level_rows(rows, level)
             edge = slice(BLOCK * level, BLOCK * (level + 1))
             ext_ref[at : at + BLOCK, lanes] = left_ref[edge, edge_lanes]
-            ext_ref[at + BLOCK : at + BLOCK + count, lanes] = level_refs[level][:, inner : inner + width]
+            ext_ref[at + BLOCK : at + BLOCK + count, lanes] = own_ref[
+                places[level] : places[level] + count, inner : inner + width
+            ]
             ext_ref[at + BLOCK + count : at + 2 * BLOCK + count, lanes] = right_ref[edge, edge_lanes]
         current = base_ref[:, edge_lanes]
         for index, level in enumerate(far):
-            current = far_level(current)
+            if index:
+                current = far_level(current)
             count = current.shape[0]
             far_ref[0:count, 0:width] = current
             for side, start in enumerate(far_starts(here, level, count)):
@@ -366,14 +372,13 @@
 
 
 def attend_kernel(rows, far, meta_ref, q_ref, bias_ref, *refs):
-    level_refs, refs = refs[:LOCAL], refs[LOCAL:]
-    left_ref, right_ref, base_ref, out_ref, log_ref, ext_ref, far_ref, slots_ref = refs
+    own_ref, left_ref, right_ref, base_ref, out_ref, log_ref, ext_ref, far_ref, slots_ref = refs
     chunk = pl.program_id(0)
 
     @pl.when(chunk == 0)
     def _():
         columns = [(0, 0, 0, 2 * WIDTH)]
-        assemble(rows, far, meta_ref[0], columns, level_refs, left_ref, right_ref, base_ref, ext_ref, far_ref)
+        assemble(rows, far, meta_ref[0], columns, own_ref, left_ref, right_ref, base_ref, ext_ref, far_ref)
 
     load_slots(rows, far, chunk, ext_ref, slots_ref)
     bias = bias_ref[0]
@@ -390,7 +395,7 @@
         log_ref[0, pair : pair + 1, :] = top + jnp.log(total)
 
 
-def attend_call(rows, devices, far, meta, q, bias, levels, left, right, base):
+def attend_call(rows, devices, far, meta, q, bias, kv, left, right, base):
     chunks = rows // CHUNK
     _, entries = extended_offsets(rows, far)
     _, slots = slot_layout(far)
@@ -406,7 +411,7 @@
             pl.BlockSpec((CHUNK, WIDTH), lambda i: (i, 0)),
             pl.BlockSpec((1, slots, CHUNK), lambda i: (i, 0, 0)),
         ]
-        + vmem_specs(LOCAL + 3),
+        + vmem_specs(4),
         out_specs=[
             pl.BlockSpec((CHUNK, WIDTH), lambda i: (i, 0)),
             pl.BlockSpec((1, 8, 2 * CHUNK), lambda i: (i, 0, 0)),
@@ -416,10 +421,10 @@
             pltpu.VMEM((8 * devices, 2 * WIDTH), bf16),
             pltpu.VMEM((slots, 2 * WIDTH), bf16),
         ],
-        compiler_params=pltpu.CompilerParams(vmem_limit_bytes=VMEM_LIMIT),
+        compiler_params=pltpu.CompilerParams(vmem_limit_bytes=56 << 20),
         cost_estimate=pl.CostEstimate(flops=20 << 30, bytes_accessed=12 << 20, transcendentals=4 << 20),
         name="attend",
-    )(meta, q, bias, *levels, left, right, base)
+    )(meta, q, bias, kv, left, right, base)
 
 
 def column_sum(values):
@@ -455,7 +460,7 @@
     refs = list(refs)
     take = lambda count: [refs.pop(0) for _ in range(count)]
     meta_ref, q_ref, grad_ref, bias_ref, log_ref = take(5)
-    level_refs, scaled_refs = take(LOCAL), take(LOCAL)
+    own_ref, own_scaled_ref = take(2)
     left_ref, right_ref, base_ref, w_ref, vec_ref = take(5)
     dq_ref, local_ref, to_left_ref, to_right_ref, far_keep_ref, far_send_ref, keep_ref, send_ref = take(8)
     ext_ref, far_ref, slots_ref, acc_ref, tree_ref, scaled_ref, dq_keep_ref = take(7)
@@ -465,8 +470,8 @@
     @pl.when(chunk == 0)
     def _():
         common = (left_ref, right_ref, base_ref)
-        assemble(rows, far, meta_ref[0], [(0, 0, 0, 2 * WIDTH)], level_refs, *common, ext_ref, far_ref)
-        assemble(rows, far, meta_ref[0], [(0, 2 * WIDTH, 0, WIDTH)], scaled_refs, *common, scaled_ref, far_ref)
+        assemble(rows, far, meta_ref[0], [(0, 0, 0, 2 * WIDTH)], own_ref, *common, ext_ref, far_ref)
+        assemble(rows, far, meta_ref[0], [(0, 2 * WIDTH, 0, WIDTH)], own_scaled_ref, *common, scaled_ref, far_ref)
         acc_ref[...] = jnp.zeros_like(acc_ref)
 
     load_slots(rows, far, chunk, ext_ref, slots_ref)
@@ -500,7 +505,7 @@
         dq = dq_keep_ref[...]
         sums = [column_sum(dq.astype(f32)), column_sum(acc_ref[:, :WIDTH]), column_sum(acc_ref[:, WIDTH:])]
         both = dot_tn(scaled_ref[...], acc_ref[...].astype(bf16))
-        parts = [dot_tn(scaled_refs[0][...], dq), both[:, :WIDTH], both[:, WIDTH:]]
+        parts = [dot_tn(own_scaled_ref[0:rows, :], dq), both[:, :WIDTH], both[:, WIDTH:]]
         first_row = lax.broadcasted_iota(jnp.int32, (16, 1), 0) == 0
         ones = jnp.where(first_row, jnp.ones((16, WIDTH), f32), 0.0).astype(bf16)
         as_column = lambda row: dot_tn(jnp.where(first_row, row, 0.0).astype(bf16), ones)
@@ -536,7 +541,7 @@
         carry = None
         for index in range(len(far) - 1, -1, -1):
             level = far[index]
-            count = base_ref.shape[0] // 2 ** (level - LOCAL + 1)
+            count = base_ref.shape[0] // 2 ** (level - LOCAL)
             tree_ref[0:count, :] = jnp.zeros((count, 2 * WIDTH), f32) if carry is None else spread(carry)
             for side, start in enumerate(far_starts(meta_ref[0], level, count)):
                 at = offsets[LOCAL + index] + side * BLOCK
@@ -545,18 +550,26 @@
         mine, other = choose_groups(meta_ref[0] & 1, jnp.concatenate([carry[:, :WIDTH], carry[:, WIDTH:]], axis=0))
         far_keep_ref[...] = mine.astype(bf16)
         far_send_ref[...] = other.astype(bf16)
-        for level in range(LOCAL - 1, 0, -1):
-            at, count = offsets[level] + BLOCK, level_rows(rows, level)
-            below = offsets[level - 1] + BLOCK
-            tile = min(count, 128)
-            for row in range(0, count, tile):
-                carry = spread(acc_ref[at + row : at + row + tile, :])
-                target = slice(below + 2 * row, below + 2 * (row + tile))
-                total = acc_ref[target, :] + carry
-                if level == 1:
-                    local_ref[2 * row : 2 * (row + tile), :] = total
-                else:
-                    acc_ref[target, :] = total
+        tile = 256
+        counts = [tile >> level for level in range(1, LOCAL - 1)]
+        token = lax.broadcasted_iota(jnp.int32, (tile, counts[0]), 0)
+        entry = lax.broadcasted_iota(jnp.int32, (tile, counts[0]), 1)
+        member = jnp.concatenate(
+            [
+                jnp.where((token >> level) == entry, 0.5**level, 0.0)[:, :count]
+                for level, count in enumerate(counts, 1)
+            ],
+            axis=1,
+        ).astype(bf16)
+        for at in range(0, rows, tile):
+            coarse = [
+                acc_ref[offsets[level] + BLOCK + (at >> level) : offsets[level] + BLOCK + ((at + tile) >> level), :]
+                for level in range(1, LOCAL - 1)
+            ]
+            total = acc_ref[BLOCK + at : BLOCK + at + tile, :]
+            for half in two_parts(jnp.concatenate(coarse, axis=0)):
+                total = total + dot_nn(member, half)
+            local_ref[at : at + tile, :] = total.astype(bf16)
 
 
 def chain_rows(rows, devices):
@@ -564,14 +577,14 @@
     return -(-(rows + 16) // unit) * unit
 
 
-def attend_back_call(rows, devices, far, owners, meta, q, grads, bias, logs, levels, scaled, left, right, base, weight, vectors):
+def attend_back_call(rows, devices, far, owners, meta, q, grads, bias, logs, kv, scaled, left, right, base, weight, vectors):
     chunks = rows // CHUNK
     _, entries = extended_offsets(rows, far)
     _, slots = slot_layout(far)
     chain = (owners // 2, chain_rows(3 * WIDTH // owners, devices), WIDTH)
     outs = [
         jax.ShapeDtypeStruct((rows, WIDTH), bf16),
-        jax.ShapeDtypeStruct((rows, 2 * WIDTH), f32),
+        jax.ShapeDtypeStruct((rows, 2 * WIDTH), bf16),
         jax.ShapeDtypeStruct((BLOCK * LOCAL, 2 * WIDTH), bf16),
         jax.ShapeDtypeStruct((BLOCK * LOCAL, 2 * WIDTH), bf16),
         jax.ShapeDtypeStruct((8 * devices, WIDTH), bf16),
@@ -590,7 +603,7 @@
             pl.BlockSpec((1, slots, CHUNK), lambda i: (i, 0, 0)),
             pl.BlockSpec((1, 8, 2 * CHUNK), lambda i: (i, 0, 0)),
         ]
-        + vmem_specs(2 * LOCAL + 5),
+        + vmem_specs(7),
         out_specs=[pl.BlockSpec((CHUNK, WIDTH), lambda i: (i, 0))] + vmem_specs(len(outs) - 1),
         scratch_shapes=[
             pltpu.VMEM((entries, 2 * WIDTH), bf16),
@@ -601,10 +614,10 @@
             pltpu.VMEM((entries, WIDTH), bf16),
             pltpu.VMEM((rows, WIDTH), bf16),
         ],
-        compiler_params=pltpu.CompilerParams(vmem_limit_bytes=VMEM_LIMIT),
+        compiler_params=pltpu.CompilerParams(vmem_limit_bytes=40 << 20),
         cost_estimate=pl.CostEstimate(flops=36 << 30, bytes_accessed=24 << 20, transcendentals=4 << 20),
         name="attend_back",
-    )(meta, q, grads, bias, logs, *levels, *scaled, left, right, base, weight, vectors)
+    )(meta, q, grads, bias, logs, kv, scaled, left, right, base, weight, vectors)
 
 
 def normal_parts(values):
@@ -633,26 +646,18 @@
     one_refs, two_refs, refs = refs[:owners], refs[owners : 2 * owners], refs[2 * owners :]
     y_ref, grad_middle_ref, grad_attended_ref, keep_ref, send_ref = refs[:5]
     down_w_ref, up_w_ref, out_w_ref, vec_grad_ref, up_bias_grad_ref, down_acc, up_acc, out_acc = refs[5:]
-    step = pl.program_id(0)
     rows = WIDTH // owners
     wide_rows = hidden_width // owners
     blocks = hidden_width // WIDTH
 
-    @pl.when(step == 0)
-    def _():
-        for at, (one, two) in enumerate(zip(one_refs, two_refs)):
-            owner = meta_ref[1 + at]
-            span = pl.ds(pl.multiple_of(owner * rows, rows), rows)
-            for block in range(blocks - 1):
-                up_w_ref[span, block * WIDTH : (block + 1) * WIDTH] = one[block * rows : (block + 1) * rows, :]
-            up_w_ref[span, (blocks - 1) * WIDTH :] = two[0:rows, :]
-            out_w_ref[span, :] = two[rows : 2 * rows, :]
-            down_w_ref[pl.ds(pl.multiple_of(owner * wide_rows, wide_rows), wide_rows), :] = two[2 * rows :, :]
-        down_acc[...] = jnp.zeros_like(down_acc)
-        up_acc[...] = jnp.zeros_like(up_acc)
-        out_acc[...] = jnp.zeros_like(out_acc)
-        vec_grad_ref[...] = jnp.zeros_like(vec_grad_ref)
-        up_bias_grad_ref[...] = jnp.zeros_like(up_bias_grad_ref)
+    for at, (one, two) in enumerate(zip(one_refs, two_refs)):
+        owner = meta_ref[1 + at]
+        span = pl.ds(pl.multiple_of(owner * rows, rows), rows)
+        for block in range(blocks - 1):
+            up_w_ref[span, block * WIDTH : (block + 1) * WIDTH] = one[block * rows : (block + 1) * rows, :]
+        up_w_ref[span, (blocks - 1) * WIDTH :] = two[0:rows, :]
+        out_w_ref[span, :] = two[rows : 2 * rows, :]
+        down_w_ref[pl.ds(pl.multiple_of(owner * wide_rows, wide_rows), wide_rows), :] = two[2 * rows :, :]
 
     out_bias, gain, shift, down_bias = (vec_ref[4 + at : 5 + at, :] for at in range(4))
     attended = attended_ref[...]
@@ -671,57 +676,52 @@
         hidden = (pre * phi).astype(bf16)
         lowered += dot_nn(hidden, down)
         grad_pre = (dot_nt(cot, down) * (phi + pre * bell)).astype(bf16)
-        up_bias_grad_ref[:, columns] += column_sum(grad_pre.astype(f32))
+        up_bias_grad_ref[:, columns] = column_sum(grad_pre.astype(f32))
         grad_normed += dot_nt(grad_pre, up_w_ref[:, columns])
-        down_acc[columns, :] += dot_tn(hidden, cot)
-        up_acc[:, columns] += dot_tn(normed, grad_pre)
+        down_acc[columns, :] = dot_tn(hidden, cot)
+        up_acc[:, columns] = dot_tn(normed, grad_pre)
     y_ref[...] = (middle + lowered + down_bias).astype(bf16)
     grad_middle = wide + norm_back(grad_normed, scaled, inverse, gain)
     grad_middle_ref[...] = grad_middle
     grad_proj = grad_middle.astype(bf16)
     grad_attended_ref[...] = dot_nt(grad_proj, out_w_ref[...]).astype(bf16)
-    out_acc[...] += dot_tn(attended, grad_proj)
-    vec_grad_ref[0:1, :] += column_sum(grad_proj.astype(f32))
-    vec_grad_ref[1:2, :] += column_sum(grad_normed * scaled)
-    vec_grad_ref[2:3, :] += column_sum(grad_normed)
-    vec_grad_ref[3:4, :] += column_sum(wide)
-
-    @pl.when(step == pl.num_programs(0) - 1)
-    def _():
-        extra = keep_ref.shape[1] - wide_rows - (blocks + 1) * rows
-        row_at = lax.broadcasted_iota(jnp.int32, (extra, 1), 0)
-        low_bit = meta_ref[1] & 1
-
-        def put(high, at, count, source):
-            mine, other = choose(low_bit, source(2 * high), source(2 * high + 1))
-            keep_ref[high, at : at + count, :] = mine.astype(bf16)
-            send_ref[high, at : at + count, :] = other.astype(bf16)
-
-        def small(owner):
-            first = [vec_grad_ref[i : i + 1, owner * rows : (owner + 1) * rows] for i in range(4)]
-            second = up_bias_grad_ref[:, owner * wide_rows : (owner + 1) * wide_rows]
-            return jnp.where(row_at == 0, jnp.concatenate(first, axis=1), jnp.where(row_at == 1, second, 0.0))
-
-        for high in range(owners // 2):
-            put(high, 0, wide_rows, lambda owner: down_acc[owner * wide_rows : (owner + 1) * wide_rows, :])
-            at = wide_rows
-            for block in range(blocks):
-                columns = slice(block * WIDTH, (block + 1) * WIDTH)
-                put(high, at, rows, lambda owner: up_acc[owner * rows : (owner + 1) * rows, columns])
-                at += rows
-            put(high, at, rows, lambda owner: out_acc[owner * rows : (owner + 1) * rows, :])
-            put(high, at + rows, extra, small)
+    out_acc[...] = dot_tn(attended, grad_proj)
+    vec_grad_ref[0:1, :] = column_sum(grad_proj.astype(f32))
+    vec_grad_ref[1:2, :] = column_sum(grad_normed * scaled)
+    vec_grad_ref[2:3, :] = column_sum(grad_normed)
+    vec_grad_ref[3:4, :] = column_sum(wide)
+
+    extra = keep_ref.shape[1] - wide_rows - (blocks + 1) * rows
+    row_at = lax.broadcasted_iota(jnp.int32, (extra, 1), 0)
+    low_bit = meta_ref[1] & 1
+
+    def put(high, at, count, source):
+        mine, other = choose(low_bit, source(2 * high), source(2 * high + 1))
+        keep_ref[high, at : at + count, :] = mine.astype(bf16)
+        send_ref[high, at : at + count, :] = other.astype(bf16)
+
+    def small(owner):
+        first = [vec_grad_ref[i : i + 1, owner * rows : (owner + 1) * rows] for i in range(4)]
+        second = up_bias_grad_ref[:, owner * wide_rows : (owner + 1) * wide_rows]
+        return jnp.where(row_at == 0, jnp.concatenate(first, axis=1), jnp.where(row_at == 1, second, 0.0))
+
+    for high in range(owners // 2):
+        put(high, 0, wide_rows, lambda owner: down_acc[owner * wide_rows : (owner + 1) * wide_rows, :])
+        at = wide_rows
+        for block in range(blocks):
+            columns = slice(block * WIDTH, (block + 1) * WIDTH)
+            put(high, at, rows, lambda owner: up_acc[owner * rows : (owner + 1) * rows, columns])
+            at += rows
+        put(high, at, rows, lambda owner: out_acc[owner * rows : (owner + 1) * rows, :])
+        put(high, at + rows, extra, small)
 
 
 def feed_call(hidden_width, devices, meta, x, attended, cot, vectors, up_bias, ones, twos):
     rows, owners = x.shape[0], len(ones)
-    tile = 256
-    row_spec = pl.BlockSpec((tile, WIDTH), lambda i: (i, 0))
     chain = chain_rows(2 * (hidden_width // owners) + WIDTH // owners, devices)
     split = jax.ShapeDtypeStruct((owners // 2, chain, WIDTH), bf16)
     return pl.pallas_call(
         partial(feed_kernel, hidden_width, owners),
-        grid=(rows // tile,),
         out_shape=[
             jax.ShapeDtypeStruct((rows, WIDTH), bf16),
             jax.ShapeDtypeStruct((rows, WIDTH), f32),
@@ -729,8 +729,8 @@
             split,
             split,
         ],
-        in_specs=[pl.BlockSpec(memory_space=pltpu.SMEM), row_spec, row_spec, row_spec] + vmem_specs(2 + 2 * owners),
-        out_specs=[row_spec, row_spec, row_spec] + vmem_specs(2),
+        in_specs=[pl.BlockSpec(memory_space=pltpu.SMEM)] + vmem_specs(5 + 2 * owners),
+        out_specs=vmem_specs(5),
         scratch_shapes=[
             pltpu.VMEM((hidden_width, WIDTH), bf16),
             pltpu.VMEM((WIDTH, hidden_width), bf16),
@@ -741,16 +741,17 @@
             pltpu.VMEM((WIDTH, hidden_width), f32),
             pltpu.VMEM((WIDTH, WIDTH), f32),
         ],
-        compiler_params=pltpu.CompilerParams(vmem_limit_bytes=VMEM_LIMIT),
+        compiler_params=pltpu.CompilerParams(vmem_limit_bytes=46 << 20),
         cost_estimate=pl.CostEstimate(flops=32 << 30, bytes_accessed=20 << 20, transcendentals=4 << 20),
         name="feed_forward",
     )(meta, x, attended, cot, vectors, up_bias, *ones, *twos)
 
 
 def input_grad_kernel(
+    rows,
     x_ref,
-    dq_refs,
-    local_refs,
+    dq_ref,
+    local_ref,
     grad_middle_ref,
     from_right_ref,
     from_left_ref,
@@ -759,66 +760,54 @@
     w_ref,
     vec_ref,
     out_ref,
-    tree_ref,
+    got_ref,
 ):
-    rows = tree_ref.shape[0]
     step = pl.program_id(0)
     tile = x_ref.shape[0]
+    edge = BLOCK * LOCAL
 
     @pl.when(step == 0)
     def _():
         folded = far_keep_ref[...].astype(f32) + far_got_ref[...].astype(f32)
-        carry = spread(jnp.concatenate([folded[:8], folded[8:]], axis=1))
-        for level in range(LOCAL - 1, -1, -1):
-            count = level_rows(rows, level)
-            edge = slice(BLOCK * level, BLOCK * (level + 1))
-            if level == LOCAL - 1:
-                tree_ref[0:count, :] = carry
-            tree_ref[0:BLOCK, :] += from_left_ref[edge, :].astype(f32)
-            tree_ref[count - BLOCK : count, :] += from_right_ref[edge, :].astype(f32)
-            if level:
-                part = min(count, 128)
-                for row in range(count - part, -1, -part):
-                    tree_ref[2 * row : 2 * (row + part), :] = spread(tree_ref[row : row + part, :])
-
-    span = pl.ds(pl.multiple_of(step * tile, tile), tile)
+        high, low = two_parts(jnp.concatenate([folded[:8], folded[8:]], axis=1))
+        got_ref[0:edge, :] = from_left_ref[...]
+        got_ref[edge : 2 * edge, :] = from_right_ref[...]
+        far = jnp.concatenate([high.astype(f32), low.astype(f32)], axis=0).astype(bf16)
+        got_ref[2 * edge : 2 * edge + BLOCK, :] = far
+        got_ref[2 * edge + BLOCK :, :] = jnp.zeros((BLOCK, 2 * WIDTH), bf16)
+
+    shape = (1, got_ref.shape[0])
+    column = lax.broadcasted_iota(jnp.int32, shape, 1)
+    within = jnp.where(column < edge, column, column - edge)
+    level = jnp.where(column < 2 * edge, within >> 4, LOCAL)
+    last = jnp.where((column >= edge) & (column < 2 * edge), (rows >> level) - BLOCK, 0)
+    entry = jnp.where(column < 2 * edge, last + (within & 15), (column - 2 * edge) & 7)
+    entry = jnp.where(column < 2 * edge + BLOCK, entry, -1)
+    scale = 1.0 / (1 << level).astype(f32)
+    token = step * tile + lax.broadcasted_iota(jnp.int32, (tile, shape[1]), 0)
+    member = jnp.where((token >> level) == entry, scale, 0.0).astype(bf16)
+
     scaled, inverse = norm_rows(x_ref[...].astype(f32))
-    grad = jnp.zeros((tile, WIDTH), f32)
-    half = dq_refs[0].shape[1]
-    for index, (dq_ref, local_ref) in enumerate(zip(dq_refs, local_refs)):
-        lane = index * half
-        grad += dot_nt(dq_ref[...], w_ref[:, lane : lane + half])
-        for block in range(2):
-            column = block * WIDTH + lane
-            dkv = (local_ref[:, block * half : (block + 1) * half] + tree_ref[span, column : column + half]).astype(bf16)
-            grad += dot_nt(dkv, w_ref[:, WIDTH + column : WIDTH + column + half])
+    dkv = (local_ref[...].astype(f32) + dot_nn(member, got_ref[...])).astype(bf16)
+    grad = dot_nt(dq_ref[...], w_ref[:, :WIDTH]) + dot_nt(dkv, w_ref[:, WIDTH:])
     out_ref[...] = grad_middle_ref[...] + norm_back(grad, scaled, inverse, vec_ref[0:1, :])
 
 
-def input_grad_call(x, dqs, locals_, grad_middle, from_right, from_left, far_keep, far_got, weight, vectors):
+def input_grad_call(x, dq, local, grad_middle, from_right, from_left, far_keep, far_got, weight, vectors):
     rows = x.shape[0]
-    tile = 256
-    count = len(dqs)
+    tile = 512
     tiled = lambda width: pl.BlockSpec((tile, width), lambda i: (i, 0))
-
-    def kernel(x_ref, *refs):
-        input_grad_kernel(x_ref, refs[:count], refs[count : 2 * count], *refs[2 * count :])
-
     return pl.pallas_call(
-        kernel,
+        partial(input_grad_kernel, rows),
         grid=(rows // tile,),
         out_shape=jax.ShapeDtypeStruct((rows, WIDTH), f32),
-        in_specs=[tiled(WIDTH)]
-        + [tiled(d.shape[1]) for d in dqs]
-        + [tiled(d.shape[1]) for d in locals_]
-        + [tiled(WIDTH)]
-        + vmem_specs(6),
+        in_specs=[tiled(WIDTH), tiled(WIDTH), tiled(2 * WIDTH), tiled(WIDTH)] + vmem_specs(6),
         out_specs=tiled(WIDTH),
-        scratch_shapes=[pltpu.VMEM((rows, 2 * WIDTH), f32)],
-        compiler_params=pltpu.CompilerParams(vmem_limit_bytes=VMEM_LIMIT),
-        cost_estimate=pl.CostEstimate(flops=8 << 30, bytes_accessed=14 << 20, transcendentals=0),
+        scratch_shapes=[pltpu.VMEM((2 * BLOCK * (LOCAL + 1), 2 * WIDTH), bf16)],
+        compiler_params=pltpu.CompilerParams(vmem_limit_bytes=24 << 20),
+        cost_estimate=pl.CostEstimate(flops=6 << 30, bytes_accessed=12 << 20, transcendentals=0),
         name="input_grad",
-    )(x, *dqs, *locals_, grad_middle, from_right, from_left, far_keep, far_got, weight, vectors)
+    )(x, dq, local, grad_middle, from_right, from_left, far_keep, far_got, weight, vectors)
 
 
 def shifted(block, axis, distance):
@@ -836,7 +825,7 @@
     other = swap(part, axis, bit)
     first = jnp.where(mine == 0, part, other)
     second = jnp.where(mine == 0, other, part)
-    return jnp.concatenate([first, second], axis=0)
+    return jnp.stack([first, second], axis=-3)
 
 
 def together(*values):
@@ -860,7 +849,7 @@
         out_shape=[jax.ShapeDtypeStruct(shape, dtype) for shape in shapes],
         in_specs=[pl.BlockSpec(memory_space=pltpu.SMEM)] + vmem_specs(len(arrays)),
         out_specs=vmem_specs(len(shapes)),
-        compiler_params=pltpu.CompilerParams(vmem_limit_bytes=VMEM_LIMIT),
+        compiler_params=pltpu.CompilerParams(vmem_limit_bytes=(4 << 20) + 16 * size),
         cost_estimate=pl.CostEstimate(flops=1 << 20, bytes_accessed=4 * size, transcendentals=0),
         name=name,
     )(meta, *arrays)
@@ -923,34 +912,54 @@
         if far:
             self.far = (out[2], None)
 
+
+    def order(self):
+        high = list(reversed(self.bits[:-1]))
+        return list(zip(high + [1], [1] + high))
+
+    def collect(self):
+        rows = self.keep.shape[0]
+        if self.far:
+            self.far = (self.far[0], self.got[0][rows:])
+        function = lambda here, owner, keep, got: halves(keep + got[:rows])
+        self.send_gather(0, self.call("collect", function, [self.keep, *self.got], (rows // 2,), (rows // 2,)))
+
+    def send_gather(self, at, keep):
+        self.keep = keep
+        self.got = [swap(part, "ctx", bit) for part, bit in zip(keep, self.order()[at])]
+
     def gather(self, at):
-        rows = self.keep.shape[0]
-        bit = self.bits[at]
-        last = at == len(self.bits) - 1
-        if last and self.far:
-            self.far = (self.far[0], self.got[0][rows:])
-
-        def function(here, owner, keep, got):
-            if last:
-                return [keep + got[:rows]]
-            return [jnp.concatenate(choose((here // bit) & 1, keep, got), axis=0)]
-
-        (self.keep,) = self.call("gather", function, [self.keep, *self.got], (rows if last else 2 * rows,))
-        self.got = [swap(self.keep, "ctx", self.bits[at - 1] if at else 1)]
-
-    def steps(self):
-        count = len(self.bits)
-        return (
-            [self.cross]
-            + [partial(self.scatter, at) for at in range(count)]
-            + [partial(self.gather, at) for at in range(count - 1, -1, -1)]
-        )
+        bits = self.order()[at]
+        rows = 2 * self.keep[0].shape[0]
+        function = lambda here, owner, *arrays: self.paired(here, bits, *arrays)
+        self.send_gather(at + 1, self.call("gather", function, [*self.keep, *self.got], (rows,), (rows,)))
+
+    def paired(self, here, bits, keep_one, keep_two, got_one, got_two):
+        one = jnp.concatenate(choose((here // bits[0]) & 1, keep_one, got_one), axis=0)
+        two = jnp.concatenate(choose((here // bits[1]) & 1, keep_two, got_two), axis=0)
+        return one, two
+
+    def scatters(self):
+        return [self.cross] + [partial(self.scatter, at) for at in range(len(self.bits))]
+
+    def gathers(self):
+        return [self.collect] + [partial(self.gather, at) for at in range(len(self.order()) - 1)]
 
     def finish(self, shapes, unpack):
-        def function(here, owner, keep, got):
-            return unpack(jnp.concatenate(choose(here & 1, keep, got), axis=0))
-
-        return step_call("finish", function, self.meta, [self.keep, *self.got], shapes, f32)
+        bits = self.order()[-1]
+        outer = lax.axis_size("ctx") // 4
+        rows = self.rows // (4 * outer)
+
+        def function(here, owner, *arrays):
+            one, two = self.paired(here, bits, *arrays)
+            parts = []
+            for low in range(2):
+                for high in range(outer):
+                    a, b = low * outer + high, 2 * high + low
+                    parts += [one[a * rows : (a + 1) * rows], two[b * rows : (b + 1) * rows]]
+            return unpack(jnp.concatenate(parts, axis=0))
+
+        return step_call("finish", function, self.meta, [*self.keep, *self.got], shapes, f32)
 
 
 def shards(
@@ -991,24 +1000,24 @@
     across, beside, one, two, bias = together(across, beside, one, two, bias)
     pieces = [own, beside, across, swap(across, "fsdp", 1)]
     one_across = swap(one, "fsdp", 2)
-    *made, one_across = together(*qkv_call(rows, hidden_width, meta, x, pieces, bias), one_across)
-    qkv_full, vec, up_shift, queries = made[:4]
-    levels, scaled, (tail, head, base) = made[4 : 4 + LOCAL], made[4 + LOCAL : 4 + 2 * LOCAL], made[4 + 2 * LOCAL :]
-
-    two, one, tail, head, base = together(two, one, tail, head, base)
-    two_across = swap(two, "fsdp", 2)
+    qkv_full, vec, up_shift, queries, kv, scaled, tail, head, base = qkv_call(
+        rows, hidden_width, meta, x, pieces, [bias, two]
+    )
+    vec, tail, head, base, one_across = together(vec, tail, head, base, one_across)
+
     one_beside, one_both = swap(one, "fsdp", 1), swap(one_across, "fsdp", 1)
     left = shifted(tail, "ctx", 1)
     right = shifted(head, "ctx", -1)
-    for at, bit in enumerate(bits_of("ctx")):
+    for at, bit in enumerate(reversed(bits_of("ctx"))):
         base = gather_step(base, "ctx", bit)
-        if at == 0:
+        if bit == 1:
             base, left, right = together(base, left, right)
-    base, one_beside, one_both, two_across = together(base, one_beside, one_both, two_across)
-
-    two_beside, two_both = swap(two, "fsdp", 1), swap(two_across, "fsdp", 1)
-    attended, logs = attend_call(rows, devices, far, meta, queries, bias, levels, left, right, base)
-    attended, logs, two_beside, two_both = together(attended, logs, two_beside, two_both)
+    base = base.reshape(-1, ENTRY)
+    base, two = together(base, two)
+    two_across, two_beside = swap(two, "fsdp", 2), swap(two, "fsdp", 1)
+    attended, logs = attend_call(rows, devices, far, meta, queries, bias, kv, left, right, base)
+    logs, two_across, two_beside = together(logs, two_across, two_beside)
+    two_both = swap(two_across, "fsdp", 1)
     output, grad_middle, grad_attended, keep, send = feed_call(
         hidden_width,
         devices,
@@ -1022,32 +1031,41 @@
         [two, two_beside, two_across, two_both],
     )
     feed = Reduction(meta, keep, send)
-    todo = feed.steps()
-    todo.pop(0)()
-    grad_attended, feed.keep = together(grad_attended, feed.keep)
+    feed.cross()
     made = attend_back_call(
-        rows, devices, far, owners, meta, queries, grad_attended, bias, logs, levels, scaled, left, right, base, qkv_full, vec
+        rows, devices, far, owners, meta, queries, grad_attended, bias, logs, kv, scaled, left, right, base, qkv_full, vec
     )
-    count = len(made)
-    made = together(*made, *feed.got)
-    feed.got = list(made[count:])
-    dq, local, to_left, to_right, far_keep, far_send, keep, send = made[:count]
+    dq, local, to_left, to_right, far_keep, far_send, keep, send = made
+    to_left, to_right, far_keep, far_send, send, *feed.got = together(
+        to_left, to_right, far_keep, far_send, send, *feed.got
+    )
     first = Reduction(meta, keep, send, (far_keep, far_send))
     back_right = shifted(to_left, "ctx", -1)
     back_left = shifted(to_right, "ctx", 1)
-    for one, two in zip(first.steps(), todo + [None]):
-        if two:
-            two()
+    pending = feed.scatters()[1:]
+    pending.pop(0)()
+    first.cross()
+    tied = together(*first.got, *feed.got)
+    first.got, feed.got = list(tied[: len(first.got)]), list(tied[len(first.got) :])
+    for one in first.scatters()[1:]:
         one()
+        if pending:
+            pending.pop(0)()
+    for one, two in zip(first.gathers(), feed.gathers()):
+        one()
+        two()
     input_grad = input_grad_call(
-        x, [dq], [local], grad_middle, back_right, back_left, *first.far, qkv_full, vec
+        x, dq, local, grad_middle, back_right, back_left, *first.far, qkv_full, vec
     )
 
     wide_rows = hidden_width // owners
+
+    def split(row):
+        return [row[:, at * part : (at + 1) * part] for at in range(row.shape[1] // part)]
 
     def unpack_first(total):
         blocks = [total[at * part : (at + 1) * part] for at in range(3)]
-        return [jnp.concatenate(blocks, axis=1), total[3 * part : 3 * part + 1]]
+        return [jnp.concatenate(blocks, axis=1), *split(total[3 * part : 3 * part + 1])]
 
     def unpack_feed(total):
         at = wide_rows
@@ -1055,35 +1073,32 @@
         for _ in range(hidden_width // WIDTH):
             blocks.append(total[at : at + part])
             at += part
-        return [
-            total[:wide_rows],
-            jnp.concatenate(blocks, axis=1),
-            total[at : at + part],
-            total[at + part : at + part + 1],
-            total[at + part + 1 : at + part + 2],
-        ]
-
-    qkv_grad, first_row = first.finish([(part, 3 * WIDTH), (1, WIDTH)], unpack_first)
-    down_grad, up_grad, out_grad, feed_row, up_row = feed.finish(
-        [(wide_rows, WIDTH), (part, hidden_width), (part, WIDTH), (1, WIDTH), (1, WIDTH)], unpack_feed
+        vectors = [*split(total[at + part : at + part + 1]), total[at + part + 1 : at + part + 2]]
+        return [total[:wide_rows], jnp.concatenate(blocks, axis=1), total[at : at + part], *vectors]
+
+    vector = (1, part)
+    qkv_grad, *firsts = first.finish([(part, 3 * WIDTH)] + [vector] * owners, unpack_first)
+    down_grad, up_grad, out_grad, *feeds = feed.finish(
+        [(wide_rows, WIDTH), (part, hidden_width), (part, WIDTH)] + [vector] * owners + [(1, wide_rows)], unpack_feed
     )
-    pick = lambda row, at: row[0, at * part : (at + 1) * part]
+    gain_first, shift_first, query_grad, value_grad = (v.reshape(-1) for v in firsts)
+    out_shift, gain_second, shift_second, down_shift, up_shift_grad = (v.reshape(-1) for v in feeds)
     return (
         output[None],
         input_grad[None],
-        pick(first_row, 0),
-        pick(first_row, 1),
+        gain_first,
+        shift_first,
         qkv_grad,
-        pick(first_row, 2),
-        pick(first_row, 3),
+        query_grad,
+        value_grad,
         out_grad,
-        pick(feed_row, 0),
-        pick(feed_row, 1),
-        pick(feed_row, 2),
+        out_shift,
+        gain_second,
+        shift_second,
         up_grad,
-        up_row[0],
+        up_shift_grad,
         down_grad,
-        pick(feed_row, 3),
+        down_shift,
     )
 
 

time: 263 us -> 235 us (0.89); the launches traced: 262 us -> 230 us
  Pallas kernels: 149 us -> 112 us
  starting transfers between devices: 37.9 us -> 48.3 us
  local copies, waits for them, and re-layouts: 16.9 us -> 11.6 us
    pallas_call x12, Pallas kernels: 27.7 us -> 11.4 us  [step_call(): pl.pallas_call(kernel, out_shape=[jax.ShapeDtypeStruct(shape, dtype) for...]
    pallas_call x2, Pallas kernels: 41.9 us -> 29.7 us  [the longest x1 25.6 us: feed_call(): pl.pallas_call(partial(feed_kernel, hidden_width, owners), out_shape=[jax...]
    ppermute x26 -> x30, starting transfers between devices: 24.4 us -> 35.2 us  [swap(): lax.ppermute(block, axis, [(i, i ^ bit) for i in range(lax.axis_size(axis...]
    pallas_call x1, Pallas kernels: 38.2 us -> 31.6 us  [attend_back_call(): pl.pallas_call(partial(attend_back_kernel, rows, far), grid=(chunks,), ou...]
    unnamed x66 -> x54, local copies, waits for them, and re-layouts: 12.6 us -> 10.8 us
    ppermute x26 -> x30, waiting for transfers between devices: 36.5 us -> 37.3 us  [swap(): lax.ppermute(block, axis, [(i, i ^ bit) for i in range(lax.axis_size(axis...]
  transfers between devices with their start and end apart: 32 -> 36, of which waited for: 14 -> 15; matrix products, arithmetic and copies ran while one was open for 2% -> 0% of each run, Pallas kernels for 41% -> 35%
where the time goes in v4:
time: 235 us; the launch traced here: 230 us
  Pallas kernels  112 us (48%)
  waiting for transfers between devices  55.7 us (24%)
  starting transfers between devices  48.3 us (21%)
  local copies, waits for them, and re-layouts  11.6 us (5%)
    ppermute x30, waiting for transfers between devices, swap(): lax.ppermute(block, axis, [(i, i ^ bit) for i in range(lax.axis_size(axis...  37.3 us
    ppermute x30, starting transfers between devices, swap(): lax.ppermute(block, axis, [(i, i ^ bit) for i in range(lax.axis_size(axis...  35.2 us
    pallas_call x1, Pallas kernels, attend_back_call(): pl.pallas_call(partial(attend_back_kernel, rows, far), grid=(chunks,), ou...  31.6 us
    pallas_call x1, Pallas kernels, feed_call(): pl.pallas_call(partial(feed_kernel, hidden_width, owners), out_shape=[jax...  25.6 us
    pallas_call x1, Pallas kernels, attend_call(): pl.pallas_call(partial(attend_kernel, rows, far), grid=(chunks,), out_sha...  21.1 us
    ppermute x4, waiting for transfers between devices, shifted(): return lax.ppermute(block, axis, route)  12.5 us
    pallas_call x1, Pallas kernels, qkv_call(): pl.pallas_call(partial(qkv_kernel, rows, owners), grid=(rows // tile,), o...  11.9 us
    pallas_call x12, Pallas kernels, step_call(): pl.pallas_call(kernel, out_shape=[jax.ShapeDtypeStruct(shape, dtype) for...  11.4 us
  transfers between devices with their start and end apart: 36, of which 15 were waited for; matrix products, arithmetic and copies ran while one was open for 0% of the time, Pallas kernels for 35%

profile of v4, /device:TPU:0, one launch (start us, length us, event | category | flops | bytes accessed | tf_op | source)
XLA Modules:
  0.0 229.8 jit_solution(17150218511546076650)
XLA Ops:
  3.0 2.5 %collective-permute-start = (bf16[144,1536]{1,0:T(8,128)(2,1)}, bf16[144,1536]{1,0:T(8,128)(2,1)S(1)}, u32[]{:S(2)}, u32[]{:S(2)}) collective-permute-start(bf16[144,1536]{1,0:T(8,128)(2,1)} %pack.1.refs_0_), channel_id=1, source_target_pairs={{0,2},{1,3},{2,0},{3,1},{4,6},{5,7},{6,4},{7,5},{8,10},{9,11},{10,... | collective-permute-start | bytes 1327112 | tf_op jit(solution)/shard_map/ppermute | solution.py:820
  5.5 2.3 pack_rest.1
  11.8 4.7 %collective-permute-done.refs_2_ = bf16[144,1536]{1,0:T(8,128)(2,1)S(1)} collective-permute-done((bf16[144,1536]{1,0:T(8,128)(2,1)}, bf16[144,1536]{1,0:T(8,128)(2,1)S(1)}, u32[]{:S(2)}, u32[]{:S(2)}) %collective-permute-start) | collective-permute-done | bytes 442400 | tf_op jit(solution)/shard_map/ppermute | solution.py:820
  19.2 11.9 %qkv_levels.1 = (bf16[512,1536]{1,0:T(8,128)(2,1)}, f32[8,512]{1,0:T(8,128)}, f32[1,2048]{1,0:T(1,128)}, bf16[1024,512]{1,0:T(8,128)(2,1)}, bf16[2032,1024]{1,0:...) custom-call(s32[5]{0:T(128)} %copy-done.2, ...), custom_call_target="tpu_custom_call" | custom-call | flops 9663676416 | bytes 12582912 | tf_op jit(solution)/shard_map/qkv_levels/pallas_call | solution.py:308
  31.1 2.9 %collective-permute-start.4 = (bf16[8,1536]{1,0:T(8,128)(2,1)}, bf16[8,1536]{1,0:T(8,128)(2,1)S(1)}, u32[]{:S(2)}, u32[]{:S(2)}) collective-permute-start(bf16[8,1536]{1,0:T(8,128)(2,1)} %get-tuple-element.121), channel_id=1, source_target_pairs={{0,16},{4,20},{8,24},{12,28},{16,0},{20,4},{24,8},{28,12},{1,17},{... | collective-permute-start | bytes 73736 | tf_op jit(solution)/shard_map/ppermute | solution.py:820
  34.0 2.1 collective-permute-done.4
  38.7 2.3 %collective-permute-done.5 = bf16[2,8,1536]{2,1,0:T(8,128)(2,1)S(1)} collective-permute-done((bf16[2,8,1536]{2,1,0:T(8,128)(2,1)S(1)}, bf16[2,8,1536]{2,1,0:T(8,128)(2,1)S(1)}, u32[]{:S(2)}, u32[]{:S(2)}) %collective-permute-start.5) | collective-permute-done | bytes 49184 | tf_op jit(solution)/shard_map/ppermute | solution.py:820
  42.8 2.2 collective-permute-start.7
  46.4 12.5 %collective-permute-done.7.refs_1_.refs_7_ = bf16[112,1536]{1,0:T(8,128)(2,1)S(1)} collective-permute-done((bf16[112,1536]{1,0:T(8,128)(2,1)}, bf16[112,1536]{1,0:T(8,128)(2,1)S(1)}, u32[]{:S(2)}, u32[]{:S(2)}) %collective-permute-start.7) | collective-permute-done | bytes 344096 | tf_op jit(solution)/shard_map/ppermute | solution.py:816
  61.4 21.1 %attend.1 = (bf16[1024,512]{1,0:T(8,128)(2,1)}, f32[8,8,256]{2,1,0:T(8,128)}) custom-call(s32[5]{0:T(128)} %copy-done.2, bf16[1024,512]{1,0:T(8,128)(2,1)} %get-tuple-element.114.q_ref.refs_1_, f32[8,528,128]{2,1,0:T(8,128)} %copy-done.13, bf16[2032,1024]{1,0:T(8,128)(2,1)} %get-tuple-element.115.refs_0_.refs_5_, bf16[112,1536]{1,0:T(8,128)(2,1)} %copy-done.7, ...), custom_call_target="tpu_custom_call" | custom-call | flops 21474836480 | bytes 12582912 | tf_op jit(solution)/shard_map/attend/pallas_call | solution.py:402
  87.2 25.6 %feed_forward.1 = (bf16[1024,512]{1,0:T(8,128)(2,1)}, f32[1024,512]{1,0:T(8,128)}, bf16[1024,512]{1,0:T(8,128)(2,1)S(1)}, bf16[2,1216,512]{2,1,0:T(8,128)(2,1)}, bf16[2,1216,512]{2,1,0:T(8,128)(2,1)}) custom-call(s32[5]{0:T(128)S(1)} %copy-done.3, bf16[1024,512]{1,0:T(8,128)(2,1)S(1)} %bitcast.34, bf16[1024,512]{1,0:T(8,128)(2,1)S(1)} %copy-done.18, ...), custom_call_target="tpu_custom_call" | custom-call | flops 34359738368 | bytes 20971520 | tf_op jit(solution)/shard_map/feed_forward/pallas_call | solution.py:723
  114.0 4.7 %collective-permute-done.14.refs_1_ = bf16[2,1216,512]{2,1,0:T(8,128)(2,1)S(1)} collective-permute-done((bf16[2,1216,512]{2,1,0:T(8,128)(2,1)}, bf16[2,1216,512]{2,1,0:T(8,128)(2,1)S(1)}, u32[]{:S(2)}, u32[]{:S(2)}) %collective-permute-start.14) | collective-permute-done | bytes 2490400 | tf_op jit(solution)/shard_map/ppermute | solution.py:820
  122.1 2.4 %collective-permute-start.15 = (bf16[608,512]{1,0:T(8,128)(2,1)S(1)}, bf16[608,512]{1,0:T(8,128)(2,1)S(1)}, u32[]{:S(2)}, u32[]{:S(2)}) collective-permute-start(bf16[608,512]{1,0:T(8,128)(2,1)S(1)} %get-tuple-element.151), channel_id=1, source_target_pairs={{0,4},{4,0},{8,12},{12,8},{16,20},{20,16},{24,28},{28,24},{1,5},{5... | collective-permute-start | bytes 1867784 | tf_op jit(solution)/shard_map/ppermute | solution.py:820
  130.1 31.6 %attend_back.1 = (bf16[1024,512]{1,0:T(8,128)(2,1)S(1)}, bf16[1024,1024]{1,0:T(8,128)(2,1)S(1)}, bf16[112,1024]{1,0:T(8,128)(2,1)S(1)}, bf16[112,1024]{1,0:T(8,1...) custom-call(s32[5]{0:T(128)S(1)} %copy-done.3, ...), custom_call_target="tpu_custom_call" | custom-call | flops 38654705664 | bytes 25165824 | tf_op jit(solution)/shard_map/attend_back/pallas_call | solution.py:595
  162.8 3.0 %collective-permute-start.24 = (bf16[304,512]{1,0:T(8,128)(2,1)S(1)}, bf16[304,512]{1,0:T(8,128)(2,1)S(1)}, u32[]{:S(2)}, u32[]{:S(2)}) collective-permute-start(bf16[304,512]{1,0:T(8,128)(2,1)S(1)} %get-tuple-element.167), channel_id=1, source_target_pairs={{0,8},{4,12},{8,0},{12,4},{16,24},{20,28},{24,16},{28,20},{1,9},{5... | collective-permute-start | bytes 933896 | tf_op jit(solution)/shard_map/ppermute | solution.py:820
  167.9 2.4 %collective-permute-start.23 = (bf16[224,512]{1,0:T(8,128)(2,1)S(1)}, bf16[224,512]{1,0:T(8,128)(2,1)S(1)}, u32[]{:S(2)}, u32[]{:S(2)}) collective-permute-start(bf16[224,512]{1,0:T(8,128)(2,1)S(1)} %get-tuple-element.162), channel_id=1, source_target_pairs={{0,6},{1,7},{2,4},{3,5},{4,2},{5,3},{6,0},{7,1},{8,14},{9,15},{10,... | collective-permute-start | bytes 688136 | tf_op jit(solution)/shard_map/ppermute | solution.py:886
  170.3 3.5 %collective-permute-done.24.refs_1_ = bf16[304,512]{1,0:T(8,128)(2,1)S(1)} collective-permute-done((bf16[304,512]{1,0:T(8,128)(2,1)S(1)}, bf16[304,512]{1,0:T(8,128)(2,1)S(1)}, u32[]{:S(2)}, u32[]{:S(2)}) %collective-permute-start.24) | collective-permute-done | bytes 311328 | tf_op jit(solution)/shard_map/ppermute | solution.py:820
  174.9 5.8 %collective-permute-done.23.refs_3_ = bf16[224,512]{1,0:T(8,128)(2,1)S(1)} collective-permute-done((bf16[224,512]{1,0:T(8,128)(2,1)S(1)}, bf16[224,512]{1,0:T(8,128)(2,1)S(1)}, u32[]{:S(2)}, u32[]{:S(2)}) %collective-permute-start.23) | collective-permute-done | bytes 229408 | tf_op jit(solution)/shard_map/ppermute | solution.py:886
  181.4 2.7 %collective-permute-start.31 = (bf16[304,512]{1,0:T(8,128)(2,1)S(1)}, bf16[304,512]{1,0:T(8,128)(2,1)S(1)}, u32[]{:S(2)}, u32[]{:S(2)}) collective-permute-start(bf16[304,512]{1,0:T(8,128)(2,1)S(1)} %scatter.7.refs_0_), channel_id=1, source_target_pairs={{0,16},{4,20},{8,24},{12,28},{16,0},{20,4},{24,8},{28,12},{1,17},{... | collective-permute-start | bytes 933896 | tf_op jit(solution)/shard_map/ppermute | solution.py:820
  186.3 7.2 %collective-permute-done.25.refs_1_ = bf16[144,512]{1,0:T(8,128)(2,1)S(1)} collective-permute-done((bf16[144,512]{1,0:T(8,128)(2,1)S(1)}, bf16[144,512]{1,0:T(8,128)(2,1)S(1)}, u32[]{:S(2)}, u32[]{:S(2)}) %collective-permute-start.25) | collective-permute-done | bytes 147488 | tf_op jit(solution)/shard_map/ppermute | solution.py:820
  197.5 4.9 %collective-permute-start.19 = (bf16[112,1024]{1,0:T(8,128)(2,1)S(1)}, bf16[112,1024]{1,0:T(8,128)(2,1)S(1)}, u32[]{:S(2)}, u32[]{:S(2)}) collective-permute-start(bf16[112,1024]{1,0:T(8,128)(2,1)S(1)} %get-tuple-element.155), channel_id=1, source_target_pairs={{0,4},{4,8},{8,12},{12,16},{16,20},{20,24},{24,28},{1,5},{5,9},{9,... | collective-permute-start | bytes 688136 | tf_op jit(solution)/shard_map/ppermute | solution.py:816
  207.2 3.8 %collective-permute-done.27.refs_2_ = bf16[56,512]{1,0:T(8,128)(2,1)S(1)} collective-permute-done((bf16[56,512]{1,0:T(8,128)(2,1)S(1)}, bf16[56,512]{1,0:T(8,128)(2,1)S(1)}, u32[]{:S(2)}, u32[]{:S(2)}) %collective-permute-start.27) | collective-permute-done | bytes 57376 | tf_op jit(solution)/shard_map/ppermute | solution.py:820
  211.0 4.1 %collective-permute-done.28.refs_3_ = bf16[56,512]{1,0:T(8,128)(2,1)S(1)} collective-permute-done((bf16[56,512]{1,0:T(8,128)(2,1)S(1)}, bf16[56,512]{1,0:T(8,128)(2,1)S(1)}, u32[]{:S(2)}, u32[]{:S(2)}) %collective-permute-start.28) | collective-permute-done | bytes 57376 | tf_op jit(solution)/shard_map/ppermute | solution.py:820
  220.7 4.1 %input_grad.1 = f32[1024,512]{1,0:T(8,128)} custom-call(bf16[1024,512]{1,0:T(8,128)(2,1)S(1)} %bitcast.35, bf16[1024,512]{1,0:T(8,128)(2,1)S(1)} %get-tuple-element.141.dq_ref, bf16[1024,1024]{1,0:T(8,128)(2,1)S(1)} %get-tuple-element.142.local_ref, f32[1024,512]{1,0:T(8,128)S(1)} %copy-done.12, ...), custom_call_target="tpu_custom_call" | custom-call | flops 6442450944 | bytes 12582912 | tf_op jit(solution)/shard_map/input_grad/pallas_call | solution.py:800
  (131 shorter events, 57.9 us)
Async XLA Ops:
  2.5 9.3 %collective-permute-start.1 = (bf16[144,1536]{1,0:T(8,128)(2,1)}, bf16[144,1536]{1,0:T(8,128)(2,1)S(1)}, u32[]{:S(2)}, u32[]{:S(2)}) collective-permute-start(bf16[144,1536]{1,0:T(8,128)(2,1)} %pack.1.refs_0_), channel_id=1, source_target_pairs={{0,1},{1,0},{2,3},{3,2},{4,5},{5,4},{6,7},{7,6},{8,9},{9,8},{10,11... | collective-permute-start | bytes 1327112 | tf_op jit(solution)/shard_map/ppermute | solution.py:820
  3.0 13.6 %collective-permute-start = (bf16[144,1536]{1,0:T(8,128)(2,1)}, bf16[144,1536]{1,0:T(8,128)(2,1)S(1)}, u32[]{:S(2)}, u32[]{:S(2)}) collective-permute-start(bf16[144,1536]{1,0:T(8,128)(2,1)} %pack.1.refs_0_), channel_id=1, source_target_pairs={{0,2},{1,3},{2,0},{3,1},{4,6},{5,7},{6,4},{7,5},{8,10},{9,11},{10,... | collective-permute-start | bytes 1327112 | tf_op jit(solution)/shard_map/ppermute | solution.py:820
  16.6 14.6 %collective-permute-start.3 = (bf16[384,512]{1,0:T(8,128)(2,1)S(1)}, bf16[384,512]{1,0:T(8,128)(2,1)S(1)}, u32[]{:S(2)}, u32[]{:S(2)}) collective-permute-start(bf16[384,512]{1,0:T(8,128)(2,1)S(1)} %copy-done.6), channel_id=1, source_target_pairs={{0,2},{1,3},{2,0},{3,1},{4,6},{5,7},{6,4},{7,5},{8,10},{9,11},{10,... | collective-permute-start | bytes 1179656 | tf_op jit(solution)/shard_map/ppermute | solution.py:820
  42.8 16.1 %collective-permute-start.7 = (bf16[112,1536]{1,0:T(8,128)(2,1)}, bf16[112,1536]{1,0:T(8,128)(2,1)S(1)}, u32[]{:S(2)}, u32[]{:S(2)}) collective-permute-start(bf16[112,1536]{1,0:T(8,128)(2,1)} %get-tuple-element.122), channel_id=1, source_target_pairs={{0,4},{4,8},{8,12},{12,16},{16,20},{20,24},{24,28},{1,5},{5,9},{9,... | collective-permute-start | bytes 1032200 | tf_op jit(solution)/shard_map/ppermute | solution.py:816
  45.1 13.9 %collective-permute-start.8 = (bf16[112,1536]{1,0:T(8,128)(2,1)}, bf16[112,1536]{1,0:T(8,128)(2,1)S(1)}, u32[]{:S(2)}, u32[]{:S(2)}) collective-permute-start(bf16[112,1536]{1,0:T(8,128)(2,1)} %get-tuple-element.123), channel_id=1, source_target_pairs={{4,0},{8,4},{12,8},{16,12},{20,16},{24,20},{28,24},{5,1},{9,5},{13... | collective-permute-start | bytes 1032200 | tf_op jit(solution)/shard_map/ppermute | solution.py:816
  59.7 22.7 %collective-permute-start.12 = (bf16[768,512]{1,0:T(8,128)(2,1)S(1)}, bf16[768,512]{1,0:T(8,128)(2,1)S(1)}, u32[]{:S(2)}, u32[]{:S(2)}) collective-permute-start(bf16[768,512]{1,0:T(8,128)(2,1)S(1)} %copy-done.5), channel_id=1, source_target_pairs={{0,1},{1,0},{2,3},{3,2},{4,5},{5,4},{6,7},{7,6},{8,9},{9,8},{10,11... | collective-permute-start | bytes 2359304 | tf_op jit(solution)/shard_map/ppermute | solution.py:820
  59.7 22.7 %collective-permute-start.11 = (bf16[768,512]{1,0:T(8,128)(2,1)S(1)}, bf16[768,512]{1,0:T(8,128)(2,1)S(1)}, u32[]{:S(2)}, u32[]{:S(2)}) collective-permute-start(bf16[768,512]{1,0:T(8,128)(2,1)S(1)} %copy-done.5), channel_id=1, source_target_pairs={{0,2},{1,3},{2,0},{3,1},{4,6},{5,7},{6,4},{7,5},{8,10},{9,11},{10,... | collective-permute-start | bytes 2359304 | tf_op jit(solution)/shard_map/ppermute | solution.py:820
  122.1 39.7 %collective-permute-start.15 = (bf16[608,512]{1,0:T(8,128)(2,1)S(1)}, bf16[608,512]{1,0:T(8,128)(2,1)S(1)}, u32[]{:S(2)}, u32[]{:S(2)}) collective-permute-start(bf16[608,512]{1,0:T(8,128)(2,1)S(1)} %get-tuple-element.151), channel_id=1, source_target_pairs={{0,4},{4,0},{8,12},{12,8},{16,20},{20,16},{24,28},{28,24},{1,5},{5... | collective-permute-start | bytes 1867784 | tf_op jit(solution)/shard_map/ppermute | solution.py:820
  124.5 37.3 %collective-permute-start.16 = (bf16[608,512]{1,0:T(8,128)(2,1)S(1)}, bf16[608,512]{1,0:T(8,128)(2,1)S(1)}, u32[]{:S(2)}, u32[]{:S(2)}) collective-permute-start(bf16[608,512]{1,0:T(8,128)(2,1)S(1)} %get-tuple-element.152), channel_id=1, source_target_pairs={{0,2},{1,3},{2,0},{3,1},{4,6},{5,7},{6,4},{7,5},{8,10},{9,11},{10,... | collective-permute-start | bytes 1867784 | tf_op jit(solution)/shard_map/ppermute | solution.py:820
  125.0 36.8 %collective-permute-start.17 = (bf16[608,512]{1,0:T(8,128)(2,1)S(1)}, bf16[608,512]{1,0:T(8,128)(2,1)S(1)}, u32[]{:S(2)}, u32[]{:S(2)}) collective-permute-start(bf16[608,512]{1,0:T(8,128)(2,1)S(1)} %get-tuple-element.153), channel_id=1, source_target_pairs={{0,6},{1,7},{2,4},{3,5},{4,2},{5,3},{6,0},{7,1},{8,14},{9,15},{10,... | collective-permute-start | bytes 1867784 | tf_op jit(solution)/shard_map/ppermute | solution.py:886
  162.8 11.0 %collective-permute-start.24 = (bf16[304,512]{1,0:T(8,128)(2,1)S(1)}, bf16[304,512]{1,0:T(8,128)(2,1)S(1)}, u32[]{:S(2)}, u32[]{:S(2)}) collective-permute-start(bf16[304,512]{1,0:T(8,128)(2,1)S(1)} %get-tuple-element.167), channel_id=1, source_target_pairs={{0,8},{4,12},{8,0},{12,4},{16,24},{20,28},{24,16},{28,20},{1,9},{5... | collective-permute-start | bytes 933896 | tf_op jit(solution)/shard_map/ppermute | solution.py:820
  166.7 14.0 %collective-permute-start.21 = (bf16[288,512]{1,0:T(8,128)(2,1)S(1)}, bf16[288,512]{1,0:T(8,128)(2,1)S(1)}, u32[]{:S(2)}, u32[]{:S(2)}) collective-permute-start(bf16[288,512]{1,0:T(8,128)(2,1)S(1)} %get-tuple-element.160), channel_id=1, source_target_pairs={{0,4},{4,0},{8,12},{12,8},{16,20},{20,16},{24,28},{28,24},{1,5},{5... | collective-permute-start | bytes 884744 | tf_op jit(solution)/shard_map/ppermute | solution.py:820
  167.9 12.8 %collective-permute-start.23 = (bf16[224,512]{1,0:T(8,128)(2,1)S(1)}, bf16[224,512]{1,0:T(8,128)(2,1)S(1)}, u32[]{:S(2)}, u32[]{:S(2)}) collective-permute-start(bf16[224,512]{1,0:T(8,128)(2,1)S(1)} %get-tuple-element.162), channel_id=1, source_target_pairs={{0,6},{1,7},{2,4},{3,5},{4,2},{5,3},{6,0},{7,1},{8,14},{9,15},{10,... | collective-permute-start | bytes 688136 | tf_op jit(solution)/shard_map/ppermute | solution.py:886
  181.4 21.0 %collective-permute-start.31 = (bf16[304,512]{1,0:T(8,128)(2,1)S(1)}, bf16[304,512]{1,0:T(8,128)(2,1)S(1)}, u32[]{:S(2)}, u32[]{:S(2)}) collective-permute-start(bf16[304,512]{1,0:T(8,128)(2,1)S(1)} %scatter.7.refs_0_), channel_id=1, source_target_pairs={{0,16},{4,20},{8,24},{12,28},{16,0},{20,4},{24,8},{28,12},{1,17},{... | collective-permute-start | bytes 933896 | tf_op jit(solution)/shard_map/ppermute | solution.py:820
  184.8 8.7 %collective-permute-start.25 = (bf16[144,512]{1,0:T(8,128)(2,1)S(1)}, bf16[144,512]{1,0:T(8,128)(2,1)S(1)}, u32[]{:S(2)}, u32[]{:S(2)}) collective-permute-start(bf16[144,512]{1,0:T(8,128)(2,1)S(1)} %get-tuple-element.173), channel_id=1, source_target_pairs={{0,8},{4,12},{8,0},{12,4},{16,24},{20,28},{24,16},{28,20},{1,9},{5... | collective-permute-start | bytes 442376 | tf_op jit(solution)/shard_map/ppermute | solution.py:820
  194.1 10.6 %collective-permute-start.26 = (bf16[128,512]{1,0:T(8,128)(2,1)S(1)}, bf16[128,512]{1,0:T(8,128)(2,1)S(1)}, u32[]{:S(2)}, u32[]{:S(2)}) collective-permute-start(bf16[128,512]{1,0:T(8,128)(2,1)S(1)} %get-tuple-element.176), channel_id=1, source_target_pairs={{0,16},{4,20},{8,24},{12,28},{16,0},{20,4},{24,8},{28,12},{1,17},{... | collective-permute-start | bytes 393224 | tf_op jit(solution)/shard_map/ppermute | solution.py:820
  196.2 23.1 %collective-permute-start.18 = (bf16[112,1024]{1,0:T(8,128)(2,1)S(1)}, bf16[112,1024]{1,0:T(8,128)(2,1)S(1)}, u32[]{:S(2)}, u32[]{:S(2)}) collective-permute-start(bf16[112,1024]{1,0:T(8,128)(2,1)S(1)} %get-tuple-element.154), channel_id=1, source_target_pairs={{4,0},{8,4},{12,8},{16,12},{20,16},{24,20},{28,24},{5,1},{9,5},{13... | collective-permute-start | bytes 688136 | tf_op jit(solution)/shard_map/ppermute | solution.py:816
  197.5 23.2 %collective-permute-start.19 = (bf16[112,1024]{1,0:T(8,128)(2,1)S(1)}, bf16[112,1024]{1,0:T(8,128)(2,1)S(1)}, u32[]{:S(2)}, u32[]{:S(2)}) collective-permute-start(bf16[112,1024]{1,0:T(8,128)(2,1)S(1)} %get-tuple-element.155), channel_id=1, source_target_pairs={{0,4},{4,8},{8,12},{12,16},{16,20},{20,24},{24,28},{1,5},{5,9},{9,... | collective-permute-start | bytes 688136 | tf_op jit(solution)/shard_map/ppermute | solution.py:816
  203.0 13.9 %collective-permute-start.32 = (bf16[152,512]{1,0:T(8,128)(2,1)S(1)}, bf16[152,512]{1,0:T(8,128)(2,1)S(1)}, u32[]{:S(2)}, u32[]{:S(2)}) collective-permute-start(bf16[152,512]{1,0:T(8,128)(2,1)S(1)} %get-tuple-element.189.refs_0_), channel_id=1, source_target_pairs={{0,8},{4,12},{8,0},{12,4},{16,24},{20,28},{24,16},{28,20},{1,9},{5... | collective-permute-start | bytes 466952 | tf_op jit(solution)/shard_map/ppermute | solution.py:820
  203.5 14.9 %collective-permute-start.33 = (bf16[152,512]{1,0:T(8,128)(2,1)S(1)}, bf16[152,512]{1,0:T(8,128)(2,1)S(1)}, u32[]{:S(2)}, u32[]{:S(2)}) collective-permute-start(bf16[152,512]{1,0:T(8,128)(2,1)S(1)} %get-tuple-element.190.refs_1_), channel_id=1, source_target_pairs={{0,4},{4,0},{8,12},{12,8},{16,20},{20,16},{24,28},{28,24},{1,5},{5... | collective-permute-start | bytes 466952 | tf_op jit(solution)/shard_map/ppermute | solution.py:820
  215.8 9.0 %collective-permute-start.29 = (bf16[112,512]{1,0:T(8,128)(2,1)S(1)}, bf16[112,512]{1,0:T(8,128)(2,1)S(1)}, u32[]{:S(2)}, u32[]{:S(2)}) collective-permute-start(bf16[112,512]{1,0:T(8,128)(2,1)S(1)} %get-tuple-element.180.refs_0_), channel_id=1, source_target_pairs={{0,4},{4,0},{8,12},{12,8},{16,20},{20,16},{24,28},{28,24},{1,5},{5... | collective-permute-start | bytes 344072 | tf_op jit(solution)/shard_map/ppermute | solution.py:820
  216.8 7.9 %collective-permute-start.30 = (bf16[112,512]{1,0:T(8,128)(2,1)S(1)}, bf16[112,512]{1,0:T(8,128)(2,1)S(1)}, u32[]{:S(2)}, u32[]{:S(2)}) collective-permute-start(bf16[112,512]{1,0:T(8,128)(2,1)S(1)} %get-tuple-element.181.refs_1_), channel_id=1, source_target_pairs={{0,8},{4,12},{8,0},{12,4},{16,24},{20,28},{24,16},{28,20},{1,9},{5... | collective-permute-start | bytes 344072 | tf_op jit(solution)/shard_map/ppermute | solution.py:820
  219.1 7.7 %collective-permute-start.34 = (bf16[304,512]{1,0:T(8,128)(2,1)S(1)}, bf16[304,512]{1,0:T(8,128)(2,1)S(1)}, u32[]{:S(2)}, u32[]{:S(2)}) collective-permute-start(bf16[304,512]{1,0:T(8,128)(2,1)S(1)} %get-tuple-element.191.refs_0_), channel_id=1, source_target_pairs={{0,4},{4,0},{8,12},{12,8},{16,20},{20,16},{24,28},{28,24},{1,5},{5... | collective-permute-start | bytes 933896 | tf_op jit(solution)/shard_map/ppermute | solution.py:820
  219.2 8.0 %collective-permute-start.35 = (bf16[304,512]{1,0:T(8,128)(2,1)S(1)}, bf16[304,512]{1,0:T(8,128)(2,1)S(1)}, u32[]{:S(2)}, u32[]{:S(2)}) collective-permute-start(bf16[304,512]{1,0:T(8,128)(2,1)S(1)} %get-tuple-element.192.refs_1_), channel_id=1, source_target_pairs={{0,8},{4,12},{8,0},{12,4},{16,24},{20,28},{24,16},{28,20},{1,9},{5... | collective-permute-start | bytes 933896 | tf_op jit(solution)/shard_map/ppermute | solution.py:820
  (39 other events, 312.2 us)
